TPU v7x, 256 devices: a whole 4x4x8 slice. The times are simulated.
256 devices in a mesh: member: 16 (over z_hi, x, core), ctx: 16 (over y, z_lo).
Axes of the slice: x: 4, y: 4, z: 8 (z_hi: 2, z_lo: 4; z = z_hi * 4 + z_lo), core: 2. Of those that a mesh axis runs over, the one named last changes fastest.
Arguments:
- queries: bfloat16 [16, 2048, 4096], P('member', 'ctx'), may hold values from -8 to 8
- response_keys: bfloat16 [16, 2048, 512], P('member', 'ctx'), may hold values from -4.5 to 4.5
- response_values: bfloat16 [16, 2048, 512], P('member', 'ctx'), may hold values from -16 to 16
- prompt_keys: bfloat16 [512, 512], P(('member', 'ctx')), may hold values from -4.5 to 4.5
- prompt_values: bfloat16 [512, 512], P(('member', 'ctx')), may hold values from -16 to 16
- block_offsets: int32 [16, 16], P('member'), may hold values from 0 to 15, each once within a row
- lengths: int32 [16], P('member'), may hold values from 512 to 2048, as said below
Outputs:
- attended: bfloat16 [16, 2048, 4096], P('member', 'ctx')
Inputs may be any that keep to these rules, and one draw needn't show every extreme that they name: `lengths`: each response has from 512 to 2048 valid slab tokens; some response has exactly 2048, some exactly 512. `block_offsets`: each row of a response's blocks names every block once.
All inputs are finite; a program needn't handle non-finite values.
Results may differ from a plain program's by a relative error of at most 0.0065.
Values may be sent and summed in bfloat16 or wider, within the bound.
No kernel may reach another device: no remote copies, remote signals or barrier semaphores. Data moves between devices by JAX's collectives and lax.ppermute only.
A program may use at most 128 MiB of HBM per device.

v0:
```python
import math

import jax
import jax.numpy as jnp
from jax import lax
from jax.sharding import PartitionSpec as P

HD = 128


key_block = 512
neg_start = -1e30


def attend(
    state_tuple,
    queries_grouped,
    key_rows,
    value_rows,
    key_positions,
    query_positions,
    valid_length,
    score_scale,
):
    running_max, totals, weighted = state_tuple
    kv_heads = queries_grouped.shape[1]
    head_size = queries_grouped.shape[3]
    row_count = key_rows.shape[0]
    for block_start in range(0, row_count, key_block):
        block_end = min(block_start + key_block, row_count)
        block_keys = key_rows[block_start:block_end].reshape(
            block_end - block_start, kv_heads, head_size
        )
        block_values = value_rows[block_start:block_end].reshape(
            block_end - block_start, kv_heads, head_size
        )
        scores = (
            jnp.einsum(
                "tgnd,sgd->tgns", queries_grouped, block_keys, preferred_element_type=jnp.float32
            )
            * score_scale
        )
        if key_positions is not None:
            block_positions = key_positions[block_start:block_end]
            visible = (block_positions[None, :] <= query_positions[:, None]) & (
                block_positions[None, :] < valid_length
            )
            scores = jnp.where(visible[:, None, None, :], scores, -jnp.inf)
        new_max = jnp.maximum(running_max, jnp.max(scores, axis=-1))
        rescale = jnp.exp(running_max - new_max)
        exponent = jnp.exp(scores - new_max[..., None])
        totals = totals * rescale + jnp.sum(exponent, axis=-1)
        weighted = weighted * rescale[..., None] + jnp.einsum(
            "tgns,sgd->tgnd",
            exponent.astype(jnp.bfloat16),
            block_values,
            preferred_element_type=jnp.float32,
        )
        running_max = new_max
    return (running_max, totals, weighted)


def body(
    queries, response_keys, response_values, prompt_keys, prompt_values, block_offsets, lengths
):
    tok_rows = queries.shape[1]
    head_size = HD
    kv_heads = response_keys.shape[2] // head_size
    head_count = queries.shape[2] // head_size
    group_size = head_count // kv_heads
    score_scale = 1.0 / math.sqrt(head_size)
    queries_grouped = queries[0].reshape(tok_rows, kv_heads, group_size, head_size)
    offsets = block_offsets[0]
    cycle_size = lax.axis_size("ctx")
    cycle_ids = jnp.arange(cycle_size, dtype=jnp.int32)
    my_index = lax.axis_index("ctx")
    my_block = jnp.sum(jnp.where(cycle_ids == my_index, offsets, 0))
    query_positions = my_block * tok_rows + jnp.arange(tok_rows, dtype=jnp.int32)
    valid_length = lengths[0]
    start_state = (
        jnp.full((tok_rows, kv_heads, group_size), neg_start, jnp.float32),
        jnp.zeros((tok_rows, kv_heads, group_size), jnp.float32),
        jnp.zeros((tok_rows, kv_heads, group_size, head_size), jnp.float32),
    )
    shard_piece = (
        lax.all_gather(prompt_keys, ("member", "ctx"), axis=0, tiled=True),
        lax.all_gather(prompt_values, ("member", "ctx"), axis=0, tiled=True),
    )
    prompt_state = attend(
        start_state,
        queries_grouped,
        shard_piece[0],
        shard_piece[1],
        None,
        query_positions,
        valid_length,
        score_scale,
    )
    shard_piece = (
        lax.all_gather(response_keys[0], "ctx", axis=0, tiled=True),
        lax.all_gather(response_values[0], "ctx", axis=0, tiled=True),
    )
    row_count = shard_piece[0].shape[0]
    row_ids = jnp.arange(row_count, dtype=jnp.int32)
    source = row_ids // tok_rows
    block_of = jnp.sum(
        jnp.where(source[:, None] == cycle_ids[None, :], offsets[None, :], 0), axis=1
    )
    key_positions = block_of * tok_rows + row_ids % tok_rows
    response_state = attend(
        prompt_state,
        queries_grouped,
        shard_piece[0],
        shard_piece[1],
        key_positions,
        query_positions,
        valid_length,
        score_scale,
    )
    attended = response_state[2] / response_state[1][..., None]
    attended = attended.reshape(tok_rows, head_count * head_size)
    return attended.astype(jnp.bfloat16)[None]


def solution(mesh):
    return jax.shard_map(
        body,
        mesh=mesh,
        in_specs=(
            P("member", "ctx", None),
            P("member", "ctx", None),
            P("member", "ctx", None),
            P(("member", "ctx"), None),
            P(("member", "ctx"), None),
            P("member", None),
            P("member"),
        ),
        out_specs=P("member", "ctx", None),
        check_vma=False,
    )
```

profile of v0, /device:TPU:32, one launch (start us, length us, event | category | flops | bytes accessed | tf_op | source)
XLA Modules:
  0.0 1352.5 jit_solution(209004778783469010)
XLA Ops:
  6.5 1.7 copy.72
  8.2 0.0 all-gather.9.cloned.1.call-start
  8.3 0.7 all-gather.9.cloned.1.call-update
  9.0 0.8 select_reduce_fusion
  10.4 1.3 fusion.71
  12.4 1.4 copy.117
  13.8 626.1 %all-gather.2 = bf16[256,2,512]{2,1,0:T(2,128)(2,1)S(1)} all-gather(bf16[1,2,512]{2,1,0:T(2,128)(2,1)} %bitcast.162), channel_id=1, replica_groups=mesh['member'=16,'ctx'=16] {'member','ctx'}, dimensions={0}, use_global_device_ids=true | all-gather | bytes 526336 | tf_op jit(solution)/shard_map/all_gather | solution.py:86
  639.9 0.3 reshape.308
  640.3 628.6 %all-gather.3 = bf16[256,2,512]{2,1,0:T(2,128)(2,1)S(1)} all-gather(bf16[1,2,512]{2,1,0:T(2,128)(2,1)} %bitcast.163), channel_id=1, replica_groups=mesh['member'=16,'ctx'=16] {'member','ctx'}, dimensions={0}, use_global_device_ids=true | all-gather | bytes 526336 | tf_op jit(solution)/shard_map/all_gather | solution.py:87
  1268.9 0.3 reshape.309
  1269.2 0.9 compare_and_fusion.3
  1270.1 4.5 bitcast_reduce_fusion
  1274.6 1.7 fusion.85
  1276.3 4.9 fusion.14
  1281.2 4.9 fusion.13
  1286.2 5.0 fusion.12
  1291.1 5.4 fusion.11
  1296.6 1.6 fusion.9
  1298.1 2.1 fusion.15
  1300.2 2.7 fusion.84
  1302.9 2.1 copy.79
  1305.0 2.0 copy.83
  1307.0 1.0 copy.87
  1308.0 7.0 fusion.19
  1315.1 7.8 fusion.5
  1323.0 3.4 fusion.17
  1326.4 1.0 copy.75
  1327.4 5.6 fusion.21
  1333.0 7.9 fusion.1
  1340.9 0.5 copy-done.4
  1341.4 2.9 fusion.44
  1344.4 1.3 copy.89
  (35 shorter events, 0.2 us)
Async XLA Ops:
  6.5 1268.1 %all-gather.7.cloned.1.call-start = ((), (), s32[]{:S(2)}) async-start(), calls=%async_computation | async-start | bytes 2228224 | tf_op jit(solution)/shard_map/all_gather | solution.py:100
  8.2 1292.0 %all-gather.9.cloned.1.call-start = ((), (), s32[]{:S(2)}) async-start(), calls=%async_computation.1 | async-start | bytes 2228224 | tf_op jit(solution)/shard_map/all_gather | solution.py:101
  1291.1 5.4 slice-start
  1291.1 5.4 slice-start.1
  1308.0 14.9 %slice-start.4 = ((s8[8388608]{0:T(1024)(128)(4,1)}), s8[4194304]{0:T(1024)(128)(4,1)S(1)}, s32[]{:S(2)}) async-start(s8[8388608]{0:T(1024)(128)(4,1)} %bitcast.148), calls=%async_computation.6 | async-start | bytes 8388608
  1315.1 7.9 slice-start.5
  1315.1 7.9 copy-start.2
  1322.9 4.5 copy-start.1
  1327.4 13.5 slice-start.2
  1332.9 8.0 slice-start.3
  1332.9 8.0 copy-start
  1333.0 8.0 copy-start.3
  1333.0 8.4 copy-start.4
Sparse Core Ops, SparseCore 0:
  9.1 85.3 all-gather.6
  96.2 89.5 all-gather.8
where the time goes:
time: 1350 us
  blocking collectives  1250 us (93%)
  matrix products  45.7 us (3%)
  other arithmetic  20.3 us (2%)
  local copies, waits for them, and re-layouts  16.1 us (1%)
  between operations  14.9 us (1%)
    all_gather x1, blocking collectives, body(): lax.all_gather(prompt_values, ('member', 'ctx'), axis=0, tiled=True)  629 us
    all_gather x1, blocking collectives, body(): lax.all_gather(prompt_keys, ('member', 'ctx'), axis=0, tiled=True)  626 us
  transfers between devices with their start and end apart: 2, of which 0 were waited for; matrix products, arithmetic and copies ran while one was open for 3% of the time, Pallas kernels for 0%

commit v1 on v0

v1 whole, which is shorter than its diff:
```python
import math

import jax
import jax.numpy as jnp
from jax import lax
from jax.experimental import pallas as pl
from jax.experimental.pallas import tpu as pltpu
from jax.sharding import PartitionSpec as P

HD = 128
KV_HEADS = 4
GROUP = 8
TOK = 128
PAIR = 2
SCALE = math.log2(math.e) / math.sqrt(HD)
NEG = -1e30
AXES = ("member", "ctx")


def moves(step):
    pairs = []
    for i in range(256):
        zh, x, c, y, z = i // 128, i // 32 % 4, i // 16 % 2, i // 4 % 4, i % 4
        zh2, x2, c2, y2, z2 = step(zh, x, c, y, z)
        pairs.append((i, (((zh2 * 4 + x2) * 2 + c2) * 4 + y2) * 4 + z2))
    return pairs


Z_STEPS = [moves(lambda zh, x, c, y, z, k=k: (zh, x, c, y, z ^ (1, 2)[c ^ k])) for k in (0, 1)]
Y_STEPS = [moves(lambda zh, x, c, y, z, k=k: (zh, x, c, y ^ (1, 3)[c ^ k], z)) for k in (0, 1)]
X_STEPS = [moves(lambda zh, x, c, y, z, k=k: (zh, x ^ (1, 3)[c ^ k], c, y, z)) for k in (0, 1)]
ZH_STEP = moves(lambda zh, x, c, y, z: (zh ^ 1, x, c, y, z))
CORE_STEP = moves(lambda zh, x, c, y, z: (zh, x, c ^ 1, y, z))


def send(value, pairs):
    return lax.ppermute(value, AXES, pairs)


def double(value, pairs):
    return jnp.concatenate([value, send(value, pairs)], axis=0)


def make_kernel(counts):
    prompt_rows = 512
    keys = prompt_rows + TOK * sum(counts)

    def kernel(offsets, length, q_ref, pk_ref, pv_ref, *refs):
        n = len(counts)
        k_refs, v_refs = refs[:n], refs[n : 2 * n]
        out_ref, k_aug, v_aug = refs[2 * n :]
        ctx, member = lax.axis_index("ctx"), lax.axis_index("member")
        core = member % 2
        y, z = ctx // 4, ctx % 4

        @pl.when(pl.program_id(0) == 0)
        def _():
            v_aug[:, HD:] = jnp.ones((keys, HD), jnp.bfloat16)
            k_aug[:prompt_rows, HD:] = jnp.zeros((prompt_rows, HD), jnp.bfloat16)
            q_pos = lax.broadcasted_iota(jnp.int32, (TOK, TOK), 1) + offsets[0, ctx] * TOK
            k_row = lax.broadcasted_iota(jnp.int32, (TOK, TOK), 0)
            for index, (ybits, zbits) in enumerate(BLOCKS):
                dy = block_delta(ybits, core, 1, 3)
                dz = block_delta(zbits, core, 1, 2)
                source = (y ^ dy) * 4 + (z ^ dz)
                k_pos = k_row + offsets[0, source] * TOK
                counted = (k_pos <= q_pos) & (k_pos < length[0])
                start = prompt_rows + index * TOK
                k_aug[start : start + TOK, HD:] = jnp.where(counted, 0.0, NEG).astype(jnp.bfloat16)

        k_aug[:prompt_rows, :HD] = pk_ref[...].reshape(prompt_rows, HD)
        v_aug[:prompt_rows, :HD] = pv_ref[...].reshape(prompt_rows, HD)
        start = prompt_rows
        for i in range(n):
            rows = counts[i] * TOK
            k_aug[start : start + rows, :HD] = k_refs[i][...].reshape(rows, HD)
            v_aug[start : start + rows, :HD] = v_refs[i][...].reshape(rows, HD)
            start += rows
        eye = (
            lax.broadcasted_iota(jnp.int32, (TOK, TOK), 0)
            == lax.broadcasted_iota(jnp.int32, (TOK, TOK), 1)
        )
        eye = jnp.where(eye, 1.0, 0.0).astype(jnp.bfloat16)
        keys_all, values_all = k_aug[...], v_aug[...]

        def score(h):
            rows = [
                jnp.concatenate([q_ref[:, (h * PAIR + u) * HD : (h * PAIR + u + 1) * HD], eye], axis=1)
                for u in range(PAIR)
            ]
            return lax.dot_general(
                jnp.concatenate(rows, axis=0),
                keys_all,
                (((1,), (1,)), ((), ())),
                preferred_element_type=jnp.float32,
            )

        def finish(h, s):
            top = jnp.max(s, axis=1, keepdims=True) * SCALE
            weights = jnp.exp2(s * SCALE - top).astype(jnp.bfloat16)
            both = lax.dot_general(
                weights, values_all, (((1,), (0,)), ((), ())), preferred_element_type=jnp.float32
            )
            result = (both[:, :HD] / both[:, HD:]).astype(jnp.bfloat16)
            for u in range(PAIR):
                out_ref[:, (h * PAIR + u) * HD : (h * PAIR + u + 1) * HD] = result[u * TOK : (u + 1) * TOK]

        s = score(0)
        for h in range(GROUP // PAIR):
            ahead = score(h + 1) if h + 1 < GROUP // PAIR else None
            finish(h, s)
            s = ahead

    return kernel


def block_delta(bits, core, first, second):
    step0 = first + core * (second - first)
    step1 = second + core * (first - second)
    return (step0 if bits & 1 else 0) ^ (step1 if bits & 2 else 0)


BLOCKS = [(yb, zb) for yb in range(4) for zb in (0, 1)] + [(yb, zb) for yb in range(4) for zb in (2, 3)]


def attend(offsets, length, q, prompt, groups):
    counts = [g.shape[0] for g in groups]
    keys = 512 + TOK * sum(counts)
    in_specs = [
        pl.BlockSpec(memory_space=pltpu.SMEM),
        pl.BlockSpec(memory_space=pltpu.SMEM),
        pl.BlockSpec((TOK, GROUP * HD), lambda g: (0, g)),
        pl.BlockSpec((None, 512, HD), lambda g: (0, 0, g)),
        pl.BlockSpec((None, 512, HD), lambda g: (1, 0, g)),
    ]
    for part in (0, 1):
        for n in counts:
            in_specs.append(pl.BlockSpec((n, None, TOK, HD), lambda g, part=part: (0, part, 0, g)))
    return pl.pallas_call(
        make_kernel(counts),
        grid=(KV_HEADS,),
        in_specs=in_specs,
        out_specs=pl.BlockSpec((TOK, GROUP * HD), lambda g: (0, g)),
        out_shape=jax.ShapeDtypeStruct((TOK, KV_HEADS * GROUP * HD), jnp.bfloat16),
        scratch_shapes=[pltpu.VMEM((keys, 2 * HD), jnp.bfloat16)] * 2,
        compiler_params=pltpu.CompilerParams(vmem_limit_bytes=48 << 20),
        cost_estimate=pl.CostEstimate(
            flops=4 * 4096 * keys * HD, bytes_accessed=8 << 20, transcendentals=4096 * keys
        ),
        name="attend",
    )(offsets, length, q, prompt, prompt, *groups, *groups)


def body(
    queries, response_keys, response_values, prompt_keys, prompt_values, block_offsets, lengths
):
    own = jnp.concatenate([response_keys, response_values], axis=0)[None]
    prompt = jnp.concatenate([prompt_keys[None], prompt_values[None]], axis=0)[None]
    near = double(own, Z_STEPS[0])
    far = send(near, Z_STEPS[1])
    for pairs in Y_STEPS:
        near = double(near, pairs)
    for pairs in Y_STEPS:
        far = double(far, pairs)
    for pairs in (Z_STEPS[0], Z_STEPS[1], ZH_STEP, Y_STEPS[0], Y_STEPS[1], X_STEPS[0], X_STEPS[1], CORE_STEP):
        prompt = double(prompt, pairs)
    prompt = prompt.transpose(1, 0, 2, 3).reshape(2, 512, KV_HEADS * HD)
    out = attend(block_offsets, lengths, queries[0], prompt, (near, far))
    return out[None]


def solution(mesh):
    return jax.shard_map(
        body,
        mesh=mesh,
        in_specs=(
            P("member", "ctx", None),
            P("member", "ctx", None),
            P("member", "ctx", None),
            P(("member", "ctx"), None),
            P(("member", "ctx"), None),
            P("member", None),
            P("member"),
        ),
        out_specs=P("member", "ctx", None),
        check_vma=False,
    )
```

time: 1350 us -> 92.9 us (0.07)
  the two profiles are of different devices: /device:TPU:32 before, /device:TPU:6 now
where the time goes in v1:
time: 92.9 us; the launch traced here: 92.2 us
  waiting for transfers between devices  37.5 us (40%)
  starting transfers between devices  24.7 us (27%)
  Pallas kernels  17.5 us (19%)
  other arithmetic  9.22 us (10%)
  local copies, waits for them, and re-layouts  2.52 us (3%)
    ppermute x14, waiting for transfers between devices, send(): return lax.ppermute(value, AXES, pairs)  37.5 us
    ppermute x14, starting transfers between devices, send(): return lax.ppermute(value, AXES, pairs)  24.7 us
    pallas_call x1, Pallas kernels, attend(): pl.pallas_call(make_kernel(counts), grid=(KV_HEADS,), in_specs=in_specs,...  17.5 us
    concatenate x8, other arithmetic, double(): return jnp.concatenate([value, send(value, pairs)], axis=0)  6.81 us
  transfers between devices with their start and end apart: 14, of which 9 were waited for; matrix products, arithmetic and copies ran while one was open for 9% of the time, Pallas kernels for 0%

profile of v1, /device:TPU:6, one launch (start us, length us, event | category | flops | bytes accessed | tf_op | source)
XLA Modules:
  0.0 92.2 jit_solution(11344963858054998382)
XLA Ops:
  0.0 1.0 %maximum_bitcast_fusion = bf16[1,2,128,512]{3,2,1,0:T(8,128)(2,1)S(1)} fusion(bf16[1,128,512]{2,1,0:T(8,128)(2,1)} %param.9, bf16[1,128,512]{2,1,0:T(8,128)(2,1)} %param.8), kind=kLoop, calls=%fused_computation.5 | loop fusion | flops 131072 | bytes 524288 | tf_op jit(solution)/shard_map/broadcast_in_dim | solution.py:157
  1.0 2.0 %collective-permute-start.8 = (bf16[1,2,128,512]{3,2,1,0:T(8,128)(2,1)S(1)}, bf16[1,2,128,512]{3,2,1,0:T(8,128)(2,1)S(1)}, u32[]{:S(2)}, u32[]{:S(2)}) collective-permute-start(bf16[1,2,128,512]{3,2,1,0:T(8,128)(2,1)S(1)} %maximum_bitcast_fusion), channel_id=1, source_target_pairs={{0,1},{1,0},{2,3},{3,2},{4,5},{5,4},{6,7},{7,6},{8,9},{9,8},{10,11... | collective-permute-start | bytes 786440 | tf_op jit(solution)/shard_map/ppermute | solution.py:37
  3.0 0.7 maximum_bitcast_fusion.1
  3.9 0.7 constant_dynamic-update-slice_fusion.25
  4.6 5.7 %collective-permute-done = bf16[1,2,2,512]{3,2,1,0:T(2,128)(2,1)S(1)} collective-permute-done((bf16[1,2,2,512]{3,2,1,0:T(2,128)(2,1)S(1)}, bf16[1,2,2,512]{3,2,1,0:T(2,128)(2,1)S(1)}, u32[]{:S(2)}, u32[]{:S(2)}) %collective-permute-start) | collective-permute-done | bytes 4128 | tf_op jit(solution)/shard_map/ppermute | solution.py:37
  10.3 2.8 %collective-permute-start.1 = (bf16[2,2,2,512]{3,2,1,0:T(2,128)(2,1)S(1)}, bf16[2,2,2,512]{3,2,1,0:T(2,128)(2,1)S(1)}, u32[]{:S(2)}, u32[]{:S(2)}) collective-permute-start(bf16[2,2,2,512]{3,2,1,0:T(2,128)(2,1)S(1)} %pad_maximum_fusion.7), channel_id=1, source_target_pairs={{0,2},{1,3},{2,0},{3,1},{4,6},{5,7},{6,4},{7,5},{8,10},{9,11},{10,... | collective-permute-start | bytes 24584 | tf_op jit(solution)/shard_map/ppermute | solution.py:37
  13.1 0.3 collective-permute-start.11
  13.5 1.6 %collective-permute-done.1 = bf16[2,2,2,512]{3,2,1,0:T(2,128)(2,1)S(1)} collective-permute-done((bf16[2,2,2,512]{3,2,1,0:T(2,128)(2,1)S(1)}, bf16[2,2,2,512]{3,2,1,0:T(2,128)(2,1)S(1)}, u32[]{:S(2)}, u32[]{:S(2)}) %collective-permute-start.1) | collective-permute-done | bytes 8224 | tf_op jit(solution)/shard_map/ppermute | solution.py:37
  15.1 6.9 %collective-permute-start.2 = (bf16[4,2,2,512]{3,2,1,0:T(2,128)(2,1)S(1)}, bf16[4,2,2,512]{3,2,1,0:T(2,128)(2,1)S(1)}, u32[]{:S(2)}, u32[]{:S(2)}) collective-permute-start(bf16[4,2,2,512]{3,2,1,0:T(2,128)(2,1)S(1)} %pad_maximum_fusion.6), channel_id=1, source_target_pairs={{0,128},{1,129},{2,130},{3,131},{4,132},{5,133},{6,134},{7,135},{8... | collective-permute-start | bytes 49160 | tf_op jit(solution)/shard_map/ppermute | solution.py:37
  22.0 1.7 %collective-permute-start.9 = (bf16[2,2,128,512]{3,2,1,0:T(8,128)(2,1)S(1)}, bf16[2,2,128,512]{3,2,1,0:T(8,128)(2,1)S(1)}, u32[]{:S(2)}, u32[]{:S(2)}) collective-permute-start(bf16[2,2,128,512]{3,2,1,0:T(8,128)(2,1)S(1)} %pad_maximum_fusion.4), channel_id=1, source_target_pairs={{0,4},{1,5},{2,6},{3,7},{4,0},{5,1},{6,2},{7,3},{8,12},{9,13},{10,... | collective-permute-start | bytes 1572872 | tf_op jit(solution)/shard_map/ppermute | solution.py:37
  23.7 8.0 %collective-permute-done.2 = bf16[4,2,2,512]{3,2,1,0:T(2,128)(2,1)S(1)} collective-permute-done((bf16[4,2,2,512]{3,2,1,0:T(2,128)(2,1)S(1)}, bf16[4,2,2,512]{3,2,1,0:T(2,128)(2,1)S(1)}, u32[]{:S(2)}, u32[]{:S(2)}) %collective-permute-start.2) | collective-permute-done | bytes 16416 | tf_op jit(solution)/shard_map/ppermute | solution.py:37
  31.8 1.7 %collective-permute-start.3 = (bf16[8,2,2,512]{3,2,1,0:T(2,128)(2,1)S(1)}, bf16[8,2,2,512]{3,2,1,0:T(2,128)(2,1)S(1)}, u32[]{:S(2)}, u32[]{:S(2)}) collective-permute-start(bf16[8,2,2,512]{3,2,1,0:T(2,128)(2,1)S(1)} %pad_maximum_fusion.5), channel_id=1, source_target_pairs={{0,4},{1,5},{2,6},{3,7},{4,0},{5,1},{6,2},{7,3},{8,12},{9,13},{10,... | collective-permute-start | bytes 98312 | tf_op jit(solution)/shard_map/ppermute | solution.py:37
  33.5 0.5 collective-permute-start.12
  34.0 1.7 %collective-permute-done.3 = bf16[8,2,2,512]{3,2,1,0:T(2,128)(2,1)S(1)} collective-permute-done((bf16[8,2,2,512]{3,2,1,0:T(2,128)(2,1)S(1)}, bf16[8,2,2,512]{3,2,1,0:T(2,128)(2,1)S(1)}, u32[]{:S(2)}, u32[]{:S(2)}) %collective-permute-start.3) | collective-permute-done | bytes 32800 | tf_op jit(solution)/shard_map/ppermute | solution.py:37
  35.9 3.1 %collective-permute-start.4 = (bf16[16,2,2,512]{3,2,1,0:T(2,128)(2,1)S(1)}, bf16[16,2,2,512]{3,2,1,0:T(2,128)(2,1)S(1)}, u32[]{:S(2)}, u32[]{:S(2)}) collective-permute-start(bf16[16,2,2,512]{3,2,1,0:T(2,128)(2,1)S(1)} %get-tuple-element.18), channel_id=1, source_target_pairs={{0,12},{1,13},{2,14},{3,15},{4,8},{5,9},{6,10},{7,11},{8,4},{9,5},... | collective-permute-start | bytes 196616 | tf_op jit(solution)/shard_map/ppermute | solution.py:37
  39.0 3.2 %collective-permute-done.4 = bf16[16,2,2,512]{3,2,1,0:T(2,128)(2,1)S(1)} collective-permute-done((bf16[16,2,2,512]{3,2,1,0:T(2,128)(2,1)S(1)}, bf16[16,2,2,512]{3,2,1,0:T(2,128)(2,1)S(1)}, u32[]{:S(2)}, u32[]{:S(2)}) %collective-permute-start.4) | collective-permute-done | bytes 65568 | tf_op jit(solution)/shard_map/ppermute | solution.py:37
  42.4 0.9 collective-permute-start.5
  43.3 1.1 %pad_maximum_fusion.2 = bf16[4,2,128,512]{3,2,1,0:T(8,128)(2,1)} fusion(bf16[2,2,128,512]{3,2,1,0:T(8,128)(2,1)S(1)} %collective-permute-done.9, bf16[1,2,128,512]{3,2,1,0:T(8,128)(2,1)S(1)} %collective-permute-done.8, bf16[1,2,128,512]{3,2,1,0:T(8,128)(2,1)S(1)} %maximum_bitcast_fusion), kind=kLoop, calls=%fused_computation.2 | loop fusion | flops 1048576 | bytes 2097152 | tf_op jit(solution)/shard_map/concatenate | solution.py:41
  44.4 2.3 %collective-permute-start.10 = (bf16[4,2,128,512]{3,2,1,0:T(8,128)(2,1)}, bf16[4,2,128,512]{3,2,1,0:T(8,128)(2,1)}, u32[]{:S(2)}, u32[]{:S(2)}) collective-permute-start(bf16[4,2,128,512]{3,2,1,0:T(8,128)(2,1)} %pad_maximum_fusion.2), channel_id=1, source_target_pairs={{0,12},{1,13},{2,14},{3,15},{4,8},{5,9},{6,10},{7,11},{8,4},{9,5},... | collective-permute-start | bytes 3145736 | tf_op jit(solution)/shard_map/ppermute | solution.py:37
  46.7 2.1 %collective-permute-done.5 = bf16[32,2,2,512]{3,2,1,0:T(2,128)(2,1)S(1)} collective-permute-done((bf16[32,2,2,512]{3,2,1,0:T(2,128)(2,1)S(1)}, bf16[32,2,2,512]{3,2,1,0:T(2,128)(2,1)S(1)}, u32[]{:S(2)}, u32[]{:S(2)}) %collective-permute-start.5) | collective-permute-done | bytes 131104 | tf_op jit(solution)/shard_map/ppermute | solution.py:37
  49.1 0.6 collective-permute-start.6
  49.6 1.1 %pad_maximum_fusion.3 = bf16[4,2,128,512]{3,2,1,0:T(8,128)(2,1)} fusion(bf16[2,2,128,512]{3,2,1,0:T(8,128)(2,1)S(1)} %collective-permute-done.12, bf16[2,2,128,512]{3,2,1,0:T(8,128)(2,1)S(1)} %collective-permute-done.11), kind=kLoop, calls=%fused_computation.3 | loop fusion | flops 524288 | bytes 2097152 | tf_op jit(solution)/shard_map/concatenate | solution.py:41
  50.8 1.5 %collective-permute-start.13 = (bf16[4,2,128,512]{3,2,1,0:T(8,128)(2,1)}, bf16[4,2,128,512]{3,2,1,0:T(8,128)(2,1)}, u32[]{:S(2)}, u32[]{:S(2)}) collective-permute-start(bf16[4,2,128,512]{3,2,1,0:T(8,128)(2,1)} %pad_maximum_fusion.3), channel_id=1, source_target_pairs={{0,12},{1,13},{2,14},{3,15},{4,8},{5,9},{6,10},{7,11},{8,4},{9,5},... | collective-permute-start | bytes 3145736 | tf_op jit(solution)/shard_map/ppermute | solution.py:37
  52.3 4.4 %collective-permute-done.6 = bf16[64,2,2,512]{3,2,1,0:T(2,128)(2,1)S(1)} collective-permute-done((bf16[64,2,2,512]{3,2,1,0:T(2,128)(2,1)S(1)}, bf16[64,2,2,512]{3,2,1,0:T(2,128)(2,1)S(1)}, u32[]{:S(2)}, u32[]{:S(2)}) %collective-permute-start.6) | collective-permute-done | bytes 262176 | tf_op jit(solution)/shard_map/ppermute | solution.py:37
  58.0 1.2 %collective-permute-done.7 = bf16[128,2,2,512]{3,2,1,0:T(2,128)(2,1)S(1)} collective-permute-done((bf16[128,2,2,512]{3,2,1,0:T(2,128)(2,1)S(1)}, bf16[128,2,2,512]{3,2,1,0:T(2,128)(2,1)S(1)}, u32[]{:S(2)}, u32[]{:S(2)}) %collective-permute-start.7) | collective-permute-done | bytes 524320 | tf_op jit(solution)/shard_map/ppermute | solution.py:37
  59.2 0.4 constant_dynamic-update-slice_fusion.26
  59.6 0.7 copy.8
  60.4 0.4 reshape.3.pk_ref.pv_ref
  60.8 1.6 %pad_maximum_fusion.refs_0_.refs_2_ = bf16[8,2,128,512]{3,2,1,0:T(8,128)(2,1)S(1)} fusion(bf16[4,2,128,512]{3,2,1,0:T(8,128)(2,1)} %collective-permute-done.10, bf16[2,2,128,512]{3,2,1,0:T(8,128)(2,1)} %copy-done.2, bf16[1,2,128,512]{3,2,1,0:T(8,128)(2,1)S(1)} %collective-permute-done.8, bf16[1,2,128,512]{3,2,1,0:T(8,128)(2,1)S(1)} %maximum_bitcast_fusion), kind=kLoop, calls=%fused_computation | loop fusion | flops 3145728 | bytes 4194304 | tf_op jit(solution)/shard_map/concatenate | solution.py:41
  62.5 9.5 %collective-permute-done.13 = bf16[4,2,128,512]{3,2,1,0:T(8,128)(2,1)} collective-permute-done((bf16[4,2,128,512]{3,2,1,0:T(8,128)(2,1)}, bf16[4,2,128,512]{3,2,1,0:T(8,128)(2,1)}, u32[]{:S(2)}, u32[]{:S(2)}) %collective-permute-start.13) | collective-permute-done | bytes 1048608 | tf_op jit(solution)/shard_map/ppermute | solution.py:37
  72.0 2.8 %pad_maximum_fusion.1.refs_1_.refs_3_ = bf16[8,2,128,512]{3,2,1,0:T(8,128)(2,1)} fusion(bf16[4,2,128,512]{3,2,1,0:T(8,128)(2,1)} %collective-permute-done.13, bf16[2,2,128,512]{3,2,1,0:T(8,128)(2,1)S(1)} %copy-done.4, bf16[2,2,128,512]{3,2,1,0:T(8,128)(2,1)S(1)} %collective-permute-done.11), kind=kLoop, calls=%fused_computation.1 | loop fusion | flops 2097152 | bytes 4194304 | tf_op jit(solution)/shard_map/concatenate | solution.py:41
  74.8 17.5 %attend.1 = bf16[128,4096]{1,0:T(8,128)(2,1)} custom-call(s32[1,16]{1,0:T(1,128)S(1)} %copy-done.1, s32[1]{0:T(128)S(6)} %copy.39.length, bf16[128,4096]{1,0:T(8,128)(2,1)S(1)} %bitcast.19, bf16[2,512,512]{2,1,0:T(8,128)(2,1)S(1)} %reshape.3.pk_ref.pv_ref, bf16[2,512,512]{2,1,0:T(8,128)(2,1)S(1)} %reshape.3.pk_ref.pv_ref, ...), custom_call_target="tpu_custom_call" | custom-call | flops 5368709120 | bytes 8388608 | tf_op jit(solution)/shard_map/attend/pallas_call | solution.py:139
  (28 shorter events, 1.6 us)
Async XLA Ops:
  1.0 12.1 %collective-permute-start.8 = (bf16[1,2,128,512]{3,2,1,0:T(8,128)(2,1)S(1)}, bf16[1,2,128,512]{3,2,1,0:T(8,128)(2,1)S(1)}, u32[]{:S(2)}, u32[]{:S(2)}) collective-permute-start(bf16[1,2,128,512]{3,2,1,0:T(8,128)(2,1)S(1)} %maximum_bitcast_fusion), channel_id=1, source_target_pairs={{0,1},{1,0},{2,3},{3,2},{4,5},{5,4},{6,7},{7,6},{8,9},{9,8},{10,11... | collective-permute-start | bytes 786440 | tf_op jit(solution)/shard_map/ppermute | solution.py:37
  3.7 6.6 %collective-permute-start = (bf16[1,2,2,512]{3,2,1,0:T(2,128)(2,1)S(1)}, bf16[1,2,2,512]{3,2,1,0:T(2,128)(2,1)S(1)}, u32[]{:S(2)}, u32[]{:S(2)}) collective-permute-start(bf16[1,2,2,512]{3,2,1,0:T(2,128)(2,1)S(1)} %maximum_bitcast_fusion.1), channel_id=1, source_target_pairs={{0,1},{1,0},{2,3},{3,2},{4,5},{5,4},{6,7},{7,6},{8,9},{9,8},{10,11... | collective-permute-start | bytes 12296 | tf_op jit(solution)/shard_map/ppermute | solution.py:37
  10.3 4.7 %collective-permute-start.1 = (bf16[2,2,2,512]{3,2,1,0:T(2,128)(2,1)S(1)}, bf16[2,2,2,512]{3,2,1,0:T(2,128)(2,1)S(1)}, u32[]{:S(2)}, u32[]{:S(2)}) collective-permute-start(bf16[2,2,2,512]{3,2,1,0:T(2,128)(2,1)S(1)} %pad_maximum_fusion.7), channel_id=1, source_target_pairs={{0,2},{1,3},{2,0},{3,1},{4,6},{5,7},{6,4},{7,5},{8,10},{9,11},{10,... | collective-permute-start | bytes 24584 | tf_op jit(solution)/shard_map/ppermute | solution.py:37
  13.1 20.4 %collective-permute-start.11 = (bf16[2,2,128,512]{3,2,1,0:T(8,128)(2,1)S(1)}, bf16[2,2,128,512]{3,2,1,0:T(8,128)(2,1)S(1)}, u32[]{:S(2)}, u32[]{:S(2)}) collective-permute-start(bf16[2,2,128,512]{3,2,1,0:T(8,128)(2,1)S(1)} %pad_maximum_fusion.4), channel_id=1, source_target_pairs={{0,2},{1,3},{2,0},{3,1},{4,6},{5,7},{6,4},{7,5},{8,10},{9,11},{10,... | collective-permute-start | bytes 1572872 | tf_op jit(solution)/shard_map/ppermute | solution.py:37
  15.1 16.6 %collective-permute-start.2 = (bf16[4,2,2,512]{3,2,1,0:T(2,128)(2,1)S(1)}, bf16[4,2,2,512]{3,2,1,0:T(2,128)(2,1)S(1)}, u32[]{:S(2)}, u32[]{:S(2)}) collective-permute-start(bf16[4,2,2,512]{3,2,1,0:T(2,128)(2,1)S(1)} %pad_maximum_fusion.6), channel_id=1, source_target_pairs={{0,128},{1,129},{2,130},{3,131},{4,132},{5,133},{6,134},{7,135},{8... | collective-permute-start | bytes 49160 | tf_op jit(solution)/shard_map/ppermute | solution.py:37
  22.0 21.3 %collective-permute-start.9 = (bf16[2,2,128,512]{3,2,1,0:T(8,128)(2,1)S(1)}, bf16[2,2,128,512]{3,2,1,0:T(8,128)(2,1)S(1)}, u32[]{:S(2)}, u32[]{:S(2)}) collective-permute-start(bf16[2,2,128,512]{3,2,1,0:T(8,128)(2,1)S(1)} %pad_maximum_fusion.4), channel_id=1, source_target_pairs={{0,4},{1,5},{2,6},{3,7},{4,0},{5,1},{6,2},{7,3},{8,12},{9,13},{10,... | collective-permute-start | bytes 1572872 | tf_op jit(solution)/shard_map/ppermute | solution.py:37
  31.8 4.0 %collective-permute-start.3 = (bf16[8,2,2,512]{3,2,1,0:T(2,128)(2,1)S(1)}, bf16[8,2,2,512]{3,2,1,0:T(2,128)(2,1)S(1)}, u32[]{:S(2)}, u32[]{:S(2)}) collective-permute-start(bf16[8,2,2,512]{3,2,1,0:T(2,128)(2,1)S(1)} %pad_maximum_fusion.5), channel_id=1, source_target_pairs={{0,4},{1,5},{2,6},{3,7},{4,0},{5,1},{6,2},{7,3},{8,12},{9,13},{10,... | collective-permute-start | bytes 98312 | tf_op jit(solution)/shard_map/ppermute | solution.py:37
  33.5 16.1 %collective-permute-start.12 = (bf16[2,2,128,512]{3,2,1,0:T(8,128)(2,1)S(1)}, bf16[2,2,128,512]{3,2,1,0:T(8,128)(2,1)S(1)}, u32[]{:S(2)}, u32[]{:S(2)}) collective-permute-start(bf16[2,2,128,512]{3,2,1,0:T(8,128)(2,1)S(1)} %collective-permute-done.11), channel_id=1, source_target_pairs={{0,4},{1,5},{2,6},{3,7},{4,0},{5,1},{6,2},{7,3},{8,12},{9,13},{10,... | collective-permute-start | bytes 1572872 | tf_op jit(solution)/shard_map/ppermute | solution.py:37
  35.9 6.3 %collective-permute-start.4 = (bf16[16,2,2,512]{3,2,1,0:T(2,128)(2,1)S(1)}, bf16[16,2,2,512]{3,2,1,0:T(2,128)(2,1)S(1)}, u32[]{:S(2)}, u32[]{:S(2)}) collective-permute-start(bf16[16,2,2,512]{3,2,1,0:T(2,128)(2,1)S(1)} %get-tuple-element.18), channel_id=1, source_target_pairs={{0,12},{1,13},{2,14},{3,15},{4,8},{5,9},{6,10},{7,11},{8,4},{9,5},... | collective-permute-start | bytes 196616 | tf_op jit(solution)/shard_map/ppermute | solution.py:37
  42.4 6.4 %collective-permute-start.5 = (bf16[32,2,2,512]{3,2,1,0:T(2,128)(2,1)S(1)}, bf16[32,2,2,512]{3,2,1,0:T(2,128)(2,1)S(1)}, u32[]{:S(2)}, u32[]{:S(2)}) collective-permute-start(bf16[32,2,2,512]{3,2,1,0:T(2,128)(2,1)S(1)} %get-tuple-element.13), channel_id=1, source_target_pairs={{0,32},{1,33},{2,34},{3,35},{4,36},{5,37},{6,38},{7,39},{8,40},{9,... | collective-permute-start | bytes 393224 | tf_op jit(solution)/shard_map/ppermute | solution.py:37
  43.3 7.5 %copy-start.2 = (bf16[2,2,128,512]{3,2,1,0:T(8,128)(2,1)}, bf16[2,2,128,512]{3,2,1,0:T(8,128)(2,1)S(1)}, u32[]{:S(2)}) copy-start(bf16[2,2,128,512]{3,2,1,0:T(8,128)(2,1)S(1)} %collective-permute-done.9) | copy-start | bytes 1572868
  44.4 16.4 %collective-permute-start.10 = (bf16[4,2,128,512]{3,2,1,0:T(8,128)(2,1)}, bf16[4,2,128,512]{3,2,1,0:T(8,128)(2,1)}, u32[]{:S(2)}, u32[]{:S(2)}) collective-permute-start(bf16[4,2,128,512]{3,2,1,0:T(8,128)(2,1)} %pad_maximum_fusion.2), channel_id=1, source_target_pairs={{0,12},{1,13},{2,14},{3,15},{4,8},{5,9},{6,10},{7,11},{8,4},{9,5},... | collective-permute-start | bytes 3145736 | tf_op jit(solution)/shard_map/ppermute | solution.py:37
  49.1 7.7 %collective-permute-start.6 = (bf16[64,2,2,512]{3,2,1,0:T(2,128)(2,1)S(1)}, bf16[64,2,2,512]{3,2,1,0:T(2,128)(2,1)S(1)}, u32[]{:S(2)}, u32[]{:S(2)}) collective-permute-start(bf16[64,2,2,512]{3,2,1,0:T(2,128)(2,1)S(1)} %get-tuple-element.9), channel_id=1, source_target_pairs={{0,96},{1,97},{2,98},{3,99},{4,100},{5,101},{6,102},{7,103},{8,104... | collective-permute-start | bytes 786440 | tf_op jit(solution)/shard_map/ppermute | solution.py:37
  49.6 10.0 %copy-start.3 = (bf16[2,2,128,512]{3,2,1,0:T(8,128)(2,1)}, bf16[2,2,128,512]{3,2,1,0:T(8,128)(2,1)S(1)}, u32[]{:S(2)}) copy-start(bf16[2,2,128,512]{3,2,1,0:T(8,128)(2,1)S(1)} %collective-permute-done.12) | copy-start | bytes 1572868
  50.8 21.2 %collective-permute-start.13 = (bf16[4,2,128,512]{3,2,1,0:T(8,128)(2,1)}, bf16[4,2,128,512]{3,2,1,0:T(8,128)(2,1)}, u32[]{:S(2)}, u32[]{:S(2)}) collective-permute-start(bf16[4,2,128,512]{3,2,1,0:T(8,128)(2,1)} %pad_maximum_fusion.3), channel_id=1, source_target_pairs={{0,12},{1,13},{2,14},{3,15},{4,8},{5,9},{6,10},{7,11},{8,4},{9,5},... | collective-permute-start | bytes 3145736 | tf_op jit(solution)/shard_map/ppermute | solution.py:37
  57.1 2.2 %collective-permute-start.7 = (bf16[128,2,2,512]{3,2,1,0:T(2,128)(2,1)S(1)}, bf16[128,2,2,512]{3,2,1,0:T(2,128)(2,1)S(1)}, u32[]{:S(2)}, u32[]{:S(2)}) collective-permute-start(bf16[128,2,2,512]{3,2,1,0:T(2,128)(2,1)S(1)} %get-tuple-element.5), channel_id=1, source_target_pairs={{0,16},{1,17},{2,18},{3,19},{4,20},{5,21},{6,22},{7,23},{8,24},{9,... | collective-permute-start | bytes 1572872 | tf_op jit(solution)/shard_map/ppermute | solution.py:37
  60.8 11.2 %copy-start.4 = (bf16[2,2,128,512]{3,2,1,0:T(8,128)(2,1)S(1)}, bf16[2,2,128,512]{3,2,1,0:T(8,128)(2,1)}, u32[]{:S(2)}) copy-start(bf16[2,2,128,512]{3,2,1,0:T(8,128)(2,1)} %copy-done.3) | copy-start | bytes 1572868
  62.5 12.3 %copy-start = (bf16[1,128,4096]{2,1,0:T(8,128)(2,1)S(1)}, bf16[1,128,4096]{2,1,0:T(8,128)(2,1)}, u32[]{:S(2)}) copy-start(bf16[1,128,4096]{2,1,0:T(8,128)(2,1)} %param.7) | copy-start | bytes 3145732
  62.5 12.3 %copy-start.1 = (s32[1,16]{1,0:T(1,128)S(1)}, s32[1,16]{1,0:T(1,128)}, u32[]{:S(2)}) copy-start(s32[1,16]{1,0:T(1,128)} %offsets.1) | copy-start | bytes 196

commit v2 on v1

v2 whole, which is shorter than its diff:
```python
import math

import jax
import jax.numpy as jnp
from jax import lax
from jax.experimental import pallas as pl
from jax.experimental.pallas import tpu as pltpu
from jax.sharding import PartitionSpec as P

HD = 128
KV_HEADS = 4
GROUP = 8
WIDE = GROUP * HD
TOK = 128
RIDE = 16
PAIR = 2
PAIRS = GROUP // PAIR
SCALE = math.log2(math.e) / math.sqrt(HD)
NEG = -1e30
GROUPS = ([3], [1], [2], [0])
AXES = ("member", "ctx")
VMEM = pl.BlockSpec(memory_space=pltpu.VMEM)
SMEM = pl.BlockSpec(memory_space=pltpu.SMEM)


def moves(step):
    pairs = []
    for i in range(256):
        zh, x, c, y, z = i // 128, i // 32 % 4, i // 16 % 2, i // 4 % 4, i % 4
        zh2, x2, c2, y2, z2 = step(zh, x, c, y, z)
        pairs.append((i, (((zh2 * 4 + x2) * 2 + c2) * 4 + y2) * 4 + z2))
    return pairs


Z_STEPS = [moves(lambda zh, x, c, y, z, k=k: (zh, x, c, y, z ^ (1, 2)[c ^ k])) for k in (0, 1)]
Z_STEPS.append(moves(lambda zh, x, c, y, z: (zh, x, c, y, z ^ 3)))
Y_STEPS = [moves(lambda zh, x, c, y, z, k=k: (zh, x, c, y ^ (1, 3)[c ^ k], z)) for k in (0, 1)]
Y_STEPS.append(moves(lambda zh, x, c, y, z: (zh, x, c, y ^ 2, z)))
X_STEPS = [moves(lambda zh, x, c, y, z, k=k: (zh, x ^ (1, 3)[c ^ k], c, y, z)) for k in (0, 1)]
X_STEPS.append(moves(lambda zh, x, c, y, z: (zh, x ^ 2, c, y, z)))
ZH_STEP = moves(lambda zh, x, c, y, z: (zh ^ 1, x, c, y, z))
CORE_STEP = moves(lambda zh, x, c, y, z: (zh, x, c ^ 1, y, z))


def send(value, pairs):
    return lax.ppermute(value, AXES, pairs)


def join(*values):
    return jnp.concatenate(values, axis=0)


def double(value, pairs):
    return join(value, send(value, pairs))


def place():
    ctx, member = lax.axis_index("ctx"), lax.axis_index("member")
    return member % 2, ctx // 4, ctx % 4


def delta(bits, core, first, second):
    step0 = first + core * (second - first)
    step1 = second + core * (first - second)
    return (step0 if bits & 1 else 0) ^ (step1 if bits & 2 else 0)


def head_of(bits):
    core, y, _ = place()
    return y ^ delta(bits, core, 1, 3)


def columns(head, width):
    return pl.ds(pl.multiple_of(head * width, width), width)


def two_rows(pair):
    row = lax.broadcasted_iota(jnp.int32, (RIDE, HD), 0)
    wide = pair.astype(jnp.float32)
    return jnp.where(row == 0, wide[:1], jnp.where(row == 1, wide[1:], 0.0)).astype(jnp.bfloat16)


def split_kv_kernel(k_ref, v_ref, pk_ref, pv_ref, *outs):
    for bits in range(4):
        part = columns(head_of(bits), HD)
        outs[bits][:TOK, :HD] = k_ref[:, part]
        outs[bits][:TOK, HD:] = v_ref[:, part]
        outs[bits][TOK:, :HD] = two_rows(pk_ref[:, part])
        outs[bits][TOK:, HD:] = two_rows(pv_ref[:, part])


def split_kv(keys, values, prompt_keys, prompt_values):
    return pl.pallas_call(
        split_kv_kernel,
        in_specs=[VMEM] * 4,
        out_specs=[VMEM] * 4,
        out_shape=[jax.ShapeDtypeStruct((TOK + RIDE, 2 * HD), jnp.bfloat16)] * 4,
        name="split_kv",
    )(keys, values, prompt_keys, prompt_values)


def split_q_kernel(q_ref, *outs):
    for bits in range(4):
        outs[bits][...] = q_ref[:, columns(head_of(bits), WIDE)]


def split_q(q):
    return pl.pallas_call(
        split_q_kernel,
        in_specs=[VMEM],
        out_specs=[VMEM] * 4,
        out_shape=[jax.ShapeDtypeStruct((TOK, WIDE), jnp.bfloat16)] * 4,
        name="split_q",
    )(q)


def merge_kernel(*refs):
    out_ref = refs[4]
    for bits in range(4):
        out_ref[:, columns(head_of(bits), WIDE)] = refs[bits][...]


def merge(parts):
    return pl.pallas_call(
        merge_kernel,
        in_specs=[VMEM] * 4,
        out_specs=VMEM,
        out_shape=jax.ShapeDtypeStruct((TOK, KV_HEADS * WIDE), jnp.bfloat16),
        name="merge",
    )(*parts)


def make_kernel(queries, sizes, blocks, carried, last):
    keys = TOK * len(blocks)
    count = len(queries)

    def kernel(offsets, length, *refs):
        q_refs, refs = refs[:count], refs[count:]
        pieces, refs = refs[: len(sizes)], refs[len(sizes) :]
        if carried:
            stat_in, sum_in, refs = refs[:count], refs[count : 2 * count], refs[2 * count :]
        if last:
            outs, refs = refs[:count], refs[count:]
        else:
            stat_out, sum_out, mark_ref = refs[:count], refs[count : 2 * count], refs[2 * count]
            refs = refs[2 * count + 1 :]
            mark_ref[...] = jnp.zeros(mark_ref.shape, jnp.float32)
        k_aug, v_aug = refs
        core, y, z = place()
        token = lax.broadcasted_iota(jnp.int32, (TOK, TOK), 1)
        k_row = lax.broadcasted_iota(jnp.int32, (TOK, TOK), 0)
        for index, bits in enumerate(blocks):
            to = slice(index * TOK, (index + 1) * TOK)
            if bits is not None:
                source = (y ^ delta(bits[0], core, 1, 3)) * 4 + (z ^ delta(bits[1], core, 1, 2))
                k_pos = k_row + offsets[0, source] * TOK
            for i in range(count):
                if bits is None:
                    bias = jnp.zeros((TOK, TOK), jnp.bfloat16)
                else:
                    q_pos = token + offsets[0, (y ^ delta(queries[i], core, 1, 3)) * 4 + z] * TOK
                    counted = (k_pos <= q_pos) & (k_pos < length[0])
                    bias = jnp.where(counted, 0.0, NEG).astype(jnp.bfloat16)
                k_aug[i, to, HD:] = bias
        v_aug[:, HD:] = jnp.ones((keys, HD), jnp.bfloat16)
        start = 0
        for piece, size in zip(pieces, sizes):
            v_aug[start : start + size, :HD] = piece[:, HD:]
            for i in range(count):
                k_aug[i, start : start + size, :HD] = piece[:, :HD]
            start += size
        eye = jnp.where(token == k_row, 1.0, 0.0).astype(jnp.bfloat16)
        low = lax.broadcasted_iota(jnp.int32, (1, HD), 1) < HD // 2

        def score(i, h):
            heads = [
                jnp.concatenate([q_refs[i][:, (h * PAIR + u) * HD : (h * PAIR + u + 1) * HD], eye], axis=1)
                for u in range(PAIR)
            ]
            return lax.dot_general(
                jnp.concatenate(heads, axis=0),
                k_aug[i],
                (((1,), (1,)), ((), ())),
                preferred_element_type=jnp.float32,
            )

        def finish(i, h, s):
            top = jnp.max(s, axis=1, keepdims=True)
            if carried:
                stat = stat_in[i][h]
                before = jnp.max(jnp.where(low, stat, -3e38), axis=1, keepdims=True)
                total = jnp.max(jnp.where(low, -3e38, stat), axis=1, keepdims=True)
                top = jnp.maximum(before, top)
                rescale = jnp.exp2((before - top) * SCALE)
            weights = jnp.exp2(s * SCALE - top * SCALE).astype(jnp.bfloat16)
            both = lax.dot_general(
                weights, v_aug[...], (((1,), (0,)), ((), ())), preferred_element_type=jnp.float32
            )
            weighted, totals = both[:, :HD], both[:, HD:]
            if carried:
                weighted = weighted + sum_in[i][h] * rescale
                totals = totals + total * rescale
            if last:
                result = (weighted / totals).astype(jnp.bfloat16)
                for u in range(PAIR):
                    outs[i][:, (h * PAIR + u) * HD : (h * PAIR + u + 1) * HD] = result[u * TOK : (u + 1) * TOK]
            else:
                stat_out[i][h] = jnp.where(low, top, totals)
                sum_out[i][h] = weighted

        steps = [(i, h) for i in range(count) for h in range(PAIRS)]
        s = score(*steps[0])
        for n, step in enumerate(steps):
            ahead = score(*steps[n + 1]) if n + 1 < len(steps) else None
            finish(*step, s)
            s = ahead

    return kernel


def attend(offsets, length, queries, q, pieces, blocks, carry=(), last=False):
    sizes = [p.shape[0] for p in pieces]
    keys, count = TOK * len(blocks), len(queries)
    state = jax.ShapeDtypeStruct((PAIRS, PAIR * TOK, HD), jnp.float32)
    result = jax.ShapeDtypeStruct((TOK, WIDE), jnp.bfloat16)
    mark = jax.ShapeDtypeStruct((8, HD), jnp.float32)
    outs = [result] * count if last else [state] * (2 * count) + [mark]
    return pl.pallas_call(
        make_kernel(queries, sizes, blocks, bool(carry), last),
        in_specs=[SMEM, SMEM] + [VMEM] * (count + len(pieces) + len(carry)),
        out_specs=[VMEM] * len(outs),
        out_shape=outs,
        scratch_shapes=[
            pltpu.VMEM((count, keys, 2 * HD), jnp.bfloat16),
            pltpu.VMEM((keys, 2 * HD), jnp.bfloat16),
        ],
        compiler_params=pltpu.CompilerParams(vmem_limit_bytes=26 << 20),
        cost_estimate=pl.CostEstimate(
            flops=4 * WIDE * count * keys * HD, bytes_accessed=count << 20, transcendentals=WIDE * count * keys
        ),
        name="attend_last" if last else "attend_first",
    )(offsets, length, *q, *pieces, *carry)


def column_blocks(zbits):
    return [(yb, zb) for zb in zbits for yb in range(4)]


def body(
    queries, response_keys, response_values, prompt_keys, prompt_values, block_offsets, lengths
):
    mine = split_kv(response_keys[0], response_values[0], prompt_keys, prompt_values)
    q_mine = split_q(queries[0])
    kv = [mine[0]] + [send(mine[bits], Y_STEPS[bits - 1]) for bits in (1, 2, 3)]
    kv, q_mine = lax.optimization_barrier((kv, q_mine))
    column = join(*(part[:TOK] for part in kv))
    prompt = join(*(part[TOK : TOK + 2] for part in kv))
    z_first = send(column, Z_STEPS[0])
    z_second = send(column, Z_STEPS[1])
    for pairs in (CORE_STEP, X_STEPS[0], X_STEPS[1]):
        prompt = double(prompt, pairs)
    q = [q_mine[0]] + [send(q_mine[bits], Y_STEPS[bits - 1]) for bits in (1, 2, 3)]
    z_first, z_second, prompt = lax.optimization_barrier((z_first, z_second, prompt))
    z_both = send(z_first, Z_STEPS[1])
    prompt = double(prompt, ZH_STEP)
    prompts = [send(prompt, pairs) for pairs in Z_STEPS]
    out = attend(block_offsets, lengths, [0, 1, 2, 3], q, [column, z_first, z_second], column_blocks((0, 1, 2)))
    state = {i: (out[i], out[4 + i]) for i in range(4)}
    pieces = [z_both, prompt] + prompts
    blocks = column_blocks((3,)) + [None] * 4
    results = [None] * 4
    for group in GROUPS:
        carry = [state[i][0] for i in group] + [state[i][1] for i in group]
        out = attend(block_offsets, lengths, group, [q[i] for i in group], pieces, blocks, carry, True)
        for i, value in zip(group, out):
            results[i] = send(value, Y_STEPS[i - 1]) if i else value
    return merge(results)[None]


def solution(mesh):
    return jax.shard_map(
        body,
        mesh=mesh,
        in_specs=(
            P("member", "ctx", None),
            P("member", "ctx", None),
            P("member", "ctx", None),
            P(("member", "ctx"), None),
            P(("member", "ctx"), None),
            P("member", None),
            P("member"),
        ),
        out_specs=P("member", "ctx", None),
        check_vma=False,
    )
```

time: 92.9 us -> 74 us (0.80)
  waiting for transfers between devices: 37.5 us -> 15.2 us
  other arithmetic: 9.22 us -> 0.03 us
  Pallas kernels: 17.5 us -> 25.9 us
  starting transfers between devices: 24.7 us -> 29.3 us
    ppermute x14 -> x19, waiting for transfers between devices: 37.5 us -> 15.2 us  [send(): return lax.ppermute(value, AXES, pairs)]
    pallas_call x1 -> x8, Pallas kernels: 17.5 us -> 25.9 us  [the longest x5 19.6 us: attend(): pl.pallas_call(make_kernel(queries, sizes, blocks, bool(carry), last), in...]
    concatenate x8 -> x2, other arithmetic: 6.81 us -> 0.03 us  [join(): return jnp.concatenate(values, axis=0)]
    ppermute x14 -> x19, starting transfers between devices: 24.7 us -> 29.3 us  [send(): return lax.ppermute(value, AXES, pairs)]
    broadcast_in_dim x2 -> x0, other arithmetic: 1.7 us -> none  [the longest x1 0.99 us: body(): own = jnp.concatenate([response_keys, response_values], axis=0)[None]]
  transfers between devices with their start and end apart: 14 -> 19, of which waited for: 9 -> 8; matrix products, arithmetic and copies ran while one was open for 9% -> 0% of each run, Pallas kernels for 0% -> 26%
where the time goes in v2:
time: 74 us; the launch traced here: 73.8 us
  starting transfers between devices  29.3 us (40%)
  Pallas kernels  25.9 us (35%)
  waiting for transfers between devices  15.2 us (21%)
  local copies, waits for them, and re-layouts  2.49 us (3%)
  between operations  0.85 us (1%)
    ppermute x19, starting transfers between devices, send(): return lax.ppermute(value, AXES, pairs)  29.3 us
    pallas_call x5, Pallas kernels, attend(): pl.pallas_call(make_kernel(queries, sizes, blocks, bool(carry), last), in...  19.6 us
    ppermute x19, waiting for transfers between devices, send(): return lax.ppermute(value, AXES, pairs)  15.2 us
    pallas_call x1, Pallas kernels, split_q(): pl.pallas_call(split_q_kernel, in_specs=[VMEM], out_specs=[VMEM] * 4, out...  2.29 us
    pallas_call x1, Pallas kernels, merge(): pl.pallas_call(merge_kernel, in_specs=[VMEM] * 4, out_specs=VMEM, out_sha...  2.23 us
    pallas_call x1, Pallas kernels, split_kv(): pl.pallas_call(split_kv_kernel, in_specs=[VMEM] * 4, out_specs=[VMEM] * 4...  1.74 us
    unnamed x27, local copies, waits for them, and re-layouts  1.48 us
  transfers between devices with their start and end apart: 19, of which 8 were waited for; matrix products, arithmetic and copies ran while one was open for 0% of the time, Pallas kernels for 26%

profile of v2, /device:TPU:6, one launch (start us, length us, event | category | flops | bytes accessed | tf_op | source)
XLA Modules:
  0.0 73.8 jit_solution(11979494554292670080)
XLA Ops:
  0.0 1.7 %split_kv.1 = (bf16[144,256]{1,0:T(8,128)(2,1)}, bf16[144,256]{1,0:T(8,128)(2,1)}, bf16[144,256]{1,0:T(8,128)(2,1)}, bf16[144,256]{1,0:T(8,128)(2,1)}) custom-call(bf16[128,512]{1,0:T(8,128)(2,1)} %bitcast.5, bf16[128,512]{1,0:T(8,128)(2,1)} %bitcast.6, bf16[2,512]{1,0:T(2,128)(2,1)} %pk_ref.1, bf16[2,512]{1,0:T(2,128)(2,1)} %pv_ref.1), custom_call_target="tpu_custom_call" | custom-call | tf_op jit(solution)/shard_map/split_kv/pallas_call | solution.py:93
  1.7 1.6 %collective-permute-start = (bf16[144,256]{1,0:T(8,128)(2,1)}, bf16[144,256]{1,0:T(8,128)(2,1)S(1)}, u32[]{:S(2)}, u32[]{:S(2)}) collective-permute-start(bf16[144,256]{1,0:T(8,128)(2,1)} %get-tuple-element.33), channel_id=1, source_target_pairs={{0,4},{1,5},{2,6},{3,7},{4,0},{5,1},{6,2},{7,3},{8,12},{9,13},{10,... | collective-permute-start | bytes 221192 | tf_op jit(solution)/shard_map/ppermute | solution.py:46
  3.3 2.2 %collective-permute-start.1 = (bf16[144,256]{1,0:T(8,128)(2,1)}, bf16[144,256]{1,0:T(8,128)(2,1)S(1)}, u32[]{:S(2)}, u32[]{:S(2)}) collective-permute-start(bf16[144,256]{1,0:T(8,128)(2,1)} %get-tuple-element.34), channel_id=1, source_target_pairs={{0,12},{1,13},{2,14},{3,15},{4,8},{5,9},{6,10},{7,11},{8,4},{9,5},... | collective-permute-start | bytes 221192 | tf_op jit(solution)/shard_map/ppermute | solution.py:46
  5.5 0.7 collective-permute-start.2
  6.2 2.3 %split_q.1 = (bf16[128,1024]{1,0:T(8,128)(2,1)}, bf16[128,1024]{1,0:T(8,128)(2,1)}, bf16[128,1024]{1,0:T(8,128)(2,1)}, bf16[128,1024]{1,0:T(8,128)(2,1)}) custom-call(bf16[128,4096]{1,0:T(8,128)(2,1)} %bitcast.4), custom_call_target="tpu_custom_call" | custom-call | tf_op jit(solution)/shard_map/split_q/pallas_call | solution.py:108
  8.5 1.4 %collective-permute-done.1 = bf16[144,256]{1,0:T(8,128)(2,1)S(1)} collective-permute-done((bf16[144,256]{1,0:T(8,128)(2,1)}, bf16[144,256]{1,0:T(8,128)(2,1)S(1)}, u32[]{:S(2)}, u32[]{:S(2)}) %collective-permute-start.1) | collective-permute-done | bytes 73760 | tf_op jit(solution)/shard_map/ppermute | solution.py:46
  9.9 1.7 %collective-permute-done.2 = bf16[144,256]{1,0:T(8,128)(2,1)S(1)} collective-permute-done((bf16[144,256]{1,0:T(8,128)(2,1)}, bf16[144,256]{1,0:T(8,128)(2,1)S(1)}, u32[]{:S(2)}, u32[]{:S(2)}) %collective-permute-start.2) | collective-permute-done | bytes 73760 | tf_op jit(solution)/shard_map/ppermute | solution.py:46
  11.6 0.9 %slice-done = bf16[128,256]{1,0:T(8,128)(2,1)S(1)} async-done(((bf16[144,256]{1,0:T(8,128)(2,1)}), bf16[128,256]{1,0:T(8,128)(2,1)S(1)}, s32[]{:S(2)}) %slice-start) | async-done | bytes 65560 | tf_op jit(solution)/shard_map/slice | solution.py:256
  12.6 2.0 %collective-permute-start.3 = (bf16[512,256]{1,0:T(8,128)(2,1)S(1)}, bf16[512,256]{1,0:T(8,128)(2,1)S(1)}, u32[]{:S(2)}, u32[]{:S(2)}) collective-permute-start(bf16[512,256]{1,0:T(8,128)(2,1)S(1)} %pad_maximum_fusion.refs_4_), channel_id=1, source_target_pairs={{0,1},{1,0},{2,3},{3,2},{4,5},{5,4},{6,7},{7,6},{8,9},{9,8},{10,11... | collective-permute-start | bytes 786440 | tf_op jit(solution)/shard_map/ppermute | solution.py:46
  14.6 3.3 %collective-permute-start.4 = (bf16[512,256]{1,0:T(8,128)(2,1)S(1)}, bf16[512,256]{1,0:T(8,128)(2,1)S(1)}, u32[]{:S(2)}, u32[]{:S(2)}) collective-permute-start(bf16[512,256]{1,0:T(8,128)(2,1)S(1)} %pad_maximum_fusion.refs_4_), channel_id=1, source_target_pairs={{0,2},{1,3},{2,0},{3,1},{4,6},{5,7},{6,4},{7,5},{8,10},{9,11},{10,... | collective-permute-start | bytes 786440 | tf_op jit(solution)/shard_map/ppermute | solution.py:46
  18.0 1.2 %collective-permute-done.5 = bf16[8,256]{1,0:T(8,128)(2,1)S(1)} collective-permute-done((bf16[8,256]{1,0:T(8,128)(2,1)S(1)}, bf16[8,256]{1,0:T(8,128)(2,1)S(1)}, u32[]{:S(2)}, u32[]{:S(2)}) %collective-permute-start.5) | collective-permute-done | bytes 4128 | tf_op jit(solution)/shard_map/ppermute | solution.py:46
  19.2 0.9 %collective-permute-start.6 = (bf16[16,256]{1,0:T(8,128)(2,1)S(1)}, bf16[16,256]{1,0:T(8,128)(2,1)S(1)}, u32[]{:S(2)}, u32[]{:S(2)}) collective-permute-start(bf16[16,256]{1,0:T(8,128)(2,1)S(1)} %concatenate.23), channel_id=1, source_target_pairs={{0,32},{1,33},{2,34},{3,35},{4,36},{5,37},{6,38},{7,39},{8,40},{9,... | collective-permute-start | bytes 24584 | tf_op jit(solution)/shard_map/ppermute | solution.py:46
  20.1 2.8 %collective-permute-done.6 = bf16[16,256]{1,0:T(8,128)(2,1)S(1)} collective-permute-done((bf16[16,256]{1,0:T(8,128)(2,1)S(1)}, bf16[16,256]{1,0:T(8,128)(2,1)S(1)}, u32[]{:S(2)}, u32[]{:S(2)}) %collective-permute-start.6) | collective-permute-done | bytes 8224 | tf_op jit(solution)/shard_map/ppermute | solution.py:46
  23.5 0.7 collective-permute-start.13
  24.2 1.2 %collective-permute-start.14 = (bf16[128,1024]{1,0:T(8,128)(2,1)S(1)}, bf16[128,1024]{1,0:T(8,128)(2,1)S(1)}, u32[]{:S(2)}, u32[]{:S(2)}) collective-permute-start(bf16[128,1024]{1,0:T(8,128)(2,1)S(1)} %copy-done.12), channel_id=1, source_target_pairs={{0,12},{1,13},{2,14},{3,15},{4,8},{5,9},{6,10},{7,11},{8,4},{9,5},... | collective-permute-start | bytes 786440 | tf_op jit(solution)/shard_map/ppermute | solution.py:46
  25.4 2.6 %collective-permute-done.7 = bf16[32,256]{1,0:T(8,128)(2,1)S(1)} collective-permute-done((bf16[32,256]{1,0:T(8,128)(2,1)S(1)}, bf16[32,256]{1,0:T(8,128)(2,1)S(1)}, u32[]{:S(2)}, u32[]{:S(2)}) %collective-permute-start.7) | collective-permute-done | bytes 16416 | tf_op jit(solution)/shard_map/ppermute | solution.py:46
  28.0 1.3 %collective-permute-start.15 = (bf16[128,1024]{1,0:T(8,128)(2,1)S(1)}, bf16[128,1024]{1,0:T(8,128)(2,1)S(1)}, u32[]{:S(2)}, u32[]{:S(2)}) collective-permute-start(bf16[128,1024]{1,0:T(8,128)(2,1)S(1)} %copy-done.11), channel_id=1, source_target_pairs={{0,8},{1,9},{2,10},{3,11},{4,12},{5,13},{6,14},{7,15},{8,0},{9,1},... | collective-permute-start | bytes 786440 | tf_op jit(solution)/shard_map/ppermute | solution.py:46
  30.0 4.6 %collective-permute-start.9 = (bf16[64,256]{1,0:T(8,128)(2,1)S(1)}, bf16[64,256]{1,0:T(8,128)(2,1)S(1)}, u32[]{:S(2)}, u32[]{:S(2)}) collective-permute-start(bf16[64,256]{1,0:T(8,128)(2,1)S(1)} %concatenate.25), channel_id=1, source_target_pairs={{0,128},{1,129},{2,130},{3,131},{4,132},{5,133},{6,134},{7,135},{8... | collective-permute-start | bytes 98312 | tf_op jit(solution)/shard_map/ppermute | solution.py:46
  34.6 1.5 %collective-permute-start.8 = (bf16[512,256]{1,0:T(8,128)(2,1)S(1)}, bf16[512,256]{1,0:T(8,128)(2,1)S(1)}, u32[]{:S(2)}, u32[]{:S(2)}) collective-permute-start(bf16[512,256]{1,0:T(8,128)(2,1)S(1)} %collective-permute-done.3.refs_5_), channel_id=1, source_target_pairs={{0,2},{1,3},{2,0},{3,1},{4,6},{5,7},{6,4},{7,5},{8,10},{9,11},{10,... | collective-permute-start | bytes 786440 | tf_op jit(solution)/shard_map/ppermute | solution.py:46
  36.1 2.4 %collective-permute-done.9 = bf16[64,256]{1,0:T(8,128)(2,1)S(1)} collective-permute-done((bf16[64,256]{1,0:T(8,128)(2,1)S(1)}, bf16[64,256]{1,0:T(8,128)(2,1)S(1)}, u32[]{:S(2)}, u32[]{:S(2)}) %collective-permute-start.9) | collective-permute-done | bytes 32800 | tf_op jit(solution)/shard_map/ppermute | solution.py:46
  39.4 3.5 %collective-permute-start.12 = (bf16[128,256]{1,0:T(8,128)(2,1)S(1)}, bf16[128,256]{1,0:T(8,128)(2,1)S(1)}, u32[]{:S(2)}, u32[]{:S(2)}) collective-permute-start(bf16[128,256]{1,0:T(8,128)(2,1)S(1)} %constant_dynamic-update-slice_fusion.refs_2_), channel_id=1, source_target_pairs={{0,3},{1,2},{2,1},{3,0},{4,7},{5,6},{6,5},{7,4},{8,11},{9,10},{10,... | collective-permute-start | bytes 196616 | tf_op jit(solution)/shard_map/ppermute | solution.py:46
  42.9 9.9 %attend_first.1 = (f32[4,256,128]{2,1,0:T(8,128)S(1)}, f32[4,256,128]{2,1,0:T(8,128)S(1)}, f32[4,256,128]{2,1,0:T(8,128)S(1)}, f32[4,256,128]{2,1,0:T(8,128)S(1)...) custom-call(s32[1,16]{1,0:T(1,128)S(1)} %copy-done.2, ...), custom_call_target="tpu_custom_call" | custom-call | flops 3221225472 | bytes 4194304 | tf_op jit(solution)/shard_map/attend_first/pallas_call | solution.py:228
  52.8 2.5 %attend_last.7 = bf16[128,1024]{1,0:T(8,128)(2,1)S(1)} custom-call(s32[1,16]{1,0:T(1,128)S(1)} %copy-done.2, s32[1]{0:T(128)S(6)} %copy.9.length, bf16[128,1024]{1,0:T(8,128)(2,1)S(1)} %collective-permute-done.15.refs_3_.refs_0_, bf16[512,256]{1,0:T(8,128)(2,1)S(1)} %collective-permute-done.8.refs_1_, ...), custom_call_target="tpu_custom_call" | custom-call | flops 536870912 | bytes 1048576 | tf_op jit(solution)/shard_map/attend_last/pallas_call | solution.py:228
  55.2 2.4 %collective-permute-start.18 = (bf16[128,1024]{1,0:T(8,128)(2,1)S(1)}, bf16[128,1024]{1,0:T(8,128)(2,1)S(1)}, u32[]{:S(2)}, u32[]{:S(2)}) collective-permute-start(bf16[128,1024]{1,0:T(8,128)(2,1)S(1)} %attend_last.7), channel_id=1, source_target_pairs={{0,8},{1,9},{2,10},{3,11},{4,12},{5,13},{6,14},{7,15},{8,0},{9,1},... | collective-permute-start | bytes 786440 | tf_op jit(solution)/shard_map/ppermute | solution.py:46
  57.6 2.4 %attend_last.6 = bf16[128,1024]{1,0:T(8,128)(2,1)S(1)} custom-call(s32[1,16]{1,0:T(1,128)S(1)} %copy-done.2, s32[1]{0:T(128)S(6)} %copy.9.length, bf16[128,1024]{1,0:T(8,128)(2,1)S(1)} %collective-permute-done.14.refs_2_.refs_0_, bf16[512,256]{1,0:T(8,128)(2,1)S(1)} %collective-permute-done.8.refs_1_, ...), custom_call_target="tpu_custom_call" | custom-call | flops 536870912 | bytes 1048576 | tf_op jit(solution)/shard_map/attend_last/pallas_call | solution.py:228
  60.0 1.9 %collective-permute-start.17 = (bf16[128,1024]{1,0:T(8,128)(2,1)S(1)}, bf16[128,1024]{1,0:T(8,128)(2,1)S(1)}, u32[]{:S(2)}, u32[]{:S(2)}) collective-permute-start(bf16[128,1024]{1,0:T(8,128)(2,1)S(1)} %attend_last.6), channel_id=1, source_target_pairs={{0,12},{1,13},{2,14},{3,15},{4,8},{5,9},{6,10},{7,11},{8,4},{9,5},... | collective-permute-start | bytes 786440 | tf_op jit(solution)/shard_map/ppermute | solution.py:46
  61.9 2.4 %attend_last.5 = bf16[128,1024]{1,0:T(8,128)(2,1)S(1)} custom-call(s32[1,16]{1,0:T(1,128)S(1)} %copy-done.2, s32[1]{0:T(128)S(6)} %copy.9.length, bf16[128,1024]{1,0:T(8,128)(2,1)S(1)} %collective-permute-done.13.refs_1_.refs_0_, bf16[512,256]{1,0:T(8,128)(2,1)S(1)} %collective-permute-done.8.refs_1_, ...), custom_call_target="tpu_custom_call" | custom-call | flops 536870912 | bytes 1048576 | tf_op jit(solution)/shard_map/attend_last/pallas_call | solution.py:228
  64.5 2.5 %attend_last.4.refs_0_ = bf16[128,1024]{1,0:T(8,128)(2,1)S(1)} custom-call(s32[1,16]{1,0:T(1,128)S(1)} %copy-done.2, s32[1]{0:T(128)S(6)} %copy.9.length, bf16[128,1024]{1,0:T(8,128)(2,1)S(1)} %copy-done.1, bf16[512,256]{1,0:T(8,128)(2,1)S(1)} %collective-permute-done.8.refs_1_, bf16[128,256]{1,0:T(8,128)(2,1)S(1)} %constant_dynamic-update-slice_fusion.refs_2_, ...), custom_call_target="tpu_custom_call" | custom-call | flops 536870912 | bytes 1048576 | tf_op jit(solution)/shard_map/attend_last/pallas_call | solution.py:228
  66.9 0.7 copy-done
  67.6 2.5 %collective-permute-done.17.refs_2_ = bf16[128,1024]{1,0:T(8,128)(2,1)S(1)} collective-permute-done((bf16[128,1024]{1,0:T(8,128)(2,1)S(1)}, bf16[128,1024]{1,0:T(8,128)(2,1)S(1)}, u32[]{:S(2)}, u32[]{:S(2)}) %collective-permute-start.17) | collective-permute-done | bytes 262176 | tf_op jit(solution)/shard_map/ppermute | solution.py:46
  70.9 0.7 copy-done.9
  71.6 2.2 %merge.1 = bf16[128,4096]{1,0:T(8,128)(2,1)} custom-call(bf16[128,1024]{1,0:T(8,128)(2,1)} %copy-done, bf16[128,1024]{1,0:T(8,128)(2,1)} %copy-done.9, bf16[128,1024]{1,0:T(8,128)(2,1)} %copy-done.8, bf16[128,1024]{1,0:T(8,128)(2,1)} %copy-done.7), custom_call_target="tpu_custom_call" | custom-call | tf_op jit(solution)/shard_map/merge/pallas_call | solution.py:124
  (57 shorter events, 2.6 us)
Async XLA Ops:
  1.7 6.8 %collective-permute-start = (bf16[144,256]{1,0:T(8,128)(2,1)}, bf16[144,256]{1,0:T(8,128)(2,1)S(1)}, u32[]{:S(2)}, u32[]{:S(2)}) collective-permute-start(bf16[144,256]{1,0:T(8,128)(2,1)} %get-tuple-element.33), channel_id=1, source_target_pairs={{0,4},{1,5},{2,6},{3,7},{4,0},{5,1},{6,2},{7,3},{8,12},{9,13},{10,... | collective-permute-start | bytes 221192 | tf_op jit(solution)/shard_map/ppermute | solution.py:46
  3.3 6.6 %collective-permute-start.1 = (bf16[144,256]{1,0:T(8,128)(2,1)}, bf16[144,256]{1,0:T(8,128)(2,1)S(1)}, u32[]{:S(2)}, u32[]{:S(2)}) collective-permute-start(bf16[144,256]{1,0:T(8,128)(2,1)} %get-tuple-element.34), channel_id=1, source_target_pairs={{0,12},{1,13},{2,14},{3,15},{4,8},{5,9},{6,10},{7,11},{8,4},{9,5},... | collective-permute-start | bytes 221192 | tf_op jit(solution)/shard_map/ppermute | solution.py:46
  5.5 6.1 %collective-permute-start.2 = (bf16[144,256]{1,0:T(8,128)(2,1)}, bf16[144,256]{1,0:T(8,128)(2,1)S(1)}, u32[]{:S(2)}, u32[]{:S(2)}) collective-permute-start(bf16[144,256]{1,0:T(8,128)(2,1)} %get-tuple-element.35), channel_id=1, source_target_pairs={{0,8},{1,9},{2,10},{3,11},{4,12},{5,13},{6,14},{7,15},{8,0},{9,1},... | collective-permute-start | bytes 221192 | tf_op jit(solution)/shard_map/ppermute | solution.py:46
  6.2 5.3 %copy-start.10 = (bf16[144,256]{1,0:T(8,128)(2,1)S(1)}, bf16[144,256]{1,0:T(8,128)(2,1)}, u32[]{:S(2)}) copy-start(bf16[144,256]{1,0:T(8,128)(2,1)} %get-tuple-element.41) | copy-start | bytes 221188
  8.5 3.1 %copy-start.3 = (bf16[144,256]{1,0:T(8,128)(2,1)}, bf16[144,256]{1,0:T(8,128)(2,1)S(1)}, u32[]{:S(2)}) copy-start(bf16[144,256]{1,0:T(8,128)(2,1)S(1)} %collective-permute-done) | copy-start | bytes 221188
  9.9 1.7 %copy-start.5 = (bf16[144,256]{1,0:T(8,128)(2,1)}, bf16[144,256]{1,0:T(8,128)(2,1)S(1)}, u32[]{:S(2)}) copy-start(bf16[144,256]{1,0:T(8,128)(2,1)S(1)} %collective-permute-done.1) | copy-start | bytes 221188
  11.6 12.6 %copy-start.12 = (bf16[128,1024]{1,0:T(8,128)(2,1)S(1)}, bf16[128,1024]{1,0:T(8,128)(2,1)}, u32[]{:S(2)}) copy-start(bf16[128,1024]{1,0:T(8,128)(2,1)} %get-tuple-element.48) | copy-start | bytes 786436
  11.6 0.9 %slice-start = ((bf16[144,256]{1,0:T(8,128)(2,1)}), bf16[128,256]{1,0:T(8,128)(2,1)S(1)}, s32[]{:S(2)}) async-start(bf16[144,256]{1,0:T(8,128)(2,1)} %copy-done.3), calls=%async_computation | async-start | bytes 131072 | tf_op jit(solution)/shard_map/slice | solution.py:256
  11.6 0.9 %slice-start.1 = ((bf16[144,256]{1,0:T(8,128)(2,1)}), bf16[128,256]{1,0:T(8,128)(2,1)S(1)}, s32[]{:S(2)}) async-start(bf16[144,256]{1,0:T(8,128)(2,1)} %copy-done.5), calls=%async_computation.1 | async-start | bytes 131072 | tf_op jit(solution)/shard_map/slice | solution.py:256
  12.5 5.3 %copy-start.4 = (bf16[144,256]{1,0:T(8,128)(2,1)S(1)}, bf16[144,256]{1,0:T(8,128)(2,1)}, u32[]{:S(2)}) copy-start(bf16[144,256]{1,0:T(8,128)(2,1)} %copy-done.3) | copy-start | bytes 221188
  12.5 5.3 %copy-start.6 = (bf16[144,256]{1,0:T(8,128)(2,1)S(1)}, bf16[144,256]{1,0:T(8,128)(2,1)}, u32[]{:S(2)}) copy-start(bf16[144,256]{1,0:T(8,128)(2,1)} %copy-done.5) | copy-start | bytes 221188
  12.5 15.4 %copy-start.11 = (bf16[128,1024]{1,0:T(8,128)(2,1)S(1)}, bf16[128,1024]{1,0:T(8,128)(2,1)}, u32[]{:S(2)}) copy-start(bf16[128,1024]{1,0:T(8,128)(2,1)} %get-tuple-element.49) | copy-start | bytes 786436
  12.6 30.3 %copy-start.1 = (bf16[128,1024]{1,0:T(8,128)(2,1)S(1)}, bf16[128,1024]{1,0:T(8,128)(2,1)}, u32[]{:S(2)}) copy-start(bf16[128,1024]{1,0:T(8,128)(2,1)} %get-tuple-element.40.refs_0_) | copy-start | bytes 786436
  12.6 17.4 %collective-permute-start.3 = (bf16[512,256]{1,0:T(8,128)(2,1)S(1)}, bf16[512,256]{1,0:T(8,128)(2,1)S(1)}, u32[]{:S(2)}, u32[]{:S(2)}) collective-permute-start(bf16[512,256]{1,0:T(8,128)(2,1)S(1)} %pad_maximum_fusion.refs_4_), channel_id=1, source_target_pairs={{0,1},{1,0},{2,3},{3,2},{4,5},{5,4},{6,7},{7,6},{8,9},{9,8},{10,11... | collective-permute-start | bytes 786440 | tf_op jit(solution)/shard_map/ppermute | solution.py:46
  14.6 15.4 %collective-permute-start.4 = (bf16[512,256]{1,0:T(8,128)(2,1)S(1)}, bf16[512,256]{1,0:T(8,128)(2,1)S(1)}, u32[]{:S(2)}, u32[]{:S(2)}) collective-permute-start(bf16[512,256]{1,0:T(8,128)(2,1)S(1)} %pad_maximum_fusion.refs_4_), channel_id=1, source_target_pairs={{0,2},{1,3},{2,0},{3,1},{4,6},{5,7},{6,4},{7,5},{8,10},{9,11},{10,... | collective-permute-start | bytes 786440 | tf_op jit(solution)/shard_map/ppermute | solution.py:46
  17.9 1.3 %collective-permute-start.5 = (bf16[8,256]{1,0:T(8,128)(2,1)S(1)}, bf16[8,256]{1,0:T(8,128)(2,1)S(1)}, u32[]{:S(2)}, u32[]{:S(2)}) collective-permute-start(bf16[8,256]{1,0:T(8,128)(2,1)S(1)} %pad_maximum_fusion.1), channel_id=1, source_target_pairs={{0,16},{1,17},{2,18},{3,19},{4,20},{5,21},{6,22},{7,23},{8,24},{9,... | collective-permute-start | bytes 12296 | tf_op jit(solution)/shard_map/ppermute | solution.py:46
  19.2 3.7 %collective-permute-start.6 = (bf16[16,256]{1,0:T(8,128)(2,1)S(1)}, bf16[16,256]{1,0:T(8,128)(2,1)S(1)}, u32[]{:S(2)}, u32[]{:S(2)}) collective-permute-start(bf16[16,256]{1,0:T(8,128)(2,1)S(1)} %concatenate.23), channel_id=1, source_target_pairs={{0,32},{1,33},{2,34},{3,35},{4,36},{5,37},{6,38},{7,39},{8,40},{9,... | collective-permute-start | bytes 24584 | tf_op jit(solution)/shard_map/ppermute | solution.py:46
  23.0 5.0 %collective-permute-start.7 = (bf16[32,256]{1,0:T(8,128)(2,1)S(1)}, bf16[32,256]{1,0:T(8,128)(2,1)S(1)}, u32[]{:S(2)}, u32[]{:S(2)}) collective-permute-start(bf16[32,256]{1,0:T(8,128)(2,1)S(1)} %concatenate.24), channel_id=1, source_target_pairs={{0,96},{1,97},{2,98},{3,99},{4,100},{5,101},{6,102},{7,103},{8,104... | collective-permute-start | bytes 49160 | tf_op jit(solution)/shard_map/ppermute | solution.py:46
  23.5 15.3 %collective-permute-start.13 = (bf16[128,1024]{1,0:T(8,128)(2,1)}, bf16[128,1024]{1,0:T(8,128)(2,1)S(1)}, u32[]{:S(2)}, u32[]{:S(2)}) collective-permute-start(bf16[128,1024]{1,0:T(8,128)(2,1)} %get-tuple-element.47), channel_id=1, source_target_pairs={{0,4},{1,5},{2,6},{3,7},{4,0},{5,1},{6,2},{7,3},{8,12},{9,13},{10,... | collective-permute-start | bytes 786440 | tf_op jit(solution)/shard_map/ppermute | solution.py:46
  24.2 15.2 %collective-permute-start.14 = (bf16[128,1024]{1,0:T(8,128)(2,1)S(1)}, bf16[128,1024]{1,0:T(8,128)(2,1)S(1)}, u32[]{:S(2)}, u32[]{:S(2)}) collective-permute-start(bf16[128,1024]{1,0:T(8,128)(2,1)S(1)} %copy-done.12), channel_id=1, source_target_pairs={{0,12},{1,13},{2,14},{3,15},{4,8},{5,9},{6,10},{7,11},{8,4},{9,5},... | collective-permute-start | bytes 786440 | tf_op jit(solution)/shard_map/ppermute | solution.py:46
  28.0 14.9 %collective-permute-start.15 = (bf16[128,1024]{1,0:T(8,128)(2,1)S(1)}, bf16[128,1024]{1,0:T(8,128)(2,1)S(1)}, u32[]{:S(2)}, u32[]{:S(2)}) collective-permute-start(bf16[128,1024]{1,0:T(8,128)(2,1)S(1)} %copy-done.11), channel_id=1, source_target_pairs={{0,8},{1,9},{2,10},{3,11},{4,12},{5,13},{6,14},{7,15},{8,0},{9,1},... | collective-permute-start | bytes 786440 | tf_op jit(solution)/shard_map/ppermute | solution.py:46
  30.0 8.4 %collective-permute-start.9 = (bf16[64,256]{1,0:T(8,128)(2,1)S(1)}, bf16[64,256]{1,0:T(8,128)(2,1)S(1)}, u32[]{:S(2)}, u32[]{:S(2)}) collective-permute-start(bf16[64,256]{1,0:T(8,128)(2,1)S(1)} %concatenate.25), channel_id=1, source_target_pairs={{0,128},{1,129},{2,130},{3,131},{4,132},{5,133},{6,134},{7,135},{8... | collective-permute-start | bytes 98312 | tf_op jit(solution)/shard_map/ppermute | solution.py:46
  34.6 8.3 %copy-start.2 = (s32[1,16]{1,0:T(1,128)S(1)}, s32[1,16]{1,0:T(1,128)}, u32[]{:S(2)}) copy-start(s32[1,16]{1,0:T(1,128)} %offsets.9) | copy-start | bytes 196
  34.6 18.1 %collective-permute-start.8 = (bf16[512,256]{1,0:T(8,128)(2,1)S(1)}, bf16[512,256]{1,0:T(8,128)(2,1)S(1)}, u32[]{:S(2)}, u32[]{:S(2)}) collective-permute-start(bf16[512,256]{1,0:T(8,128)(2,1)S(1)} %collective-permute-done.3.refs_5_), channel_id=1, source_target_pairs={{0,2},{1,3},{2,0},{3,1},{4,6},{5,7},{6,4},{7,5},{8,10},{9,11},{10,... | collective-permute-start | bytes 786440 | tf_op jit(solution)/shard_map/ppermute | solution.py:46
  38.5 14.3 %collective-permute-start.10 = (bf16[128,256]{1,0:T(8,128)(2,1)S(1)}, bf16[128,256]{1,0:T(8,128)(2,1)S(1)}, u32[]{:S(2)}, u32[]{:S(2)}) collective-permute-start(bf16[128,256]{1,0:T(8,128)(2,1)S(1)} %constant_dynamic-update-slice_fusion.refs_2_), channel_id=1, source_target_pairs={{0,1},{1,0},{2,3},{3,2},{4,5},{5,4},{6,7},{7,6},{8,9},{9,8},{10,11... | collective-permute-start | bytes 196616 | tf_op jit(solution)/shard_map/ppermute | solution.py:46
  38.8 14.0 %collective-permute-start.11 = (bf16[128,256]{1,0:T(8,128)(2,1)S(1)}, bf16[128,256]{1,0:T(8,128)(2,1)S(1)}, u32[]{:S(2)}, u32[]{:S(2)}) collective-permute-start(bf16[128,256]{1,0:T(8,128)(2,1)S(1)} %constant_dynamic-update-slice_fusion.refs_2_), channel_id=1, source_target_pairs={{0,2},{1,3},{2,0},{3,1},{4,6},{5,7},{6,4},{7,5},{8,10},{9,11},{10,... | collective-permute-start | bytes 196616 | tf_op jit(solution)/shard_map/ppermute | solution.py:46
  39.4 13.3 %collective-permute-start.12 = (bf16[128,256]{1,0:T(8,128)(2,1)S(1)}, bf16[128,256]{1,0:T(8,128)(2,1)S(1)}, u32[]{:S(2)}, u32[]{:S(2)}) collective-permute-start(bf16[128,256]{1,0:T(8,128)(2,1)S(1)} %constant_dynamic-update-slice_fusion.refs_2_), channel_id=1, source_target_pairs={{0,3},{1,2},{2,1},{3,0},{4,7},{5,6},{6,5},{7,4},{8,11},{9,10},{10,... | collective-permute-start | bytes 196616 | tf_op jit(solution)/shard_map/ppermute | solution.py:46
  55.2 12.4 %collective-permute-start.18 = (bf16[128,1024]{1,0:T(8,128)(2,1)S(1)}, bf16[128,1024]{1,0:T(8,128)(2,1)S(1)}, u32[]{:S(2)}, u32[]{:S(2)}) collective-permute-start(bf16[128,1024]{1,0:T(8,128)(2,1)S(1)} %attend_last.7), channel_id=1, source_target_pairs={{0,8},{1,9},{2,10},{3,11},{4,12},{5,13},{6,14},{7,15},{8,0},{9,1},... | collective-permute-start | bytes 786440 | tf_op jit(solution)/shard_map/ppermute | solution.py:46
  60.0 10.2 %collective-permute-start.17 = (bf16[128,1024]{1,0:T(8,128)(2,1)S(1)}, bf16[128,1024]{1,0:T(8,128)(2,1)S(1)}, u32[]{:S(2)}, u32[]{:S(2)}) collective-permute-start(bf16[128,1024]{1,0:T(8,128)(2,1)S(1)} %attend_last.6), channel_id=1, source_target_pairs={{0,12},{1,13},{2,14},{3,15},{4,8},{5,9},{6,10},{7,11},{8,4},{9,5},... | collective-permute-start | bytes 786440 | tf_op jit(solution)/shard_map/ppermute | solution.py:46
  64.4 6.5 %collective-permute-start.16 = (bf16[128,1024]{1,0:T(8,128)(2,1)S(1)}, bf16[128,1024]{1,0:T(8,128)(2,1)S(1)}, u32[]{:S(2)}, u32[]{:S(2)}) collective-permute-start(bf16[128,1024]{1,0:T(8,128)(2,1)S(1)} %attend_last.5), channel_id=1, source_target_pairs={{0,4},{1,5},{2,6},{3,7},{4,0},{5,1},{6,2},{7,3},{8,12},{9,13},{10,... | collective-permute-start | bytes 786440 | tf_op jit(solution)/shard_map/ppermute | solution.py:46
  67.6 3.2 %copy-start.7 = (bf16[128,1024]{1,0:T(8,128)(2,1)}, bf16[128,1024]{1,0:T(8,128)(2,1)S(1)}, u32[]{:S(2)}) copy-start(bf16[128,1024]{1,0:T(8,128)(2,1)S(1)} %collective-permute-done.18.refs_3_) | copy-start | bytes 786436
  70.2 0.7 copy-start.8
  (2 other events, 1.4 us)

commit v3 on v2

--- a/solution.py
+++ b/solution.py
@@ -17,10 +17,10 @@
 PAIRS = GROUP // PAIR
 SCALE = math.log2(math.e) / math.sqrt(HD)
 NEG = -1e30
-GROUPS = ([3], [1], [2], [0])
 AXES = ("member", "ctx")
 VMEM = pl.BlockSpec(memory_space=pltpu.VMEM)
 SMEM = pl.BlockSpec(memory_space=pltpu.SMEM)
+HBM = pl.BlockSpec(memory_space=pltpu.HBM)
 
 
 def moves(step):
@@ -80,52 +80,124 @@
     return jnp.where(row == 0, wide[:1], jnp.where(row == 1, wide[1:], 0.0)).astype(jnp.bfloat16)
 
 
-def split_kv_kernel(k_ref, v_ref, pk_ref, pv_ref, *outs):
+def run(copies):
+    for copy in copies:
+        copy.start()
+    for copy in copies:
+        copy.wait()
+
+
+def split_kv_kernel(k_ref, v_ref, pk_ref, pv_ref, *refs):
+    outs, rows, sems = refs[:4], refs[4], refs[5]
+    copies = [
+        pltpu.make_async_copy(pk_ref, rows.at[0], sems.at[8]),
+        pltpu.make_async_copy(pv_ref, rows.at[1], sems.at[9]),
+    ]
     for bits in range(4):
         part = columns(head_of(bits), HD)
-        outs[bits][:TOK, :HD] = k_ref[:, part]
-        outs[bits][:TOK, HD:] = v_ref[:, part]
-        outs[bits][TOK:, :HD] = two_rows(pk_ref[:, part])
-        outs[bits][TOK:, HD:] = two_rows(pv_ref[:, part])
+        copies.append(pltpu.make_async_copy(k_ref.at[:, part], outs[bits].at[:TOK, :HD], sems.at[bits]))
+        copies.append(pltpu.make_async_copy(v_ref.at[:, part], outs[bits].at[:TOK, HD:], sems.at[4 + bits]))
+    run(copies)
+    for bits in range(4):
+        part = columns(head_of(bits), HD)
+        outs[bits][TOK:, :HD] = two_rows(rows[0, :, part])
+        outs[bits][TOK:, HD:] = two_rows(rows[1, :, part])
 
 
 def split_kv(keys, values, prompt_keys, prompt_values):
     return pl.pallas_call(
         split_kv_kernel,
-        in_specs=[VMEM] * 4,
+        in_specs=[HBM] * 4,
         out_specs=[VMEM] * 4,
         out_shape=[jax.ShapeDtypeStruct((TOK + RIDE, 2 * HD), jnp.bfloat16)] * 4,
+        scratch_shapes=[pltpu.VMEM((2, 2, KV_HEADS * HD), jnp.bfloat16), pltpu.SemaphoreType.DMA((10,))],
         name="split_kv",
     )(keys, values, prompt_keys, prompt_values)
 
 
-def split_q_kernel(q_ref, *outs):
-    for bits in range(4):
-        outs[bits][...] = q_ref[:, columns(head_of(bits), WIDE)]
+def split_q_kernel(q_ref, *refs):
+    outs, sems = refs[:4], refs[4]
+    run(
+        [
+            pltpu.make_async_copy(q_ref.at[:, columns(head_of(bits), WIDE)], outs[bits], sems.at[bits])
+            for bits in range(4)
+        ]
+    )
 
 
 def split_q(q):
     return pl.pallas_call(
         split_q_kernel,
-        in_specs=[VMEM],
+        in_specs=[HBM],
         out_specs=[VMEM] * 4,
         out_shape=[jax.ShapeDtypeStruct((TOK, WIDE), jnp.bfloat16)] * 4,
+        scratch_shapes=[pltpu.SemaphoreType.DMA((4,))],
         name="split_q",
     )(q)
 
 
+def place_kernel(offsets, length, info_ref):
+    core, y, z = place()
+    row = lax.broadcasted_iota(jnp.int32, info_ref.shape, 0)
+    info = jnp.where(row == 16, length[0], 0)
+    for zbits in range(4):
+        for ybits in range(4):
+            source = (y ^ delta(ybits, core, 1, 3)) * 4 + (z ^ delta(zbits, core, 1, 2))
+            info = jnp.where(row == zbits * 4 + ybits, offsets[0, source] * TOK, info)
+    info_ref[...] = info
+
+
+def places(offsets, length):
+    return pl.pallas_call(
+        place_kernel,
+        in_specs=[SMEM, SMEM],
+        out_specs=VMEM,
+        out_shape=jax.ShapeDtypeStruct((24, HD), jnp.int32),
+        compiler_params=pltpu.CompilerParams(vmem_limit_bytes=4 << 20),
+        name="places",
+    )(offsets, length)
+
+
+def stack_kernel(*refs):
+    parts, column_ref, sems = refs[:4], refs[4], refs[5]
+    run(
+        [
+            pltpu.make_async_copy(parts[i].at[:TOK], column_ref.at[i * TOK : (i + 1) * TOK], sems.at[i])
+            for i in range(4)
+        ]
+    )
+
+
+def stack(parts):
+    return pl.pallas_call(
+        stack_kernel,
+        in_specs=[pl.BlockSpec(memory_space=pl.ANY)] * 4,
+        out_specs=VMEM,
+        out_shape=jax.ShapeDtypeStruct((4 * TOK, 2 * HD), jnp.bfloat16),
+        scratch_shapes=[pltpu.SemaphoreType.DMA((4,))],
+        compiler_params=pltpu.CompilerParams(vmem_limit_bytes=4 << 20),
+        name="stack",
+    )(*parts)
+
+
 def merge_kernel(*refs):
-    out_ref = refs[4]
-    for bits in range(4):
-        out_ref[:, columns(head_of(bits), WIDE)] = refs[bits][...]
+    parts, out_ref, sems = refs[:4], refs[4], refs[5]
+    run(
+        [
+            pltpu.make_async_copy(parts[bits], out_ref.at[:, columns(head_of(bits), WIDE)], sems.at[bits])
+            for bits in range(4)
+        ]
+    )
 
 
 def merge(parts):
     return pl.pallas_call(
         merge_kernel,
         in_specs=[VMEM] * 4,
-        out_specs=VMEM,
+        out_specs=pl.BlockSpec(memory_space=pl.ANY),
         out_shape=jax.ShapeDtypeStruct((TOK, KV_HEADS * WIDE), jnp.bfloat16),
+        scratch_shapes=[pltpu.SemaphoreType.DMA((4,))],
+        compiler_params=pltpu.CompilerParams(vmem_limit_bytes=8 << 20),
         name="merge",
     )(*parts)
 
@@ -134,7 +206,7 @@
     keys = TOK * len(blocks)
     count = len(queries)
 
-    def kernel(offsets, length, *refs):
+    def kernel(info_ref, *refs):
         q_refs, refs = refs[:count], refs[count:]
         pieces, refs = refs[: len(sizes)], refs[len(sizes) :]
         if carried:
@@ -146,20 +218,22 @@
             refs = refs[2 * count + 1 :]
             mark_ref[...] = jnp.zeros(mark_ref.shape, jnp.float32)
         k_aug, v_aug = refs
-        core, y, z = place()
         token = lax.broadcasted_iota(jnp.int32, (TOK, TOK), 1)
         k_row = lax.broadcasted_iota(jnp.int32, (TOK, TOK), 0)
+
+        def first_position(ybits, zbits):
+            return info_ref[zbits * 4 + ybits : zbits * 4 + ybits + 1, :]
+
         for index, bits in enumerate(blocks):
             to = slice(index * TOK, (index + 1) * TOK)
             if bits is not None:
-                source = (y ^ delta(bits[0], core, 1, 3)) * 4 + (z ^ delta(bits[1], core, 1, 2))
-                k_pos = k_row + offsets[0, source] * TOK
+                k_pos = k_row + first_position(bits[0], bits[1])
             for i in range(count):
                 if bits is None:
                     bias = jnp.zeros((TOK, TOK), jnp.bfloat16)
                 else:
-                    q_pos = token + offsets[0, (y ^ delta(queries[i], core, 1, 3)) * 4 + z] * TOK
-                    counted = (k_pos <= q_pos) & (k_pos < length[0])
+                    q_pos = token + first_position(queries[i], 0)
+                    counted = (k_pos <= q_pos) & (k_pos < info_ref[16:17, :])
                     bias = jnp.where(counted, 0.0, NEG).astype(jnp.bfloat16)
                 k_aug[i, to, HD:] = bias
         v_aug[:, HD:] = jnp.ones((keys, HD), jnp.bfloat16)
@@ -218,7 +292,7 @@
     return kernel
 
 
-def attend(offsets, length, queries, q, pieces, blocks, carry=(), last=False):
+def attend(info, queries, q, pieces, blocks, carry=(), last=False):
     sizes = [p.shape[0] for p in pieces]
     keys, count = TOK * len(blocks), len(queries)
     state = jax.ShapeDtypeStruct((PAIRS, PAIR * TOK, HD), jnp.float32)
@@ -227,7 +301,7 @@
     outs = [result] * count if last else [state] * (2 * count) + [mark]
     return pl.pallas_call(
         make_kernel(queries, sizes, blocks, bool(carry), last),
-        in_specs=[SMEM, SMEM] + [VMEM] * (count + len(pieces) + len(carry)),
+        in_specs=[VMEM] * (1 + count + len(pieces) + len(carry)),
         out_specs=[VMEM] * len(outs),
         out_shape=outs,
         scratch_shapes=[
@@ -239,7 +313,7 @@
             flops=4 * WIDE * count * keys * HD, bytes_accessed=count << 20, transcendentals=WIDE * count * keys
         ),
         name="attend_last" if last else "attend_first",
-    )(offsets, length, *q, *pieces, *carry)
+    )(info, *q, *pieces, *carry)
 
 
 def column_blocks(zbits):
@@ -250,30 +324,45 @@
     queries, response_keys, response_values, prompt_keys, prompt_values, block_offsets, lengths
 ):
     mine = split_kv(response_keys[0], response_values[0], prompt_keys, prompt_values)
+    queries, mine = lax.optimization_barrier((queries, mine))
     q_mine = split_q(queries[0])
     kv = [mine[0]] + [send(mine[bits], Y_STEPS[bits - 1]) for bits in (1, 2, 3)]
-    kv, q_mine = lax.optimization_barrier((kv, q_mine))
-    column = join(*(part[:TOK] for part in kv))
+    column = stack(kv)
     prompt = join(*(part[TOK : TOK + 2] for part in kv))
     z_first = send(column, Z_STEPS[0])
     z_second = send(column, Z_STEPS[1])
-    for pairs in (CORE_STEP, X_STEPS[0], X_STEPS[1]):
-        prompt = double(prompt, pairs)
+    column, q_mine = lax.optimization_barrier((column, q_mine))
     q = [q_mine[0]] + [send(q_mine[bits], Y_STEPS[bits - 1]) for bits in (1, 2, 3)]
+    prompt = double(prompt, CORE_STEP)
+    prompt = double(prompt, X_STEPS[0])
+    block_offsets, prompt = lax.optimization_barrier((block_offsets, prompt))
+    info = places(block_offsets, lengths)
+    q[1], prompt = lax.optimization_barrier((q[1], prompt))
+    prompt = double(prompt, X_STEPS[1])
     z_first, z_second, prompt = lax.optimization_barrier((z_first, z_second, prompt))
     z_both = send(z_first, Z_STEPS[1])
     prompt = double(prompt, ZH_STEP)
+    near = [column, z_first, z_second]
+
+    def begin(group):
+        out = attend(info, group, [q[i] for i in group], near, column_blocks((0, 1, 2)))
+        return {i: [out[n], out[len(group) + n]] for n, i in enumerate(group)}, out[-1]
+
+    state, mark = begin([3, 1])
+    mark, prompt = lax.optimization_barrier((mark, prompt))
     prompts = [send(prompt, pairs) for pairs in Z_STEPS]
-    out = attend(block_offsets, lengths, [0, 1, 2, 3], q, [column, z_first, z_second], column_blocks((0, 1, 2)))
-    state = {i: (out[i], out[4 + i]) for i in range(4)}
+    state |= begin([2])[0]
     pieces = [z_both, prompt] + prompts
-    blocks = column_blocks((3,)) + [None] * 4
+    late = column_blocks((3,)) + [None] * 4
     results = [None] * 4
-    for group in GROUPS:
-        carry = [state[i][0] for i in group] + [state[i][1] for i in group]
-        out = attend(block_offsets, lengths, group, [q[i] for i in group], pieces, blocks, carry, True)
-        for i, value in zip(group, out):
-            results[i] = send(value, Y_STEPS[i - 1]) if i else value
+    for i in (3, 1, 2, 0):
+        if i in state:
+            out = attend(info, [i], [q[i]], pieces, late, state[i], True)[0]
+        else:
+            out = attend(
+                info, [i], [q[i]], near + pieces, column_blocks((0, 1, 2)) + late, (), True
+            )[0]
+        results[i] = send(out, Y_STEPS[i - 1]) if i else out
     return merge(results)[None]
 
 

time: 74 us -> 70.1 us (0.947)
  Pallas kernels: 25.9 us -> 23.2 us
  starting transfers between devices: 29.3 us -> 31.9 us
  local copies, waits for them, and re-layouts: 2.49 us -> 0.09 us
  waiting for transfers between devices: 15.2 us -> 13.8 us
    ppermute x19, starting transfers between devices: 29.3 us -> 31.9 us  [send(): return lax.ppermute(value, AXES, pairs)]
    pallas_call x5 -> x6, Pallas kernels: 19.6 us -> 17.3 us  [attend(): pl.pallas_call(make_kernel(queries, sizes, blocks, bool(carry), last), in...]
    unnamed x27 -> x10, local copies, waits for them, and re-layouts: 1.48 us -> 0.02 us
    ppermute x19, waiting for transfers between devices: 15.2 us -> 13.8 us  [send(): return lax.ppermute(value, AXES, pairs)]
    slice x6 -> x0, local copies, waits for them, and re-layouts: 0.91 us -> none  [body(): column = join(*(part[:TOK] for part in kv))]
    pallas_call x3 -> x5, Pallas kernels: 6.27 us -> 5.86 us  [the longest x1 2.21 us: split_q(): pl.pallas_call(split_q_kernel, in_specs=[HBM], out_specs=[VMEM] * 4, out_...]
  transfers between devices with their start and end apart: 19 -> 19, of which waited for: 8 -> 7; matrix products, arithmetic and copies ran while one was open for 0% -> 0% of each run, Pallas kernels for 26% -> 26%
where the time goes in v3:
time: 70.1 us; the launch traced here: 69.9 us
  starting transfers between devices  31.9 us (46%)
  Pallas kernels  23.2 us (33%)
  waiting for transfers between devices  13.8 us (20%)
  between operations  1.02 us (1%)
    ppermute x19, starting transfers between devices, send(): return lax.ppermute(value, AXES, pairs)  31.9 us
    pallas_call x6, Pallas kernels, attend(): pl.pallas_call(make_kernel(queries, sizes, blocks, bool(carry), last), in...  17.3 us
    ppermute x19, waiting for transfers between devices, send(): return lax.ppermute(value, AXES, pairs)  13.8 us
    pallas_call x1, Pallas kernels, split_q(): pl.pallas_call(split_q_kernel, in_specs=[HBM], out_specs=[VMEM] * 4, out_...  2.21 us
    pallas_call x1, Pallas kernels, split_kv(): pl.pallas_call(split_kv_kernel, in_specs=[HBM] * 4, out_specs=[VMEM] * 4,...  1.71 us
  transfers between devices with their start and end apart: 19, of which 7 were waited for; matrix products, arithmetic and copies ran while one was open for 0% of the time, Pallas kernels for 26%

profile of v3, /device:TPU:6, one launch (start us, length us, event | category | flops | bytes accessed | tf_op | source)
XLA Modules:
  0.0 69.9 jit_solution(1947299647088299841)
XLA Ops:
  0.0 1.7 %split_kv.1 = (bf16[144,256]{1,0:T(8,128)(2,1)}, bf16[144,256]{1,0:T(8,128)(2,1)}, bf16[144,256]{1,0:T(8,128)(2,1)}, bf16[144,256]{1,0:T(8,128)(2,1)}) custom-call(bf16[128,512]{1,0:T(8,128)(2,1)} %bitcast.5, bf16[128,512]{1,0:T(8,128)(2,1)} %bitcast.6, bf16[2,512]{1,0:T(2,128)(2,1)} %pk_ref.1, bf16[2,512]{1,0:T(2,128)(2,1)} %pv_ref.1), custom_call_target="tpu_custom_call" | custom-call | tf_op jit(solution)/shard_map/split_kv/pallas_call | solution.py:108
  1.7 1.7 %collective-permute-start = (bf16[144,256]{1,0:T(8,128)(2,1)}, bf16[144,256]{1,0:T(8,128)(2,1)S(1)}, u32[]{:S(2)}, u32[]{:S(2)}) collective-permute-start(bf16[144,256]{1,0:T(8,128)(2,1)} %get-tuple-element.41), channel_id=1, source_target_pairs={{0,4},{1,5},{2,6},{3,7},{4,0},{5,1},{6,2},{7,3},{8,12},{9,13},{10,... | collective-permute-start | bytes 221192 | tf_op jit(solution)/shard_map/ppermute | solution.py:46
  3.4 2.2 %collective-permute-start.1 = (bf16[144,256]{1,0:T(8,128)(2,1)}, bf16[144,256]{1,0:T(8,128)(2,1)S(1)}, u32[]{:S(2)}, u32[]{:S(2)}) collective-permute-start(bf16[144,256]{1,0:T(8,128)(2,1)} %get-tuple-element.42), channel_id=1, source_target_pairs={{0,12},{1,13},{2,14},{3,15},{4,8},{5,9},{6,10},{7,11},{8,4},{9,5},... | collective-permute-start | bytes 221192 | tf_op jit(solution)/shard_map/ppermute | solution.py:46
  5.6 0.7 %collective-permute-start.2 = (bf16[144,256]{1,0:T(8,128)(2,1)}, bf16[144,256]{1,0:T(8,128)(2,1)S(1)}, u32[]{:S(2)}, u32[]{:S(2)}) collective-permute-start(bf16[144,256]{1,0:T(8,128)(2,1)} %get-tuple-element.43), channel_id=1, source_target_pairs={{0,8},{1,9},{2,10},{3,11},{4,12},{5,13},{6,14},{7,15},{8,0},{9,1},... | collective-permute-start | bytes 221192 | tf_op jit(solution)/shard_map/ppermute | solution.py:46
  6.3 2.2 %split_q.1 = (bf16[128,1024]{1,0:T(8,128)(2,1)}, bf16[128,1024]{1,0:T(8,128)(2,1)}, bf16[128,1024]{1,0:T(8,128)(2,1)}, bf16[128,1024]{1,0:T(8,128)(2,1)}) custom-call(bf16[128,4096]{1,0:T(8,128)(2,1)} %bitcast.4), custom_call_target="tpu_custom_call" | custom-call | tf_op jit(solution)/shard_map/split_q/pallas_call | solution.py:129
  8.5 1.4 %collective-permute-done.1.refs_2_ = bf16[144,256]{1,0:T(8,128)(2,1)S(1)} collective-permute-done((bf16[144,256]{1,0:T(8,128)(2,1)}, bf16[144,256]{1,0:T(8,128)(2,1)S(1)}, u32[]{:S(2)}, u32[]{:S(2)}) %collective-permute-start.1) | collective-permute-done | bytes 73760 | tf_op jit(solution)/shard_map/ppermute | solution.py:46
  9.9 1.7 %collective-permute-done.2.refs_3_ = bf16[144,256]{1,0:T(8,128)(2,1)S(1)} collective-permute-done((bf16[144,256]{1,0:T(8,128)(2,1)}, bf16[144,256]{1,0:T(8,128)(2,1)S(1)}, u32[]{:S(2)}, u32[]{:S(2)}) %collective-permute-start.2) | collective-permute-done | bytes 73760 | tf_op jit(solution)/shard_map/ppermute | solution.py:46
  12.0 0.8 %collective-permute-start.7 = (bf16[128,1024]{1,0:T(8,128)(2,1)}, bf16[128,1024]{1,0:T(8,128)(2,1)S(1)}, u32[]{:S(2)}, u32[]{:S(2)}) collective-permute-start(bf16[128,1024]{1,0:T(8,128)(2,1)} %get-tuple-element.52), channel_id=1, source_target_pairs={{0,4},{1,5},{2,6},{3,7},{4,0},{5,1},{6,2},{7,3},{8,12},{9,13},{10,... | collective-permute-start | bytes 786440 | tf_op jit(solution)/shard_map/ppermute | solution.py:46
  12.8 3.3 %collective-permute-start.6 = (bf16[512,256]{1,0:T(8,128)(2,1)S(1)}, bf16[512,256]{1,0:T(8,128)(2,1)S(1)}, u32[]{:S(2)}, u32[]{:S(2)}) collective-permute-start(bf16[512,256]{1,0:T(8,128)(2,1)S(1)} %stack.1.refs_1_.refs_2_), channel_id=1, source_target_pairs={{0,2},{1,3},{2,0},{3,1},{4,6},{5,7},{6,4},{7,5},{8,10},{9,11},{10,... | collective-permute-start | bytes 786440 | tf_op jit(solution)/shard_map/ppermute | solution.py:46
  16.0 1.9 %collective-permute-start.5 = (bf16[512,256]{1,0:T(8,128)(2,1)S(1)}, bf16[512,256]{1,0:T(8,128)(2,1)S(1)}, u32[]{:S(2)}, u32[]{:S(2)}) collective-permute-start(bf16[512,256]{1,0:T(8,128)(2,1)S(1)} %stack.1.refs_1_.refs_2_), channel_id=1, source_target_pairs={{0,1},{1,0},{2,3},{3,2},{4,5},{5,4},{6,7},{7,6},{8,9},{9,8},{10,11... | collective-permute-start | bytes 786440 | tf_op jit(solution)/shard_map/ppermute | solution.py:46
  18.0 2.1 %collective-permute-start.14 = (bf16[128,1024]{1,0:T(8,128)(2,1)S(1)}, bf16[128,1024]{1,0:T(8,128)(2,1)S(1)}, u32[]{:S(2)}, u32[]{:S(2)}) collective-permute-start(bf16[128,1024]{1,0:T(8,128)(2,1)S(1)} %copy-done.4), channel_id=1, source_target_pairs={{0,8},{1,9},{2,10},{3,11},{4,12},{5,13},{6,14},{7,15},{8,0},{9,1},... | collective-permute-start | bytes 786440 | tf_op jit(solution)/shard_map/ppermute | solution.py:46
  20.2 1.2 %collective-permute-done.3 = bf16[8,256]{1,0:T(8,128)(2,1)S(1)} collective-permute-done((bf16[8,256]{1,0:T(8,128)(2,1)S(1)}, bf16[8,256]{1,0:T(8,128)(2,1)S(1)}, u32[]{:S(2)}, u32[]{:S(2)}) %collective-permute-start.3) | collective-permute-done | bytes 4128 | tf_op jit(solution)/shard_map/ppermute | solution.py:46
  21.4 0.9 %collective-permute-start.4 = (bf16[16,256]{1,0:T(8,128)(2,1)S(1)}, bf16[16,256]{1,0:T(8,128)(2,1)S(1)}, u32[]{:S(2)}, u32[]{:S(2)}) collective-permute-start(bf16[16,256]{1,0:T(8,128)(2,1)S(1)} %concatenate.18), channel_id=1, source_target_pairs={{0,32},{1,33},{2,34},{3,35},{4,36},{5,37},{6,38},{7,39},{8,40},{9,... | collective-permute-start | bytes 24584 | tf_op jit(solution)/shard_map/ppermute | solution.py:46
  22.3 2.8 %collective-permute-done.4 = bf16[16,256]{1,0:T(8,128)(2,1)S(1)} collective-permute-done((bf16[16,256]{1,0:T(8,128)(2,1)S(1)}, bf16[16,256]{1,0:T(8,128)(2,1)S(1)}, u32[]{:S(2)}, u32[]{:S(2)}) %collective-permute-start.4) | collective-permute-done | bytes 8224 | tf_op jit(solution)/shard_map/ppermute | solution.py:46
  26.4 2.0 %collective-permute-start.16 = (bf16[128,1024]{1,0:T(8,128)(2,1)S(1)}, bf16[128,1024]{1,0:T(8,128)(2,1)S(1)}, u32[]{:S(2)}, u32[]{:S(2)}) collective-permute-start(bf16[128,1024]{1,0:T(8,128)(2,1)S(1)} %copy-done.3), channel_id=1, source_target_pairs={{0,12},{1,13},{2,14},{3,15},{4,8},{5,9},{6,10},{7,11},{8,4},{9,5},... | collective-permute-start | bytes 786440 | tf_op jit(solution)/shard_map/ppermute | solution.py:46
  28.4 0.6 places.1.info_ref
  29.0 1.2 %collective-permute-done.8 = bf16[32,256]{1,0:T(8,128)(2,1)S(1)} collective-permute-done((bf16[32,256]{1,0:T(8,128)(2,1)S(1)}, bf16[32,256]{1,0:T(8,128)(2,1)S(1)}, u32[]{:S(2)}, u32[]{:S(2)}) %collective-permute-start.8) | collective-permute-done | bytes 16416 | tf_op jit(solution)/shard_map/ppermute | solution.py:46
  30.2 4.6 %collective-permute-start.10 = (bf16[64,256]{1,0:T(8,128)(2,1)S(1)}, bf16[64,256]{1,0:T(8,128)(2,1)S(1)}, u32[]{:S(2)}, u32[]{:S(2)}) collective-permute-start(bf16[64,256]{1,0:T(8,128)(2,1)S(1)} %pad_maximum_fusion.1), channel_id=1, source_target_pairs={{0,128},{1,129},{2,130},{3,131},{4,132},{5,133},{6,134},{7,135},{8... | collective-permute-start | bytes 98312 | tf_op jit(solution)/shard_map/ppermute | solution.py:46
  34.8 1.5 %collective-permute-start.9 = (bf16[512,256]{1,0:T(8,128)(2,1)S(1)}, bf16[512,256]{1,0:T(8,128)(2,1)S(1)}, u32[]{:S(2)}, u32[]{:S(2)}) collective-permute-start(bf16[512,256]{1,0:T(8,128)(2,1)S(1)} %collective-permute-done.5.refs_2_.refs_3_), channel_id=1, source_target_pairs={{0,2},{1,3},{2,0},{3,1},{4,6},{5,7},{6,4},{7,5},{8,10},{9,11},{10,... | collective-permute-start | bytes 786440 | tf_op jit(solution)/shard_map/ppermute | solution.py:46
  36.2 5.1 %attend_first.2 = (f32[4,256,128]{2,1,0:T(8,128)S(1)}, f32[4,256,128]{2,1,0:T(8,128)S(1)}, f32[4,256,128]{2,1,0:T(8,128)S(1)}, f32[4,256,128]{2,1,0:T(8,128)S(1)}, f32[8,128]{1,0:T(8,128)}) custom-call(s32[24,128]{1,0:T(8,128)S(1)} %places.1.info_ref, bf16[128,1024]{1,0:T(8,128)(2,1)S(1)} %collective-permute-done.14.refs_0_, ...), custom_call_target="tpu_custom_call" | custom-call | flops 1610612736 | bytes 2097152 | tf_op jit(solution)/shard_map/attend_first/pallas_call | solution.py:302
  41.3 2.0 %collective-permute-start.13 = (bf16[128,256]{1,0:T(8,128)(2,1)S(1)}, bf16[128,256]{1,0:T(8,128)(2,1)S(1)}, u32[]{:S(2)}, u32[]{:S(2)}) collective-permute-start(bf16[128,256]{1,0:T(8,128)(2,1)S(1)} %pad_maximum_fusion.refs_5_.refs_2_), channel_id=1, source_target_pairs={{0,3},{1,2},{2,1},{3,0},{4,7},{5,6},{6,5},{7,4},{8,11},{9,10},{10,... | collective-permute-start | bytes 196616 | tf_op jit(solution)/shard_map/ppermute | solution.py:46
  43.9 1.9 %collective-permute-start.11 = (bf16[128,256]{1,0:T(8,128)(2,1)S(1)}, bf16[128,256]{1,0:T(8,128)(2,1)S(1)}, u32[]{:S(2)}, u32[]{:S(2)}) collective-permute-start(bf16[128,256]{1,0:T(8,128)(2,1)S(1)} %pad_maximum_fusion.refs_5_.refs_2_), channel_id=1, source_target_pairs={{0,1},{1,0},{2,3},{3,2},{4,5},{5,4},{6,7},{7,6},{8,9},{9,8},{10,11... | collective-permute-start | bytes 196616 | tf_op jit(solution)/shard_map/ppermute | solution.py:46
  45.8 2.9 %attend_first.3 = (f32[4,256,128]{2,1,0:T(8,128)S(1)}, f32[4,256,128]{2,1,0:T(8,128)S(1)}, f32[8,128]{1,0:T(8,128)}) custom-call(s32[24,128]{1,0:T(8,128)S(1)} %places.1.info_ref, bf16[128,1024]{1,0:T(8,128)(2,1)S(1)} %collective-permute-done.16.refs_0_, bf16[512,256]{1,0:T(8,128)(2,1)S(1)} %stack.1.refs_1_.refs_2_, ...), custom_call_target="tpu_custom_call" | custom-call | flops 805306368 | bytes 1048576 | tf_op jit(solution)/shard_map/attend_first/pallas_call | solution.py:302
  48.8 1.7 %collective-permute-done.12.refs_7_.refs_4_ = bf16[128,256]{1,0:T(8,128)(2,1)S(1)} collective-permute-done((bf16[128,256]{1,0:T(8,128)(2,1)S(1)}, bf16[128,256]{1,0:T(8,128)(2,1)S(1)}, u32[]{:S(2)}, u32[]{:S(2)}) %collective-permute-start.12) | collective-permute-done | bytes 65568 | tf_op jit(solution)/shard_map/ppermute | solution.py:46
  50.5 1.8 %attend_last.6 = bf16[128,1024]{1,0:T(8,128)(2,1)S(1)} custom-call(s32[24,128]{1,0:T(8,128)S(1)} %places.1.info_ref, bf16[128,1024]{1,0:T(8,128)(2,1)S(1)} %collective-permute-done.16.refs_0_, bf16[512,256]{1,0:T(8,128)(2,1)S(1)} %collective-permute-done.9.refs_4_.refs_1_, bf16[128,256]{1,0:T(8,128)(2,1)S(1)} %pad_maximum_fusion.refs_5_.refs_2_, ...), custom_call_target="tpu_custom_call" | custom-call | flops 536870912 | bytes 1048576 | tf_op jit(solution)/shard_map/attend_last/pallas_call | solution.py:302
  52.3 2.2 %collective-permute-start.17 = (bf16[128,1024]{1,0:T(8,128)(2,1)S(1)}, bf16[128,1024]{1,0:T(8,128)(2,1)S(1)}, u32[]{:S(2)}, u32[]{:S(2)}) collective-permute-start(bf16[128,1024]{1,0:T(8,128)(2,1)S(1)} %attend_last.6), channel_id=1, source_target_pairs={{0,12},{1,13},{2,14},{3,15},{4,8},{5,9},{6,10},{7,11},{8,4},{9,5},... | collective-permute-start | bytes 786440 | tf_op jit(solution)/shard_map/ppermute | solution.py:46
  54.6 1.8 %attend_last.5 = bf16[128,1024]{1,0:T(8,128)(2,1)S(1)} custom-call(s32[24,128]{1,0:T(8,128)S(1)} %places.1.info_ref, bf16[128,1024]{1,0:T(8,128)(2,1)S(1)} %collective-permute-done.7.refs_1_.refs_0_, bf16[512,256]{1,0:T(8,128)(2,1)S(1)} %collective-permute-done.9.refs_4_.refs_1_, bf16[128,256]{1,0:T(8,128)(2,1)S(1)} %pad_maximum_fusion.refs_5_.refs_2_, ...), custom_call_target="tpu_custom_call" | custom-call | flops 536870912 | bytes 1048576 | tf_op jit(solution)/shard_map/attend_last/pallas_call | solution.py:302
  56.5 1.8 %attend_last.7 = bf16[128,1024]{1,0:T(8,128)(2,1)S(1)} custom-call(s32[24,128]{1,0:T(8,128)S(1)} %places.1.info_ref, bf16[128,1024]{1,0:T(8,128)(2,1)S(1)} %collective-permute-done.14.refs_0_, bf16[512,256]{1,0:T(8,128)(2,1)S(1)} %collective-permute-done.9.refs_4_.refs_1_, bf16[128,256]{1,0:T(8,128)(2,1)S(1)} %pad_maximum_fusion.refs_5_.refs_2_, ...), custom_call_target="tpu_custom_call" | custom-call | flops 536870912 | bytes 1048576 | tf_op jit(solution)/shard_map/attend_last/pallas_call | solution.py:302
  58.3 2.8 %collective-permute-start.18 = (bf16[128,1024]{1,0:T(8,128)(2,1)S(1)}, bf16[128,1024]{1,0:T(8,128)(2,1)S(1)}, u32[]{:S(2)}, u32[]{:S(2)}) collective-permute-start(bf16[128,1024]{1,0:T(8,128)(2,1)S(1)} %attend_last.7), channel_id=1, source_target_pairs={{0,8},{1,9},{2,10},{3,11},{4,12},{5,13},{6,14},{7,15},{8,0},{9,1},... | collective-permute-start | bytes 786440 | tf_op jit(solution)/shard_map/ppermute | solution.py:46
  61.2 3.8 %attend_last.4.refs_0_ = bf16[128,1024]{1,0:T(8,128)(2,1)S(1)} custom-call(s32[24,128]{1,0:T(8,128)S(1)} %places.1.info_ref, bf16[128,1024]{1,0:T(8,128)(2,1)S(1)} %copy-done.2, bf16[512,256]{1,0:T(8,128)(2,1)S(1)} %stack.1.refs_1_.refs_2_, bf16[512,256]{1,0:T(8,128)(2,1)S(1)} %collective-permute-done.5.refs_2_.refs_3_, ...), custom_call_target="tpu_custom_call" | custom-call | flops 1342177280 | bytes 1048576 | tf_op jit(solution)/shard_map/attend_last/pallas_call | solution.py:302
  65.0 3.8 %collective-permute-done.18.refs_3_ = bf16[128,1024]{1,0:T(8,128)(2,1)S(1)} collective-permute-done((bf16[128,1024]{1,0:T(8,128)(2,1)S(1)}, bf16[128,1024]{1,0:T(8,128)(2,1)S(1)}, u32[]{:S(2)}, u32[]{:S(2)}) %collective-permute-start.18) | collective-permute-done | bytes 262176 | tf_op jit(solution)/shard_map/ppermute | solution.py:46
  68.8 1.0 %merge.1 = bf16[128,4096]{1,0:T(8,128)(2,1)} custom-call(bf16[128,1024]{1,0:T(8,128)(2,1)S(1)} %attend_last.4.refs_0_, bf16[128,1024]{1,0:T(8,128)(2,1)S(1)} %collective-permute-done.15.refs_1_, bf16[128,1024]{1,0:T(8,128)(2,1)S(1)} %collective-permute-done.17.refs_2_, bf16[128,1024]{1,0:T(8,128)(2,1)S(1)} %collective-permute-done.18.refs_3_), custom_call_target="tpu_custom_call" | custom-call | tf_op jit(solution)/shard_map/merge/pallas_call | solution.py:194
  (36 shorter events, 1.8 us)
Async XLA Ops:
  1.7 6.8 %collective-permute-start = (bf16[144,256]{1,0:T(8,128)(2,1)}, bf16[144,256]{1,0:T(8,128)(2,1)S(1)}, u32[]{:S(2)}, u32[]{:S(2)}) collective-permute-start(bf16[144,256]{1,0:T(8,128)(2,1)} %get-tuple-element.41), channel_id=1, source_target_pairs={{0,4},{1,5},{2,6},{3,7},{4,0},{5,1},{6,2},{7,3},{8,12},{9,13},{10,... | collective-permute-start | bytes 221192 | tf_op jit(solution)/shard_map/ppermute | solution.py:46
  3.4 6.6 %collective-permute-start.1 = (bf16[144,256]{1,0:T(8,128)(2,1)}, bf16[144,256]{1,0:T(8,128)(2,1)S(1)}, u32[]{:S(2)}, u32[]{:S(2)}) collective-permute-start(bf16[144,256]{1,0:T(8,128)(2,1)} %get-tuple-element.42), channel_id=1, source_target_pairs={{0,12},{1,13},{2,14},{3,15},{4,8},{5,9},{6,10},{7,11},{8,4},{9,5},... | collective-permute-start | bytes 221192 | tf_op jit(solution)/shard_map/ppermute | solution.py:46
  5.6 6.1 %collective-permute-start.2 = (bf16[144,256]{1,0:T(8,128)(2,1)}, bf16[144,256]{1,0:T(8,128)(2,1)S(1)}, u32[]{:S(2)}, u32[]{:S(2)}) collective-permute-start(bf16[144,256]{1,0:T(8,128)(2,1)} %get-tuple-element.43), channel_id=1, source_target_pairs={{0,8},{1,9},{2,10},{3,11},{4,12},{5,13},{6,14},{7,15},{8,0},{9,1},... | collective-permute-start | bytes 221192 | tf_op jit(solution)/shard_map/ppermute | solution.py:46
  6.3 5.3 %copy-start = (bf16[144,256]{1,0:T(8,128)(2,1)S(1)}, bf16[144,256]{1,0:T(8,128)(2,1)}, u32[]{:S(2)}) copy-start(bf16[144,256]{1,0:T(8,128)(2,1)} %get-tuple-element.40.refs_0_) | copy-start | bytes 221188
  8.5 9.4 %copy-start.4 = (bf16[128,1024]{1,0:T(8,128)(2,1)S(1)}, bf16[128,1024]{1,0:T(8,128)(2,1)}, u32[]{:S(2)}) copy-start(bf16[128,1024]{1,0:T(8,128)(2,1)} %get-tuple-element.59) | copy-start | bytes 786436
  8.5 17.8 %copy-start.3 = (bf16[128,1024]{1,0:T(8,128)(2,1)S(1)}, bf16[128,1024]{1,0:T(8,128)(2,1)}, u32[]{:S(2)}) copy-start(bf16[128,1024]{1,0:T(8,128)(2,1)} %get-tuple-element.62) | copy-start | bytes 786436
  12.0 13.1 %collective-permute-start.7 = (bf16[128,1024]{1,0:T(8,128)(2,1)}, bf16[128,1024]{1,0:T(8,128)(2,1)S(1)}, u32[]{:S(2)}, u32[]{:S(2)}) collective-permute-start(bf16[128,1024]{1,0:T(8,128)(2,1)} %get-tuple-element.52), channel_id=1, source_target_pairs={{0,4},{1,5},{2,6},{3,7},{4,0},{5,1},{6,2},{7,3},{8,12},{9,13},{10,... | collective-permute-start | bytes 786440 | tf_op jit(solution)/shard_map/ppermute | solution.py:46
  12.8 17.4 %collective-permute-start.6 = (bf16[512,256]{1,0:T(8,128)(2,1)S(1)}, bf16[512,256]{1,0:T(8,128)(2,1)S(1)}, u32[]{:S(2)}, u32[]{:S(2)}) collective-permute-start(bf16[512,256]{1,0:T(8,128)(2,1)S(1)} %stack.1.refs_1_.refs_2_), channel_id=1, source_target_pairs={{0,2},{1,3},{2,0},{3,1},{4,6},{5,7},{6,4},{7,5},{8,10},{9,11},{10,... | collective-permute-start | bytes 786440 | tf_op jit(solution)/shard_map/ppermute | solution.py:46
  16.0 14.2 %collective-permute-start.5 = (bf16[512,256]{1,0:T(8,128)(2,1)S(1)}, bf16[512,256]{1,0:T(8,128)(2,1)S(1)}, u32[]{:S(2)}, u32[]{:S(2)}) collective-permute-start(bf16[512,256]{1,0:T(8,128)(2,1)S(1)} %stack.1.refs_1_.refs_2_), channel_id=1, source_target_pairs={{0,1},{1,0},{2,3},{3,2},{4,5},{5,4},{6,7},{7,6},{8,9},{9,8},{10,11... | collective-permute-start | bytes 786440 | tf_op jit(solution)/shard_map/ppermute | solution.py:46
  18.0 18.3 %collective-permute-start.14 = (bf16[128,1024]{1,0:T(8,128)(2,1)S(1)}, bf16[128,1024]{1,0:T(8,128)(2,1)S(1)}, u32[]{:S(2)}, u32[]{:S(2)}) collective-permute-start(bf16[128,1024]{1,0:T(8,128)(2,1)S(1)} %copy-done.4), channel_id=1, source_target_pairs={{0,8},{1,9},{2,10},{3,11},{4,12},{5,13},{6,14},{7,15},{8,0},{9,1},... | collective-permute-start | bytes 786440 | tf_op jit(solution)/shard_map/ppermute | solution.py:46
  20.1 1.3 %collective-permute-start.3 = (bf16[8,256]{1,0:T(8,128)(2,1)S(1)}, bf16[8,256]{1,0:T(8,128)(2,1)S(1)}, u32[]{:S(2)}, u32[]{:S(2)}) collective-permute-start(bf16[8,256]{1,0:T(8,128)(2,1)S(1)} %pad_maximum_fusion.2), channel_id=1, source_target_pairs={{0,16},{1,17},{2,18},{3,19},{4,20},{5,21},{6,22},{7,23},{8,24},{9,... | collective-permute-start | bytes 12296 | tf_op jit(solution)/shard_map/ppermute | solution.py:46
  21.4 3.7 %collective-permute-start.4 = (bf16[16,256]{1,0:T(8,128)(2,1)S(1)}, bf16[16,256]{1,0:T(8,128)(2,1)S(1)}, u32[]{:S(2)}, u32[]{:S(2)}) collective-permute-start(bf16[16,256]{1,0:T(8,128)(2,1)S(1)} %concatenate.18), channel_id=1, source_target_pairs={{0,32},{1,33},{2,34},{3,35},{4,36},{5,37},{6,38},{7,39},{8,40},{9,... | collective-permute-start | bytes 24584 | tf_op jit(solution)/shard_map/ppermute | solution.py:46
  25.1 3.3 %copy-start.1 = (s32[1,16]{1,0:T(1,128)S(1)}, s32[1,16]{1,0:T(1,128)}, u32[]{:S(2)}) copy-start(s32[1,16]{1,0:T(1,128)} %offsets) | copy-start | bytes 196
  25.1 5.0 %collective-permute-start.8 = (bf16[32,256]{1,0:T(8,128)(2,1)S(1)}, bf16[32,256]{1,0:T(8,128)(2,1)S(1)}, u32[]{:S(2)}, u32[]{:S(2)}) collective-permute-start(bf16[32,256]{1,0:T(8,128)(2,1)S(1)} %concatenate.19), channel_id=1, source_target_pairs={{0,96},{1,97},{2,98},{3,99},{4,100},{5,101},{6,102},{7,103},{8,104... | collective-permute-start | bytes 49160 | tf_op jit(solution)/shard_map/ppermute | solution.py:46
  26.4 19.4 %collective-permute-start.16 = (bf16[128,1024]{1,0:T(8,128)(2,1)S(1)}, bf16[128,1024]{1,0:T(8,128)(2,1)S(1)}, u32[]{:S(2)}, u32[]{:S(2)}) collective-permute-start(bf16[128,1024]{1,0:T(8,128)(2,1)S(1)} %copy-done.3), channel_id=1, source_target_pairs={{0,12},{1,13},{2,14},{3,15},{4,8},{5,9},{6,10},{7,11},{8,4},{9,5},... | collective-permute-start | bytes 786440 | tf_op jit(solution)/shard_map/ppermute | solution.py:46
  30.2 11.1 %collective-permute-start.10 = (bf16[64,256]{1,0:T(8,128)(2,1)S(1)}, bf16[64,256]{1,0:T(8,128)(2,1)S(1)}, u32[]{:S(2)}, u32[]{:S(2)}) collective-permute-start(bf16[64,256]{1,0:T(8,128)(2,1)S(1)} %pad_maximum_fusion.1), channel_id=1, source_target_pairs={{0,128},{1,129},{2,130},{3,131},{4,132},{5,133},{6,134},{7,135},{8... | collective-permute-start | bytes 98312 | tf_op jit(solution)/shard_map/ppermute | solution.py:46
  34.8 15.7 %collective-permute-start.9 = (bf16[512,256]{1,0:T(8,128)(2,1)S(1)}, bf16[512,256]{1,0:T(8,128)(2,1)S(1)}, u32[]{:S(2)}, u32[]{:S(2)}) collective-permute-start(bf16[512,256]{1,0:T(8,128)(2,1)S(1)} %collective-permute-done.5.refs_2_.refs_3_), channel_id=1, source_target_pairs={{0,2},{1,3},{2,0},{3,1},{4,6},{5,7},{6,4},{7,5},{8,10},{9,11},{10,... | collective-permute-start | bytes 786440 | tf_op jit(solution)/shard_map/ppermute | solution.py:46
  41.3 7.4 %collective-permute-start.13 = (bf16[128,256]{1,0:T(8,128)(2,1)S(1)}, bf16[128,256]{1,0:T(8,128)(2,1)S(1)}, u32[]{:S(2)}, u32[]{:S(2)}) collective-permute-start(bf16[128,256]{1,0:T(8,128)(2,1)S(1)} %pad_maximum_fusion.refs_5_.refs_2_), channel_id=1, source_target_pairs={{0,3},{1,2},{2,1},{3,0},{4,7},{5,6},{6,5},{7,4},{8,11},{9,10},{10,... | collective-permute-start | bytes 196616 | tf_op jit(solution)/shard_map/ppermute | solution.py:46
  43.3 7.1 %collective-permute-start.12 = (bf16[128,256]{1,0:T(8,128)(2,1)S(1)}, bf16[128,256]{1,0:T(8,128)(2,1)S(1)}, u32[]{:S(2)}, u32[]{:S(2)}) collective-permute-start(bf16[128,256]{1,0:T(8,128)(2,1)S(1)} %pad_maximum_fusion.refs_5_.refs_2_), channel_id=1, source_target_pairs={{0,2},{1,3},{2,0},{3,1},{4,6},{5,7},{6,4},{7,5},{8,10},{9,11},{10,... | collective-permute-start | bytes 196616 | tf_op jit(solution)/shard_map/ppermute | solution.py:46
  43.9 6.6 %collective-permute-start.11 = (bf16[128,256]{1,0:T(8,128)(2,1)S(1)}, bf16[128,256]{1,0:T(8,128)(2,1)S(1)}, u32[]{:S(2)}, u32[]{:S(2)}) collective-permute-start(bf16[128,256]{1,0:T(8,128)(2,1)S(1)} %pad_maximum_fusion.refs_5_.refs_2_), channel_id=1, source_target_pairs={{0,1},{1,0},{2,3},{3,2},{4,5},{5,4},{6,7},{7,6},{8,9},{9,8},{10,11... | collective-permute-start | bytes 196616 | tf_op jit(solution)/shard_map/ppermute | solution.py:46
  52.3 12.6 %collective-permute-start.17 = (bf16[128,1024]{1,0:T(8,128)(2,1)S(1)}, bf16[128,1024]{1,0:T(8,128)(2,1)S(1)}, u32[]{:S(2)}, u32[]{:S(2)}) collective-permute-start(bf16[128,1024]{1,0:T(8,128)(2,1)S(1)} %attend_last.6), channel_id=1, source_target_pairs={{0,12},{1,13},{2,14},{3,15},{4,8},{5,9},{6,10},{7,11},{8,4},{9,5},... | collective-permute-start | bytes 786440 | tf_op jit(solution)/shard_map/ppermute | solution.py:46
  56.4 8.6 %collective-permute-start.15 = (bf16[128,1024]{1,0:T(8,128)(2,1)S(1)}, bf16[128,1024]{1,0:T(8,128)(2,1)S(1)}, u32[]{:S(2)}, u32[]{:S(2)}) collective-permute-start(bf16[128,1024]{1,0:T(8,128)(2,1)S(1)} %attend_last.5), channel_id=1, source_target_pairs={{0,4},{1,5},{2,6},{3,7},{4,0},{5,1},{6,2},{7,3},{8,12},{9,13},{10,... | collective-permute-start | bytes 786440 | tf_op jit(solution)/shard_map/ppermute | solution.py:46
  56.5 4.7 %copy-start.2 = (bf16[128,1024]{1,0:T(8,128)(2,1)S(1)}, bf16[128,1024]{1,0:T(8,128)(2,1)}, u32[]{:S(2)}) copy-start(bf16[128,1024]{1,0:T(8,128)(2,1)} %get-tuple-element.50.refs_0_) | copy-start | bytes 786436
  58.3 10.4 %collective-permute-start.18 = (bf16[128,1024]{1,0:T(8,128)(2,1)S(1)}, bf16[128,1024]{1,0:T(8,128)(2,1)S(1)}, u32[]{:S(2)}, u32[]{:S(2)}) collective-permute-start(bf16[128,1024]{1,0:T(8,128)(2,1)S(1)} %attend_last.7), channel_id=1, source_target_pairs={{0,8},{1,9},{2,10},{3,11},{4,12},{5,13},{6,14},{7,15},{8,0},{9,1},... | collective-permute-start | bytes 786440 | tf_op jit(solution)/shard_map/ppermute | solution.py:46

commit v4 on v3

--- a/solution.py
+++ b/solution.py
@@ -13,7 +13,7 @@
 WIDE = GROUP * HD
 TOK = 128
 RIDE = 16
-PAIR = 2
+PAIR = 4
 PAIRS = GROUP // PAIR
 SCALE = math.log2(math.e) / math.sqrt(HD)
 NEG = -1e30
@@ -109,7 +109,7 @@
         split_kv_kernel,
         in_specs=[HBM] * 4,
         out_specs=[VMEM] * 4,
-        out_shape=[jax.ShapeDtypeStruct((TOK + RIDE, 2 * HD), jnp.bfloat16)] * 4,
+        out_shape=[pltpu.VMEM((TOK + RIDE, 2 * HD), jnp.bfloat16)] * 4,
         scratch_shapes=[pltpu.VMEM((2, 2, KV_HEADS * HD), jnp.bfloat16), pltpu.SemaphoreType.DMA((10,))],
         name="split_kv",
     )(keys, values, prompt_keys, prompt_values)
@@ -130,7 +130,7 @@
         split_q_kernel,
         in_specs=[HBM],
         out_specs=[VMEM] * 4,
-        out_shape=[jax.ShapeDtypeStruct((TOK, WIDE), jnp.bfloat16)] * 4,
+        out_shape=[pltpu.VMEM((TOK, WIDE), jnp.bfloat16)] * 4,
         scratch_shapes=[pltpu.SemaphoreType.DMA((4,))],
         name="split_q",
     )(q)
@@ -348,10 +348,10 @@
         out = attend(info, group, [q[i] for i in group], near, column_blocks((0, 1, 2)))
         return {i: [out[n], out[len(group) + n]] for n, i in enumerate(group)}, out[-1]
 
-    state, mark = begin([3, 1])
+    state, mark = begin([1, 2])
     mark, prompt = lax.optimization_barrier((mark, prompt))
     prompts = [send(prompt, pairs) for pairs in Z_STEPS]
-    state |= begin([2])[0]
+    state |= begin([3])[0]
     pieces = [z_both, prompt] + prompts
     late = column_blocks((3,)) + [None] * 4
     results = [None] * 4

time: 70.1 us -> 66.7 us (0.951)
  Pallas kernels: 23.2 us -> 20.8 us
  starting transfers between devices: 31.9 us -> 30.7 us
    ppermute x19, starting transfers between devices: 31.9 us -> 30.7 us  [send(): return lax.ppermute(value, AXES, pairs)]
    pallas_call x1, Pallas kernels: 2.21 us -> 1.22 us  [split_q(): pl.pallas_call(split_q_kernel, in_specs=[HBM], out_specs=[VMEM] * 4, out_...]
    pallas_call x1, Pallas kernels: 1.71 us -> 1 us  [split_kv(): pl.pallas_call(split_kv_kernel, in_specs=[HBM] * 4, out_specs=[VMEM] * 4,...]
  transfers between devices with their start and end apart: 19 -> 19, of which waited for: 7 -> 8; matrix products, arithmetic and copies ran while one was open for 0% -> 0% of each run, Pallas kernels for 26% -> 25%
where the time goes in v4:
time: 66.7 us; the launch traced here: 66 us
  starting transfers between devices  30.7 us (46%)
  Pallas kernels  20.8 us (31%)
  waiting for transfers between devices  13.6 us (20%)
  between operations  0.97 us (1%)
    ppermute x19, starting transfers between devices, send(): return lax.ppermute(value, AXES, pairs)  30.7 us
    pallas_call x6, Pallas kernels, attend(): pl.pallas_call(make_kernel(queries, sizes, blocks, bool(carry), last), in...  16.6 us
    ppermute x19, waiting for transfers between devices, send(): return lax.ppermute(value, AXES, pairs)  13.6 us
  transfers between devices with their start and end apart: 19, of which 8 were waited for; matrix products, arithmetic and copies ran while one was open for 0% of the time, Pallas kernels for 25%

profile of v4, /device:TPU:6, one launch (start us, length us, event | category | flops | bytes accessed | tf_op | source)
XLA Modules:
  0.0 66.0 jit_solution(8246690101466990759)
XLA Ops:
  0.0 1.0 %split_kv.1 = (bf16[144,256]{1,0:T(8,128)(2,1)S(1)}, bf16[144,256]{1,0:T(8,128)(2,1)S(1)}, bf16[144,256]{1,0:T(8,128)(2,1)S(1)}, bf16[144,256]{1,0:T(8,128)(2,1)S(1)}) custom-call(bf16[128,512]{1,0:T(8,128)(2,1)} %bitcast.5, bf16[128,512]{1,0:T(8,128)(2,1)} %bitcast.6, bf16[2,512]{1,0:T(2,128)(2,1)} %pk_ref.1, bf16[2,512]{1,0:T(2,128)(2,1)} %pv_ref.1), custom_call_target="tpu_custom_call" | custom-call | tf_op jit(solution)/shard_map/split_kv/pallas_call | solution.py:108
  1.0 1.7 %collective-permute-start = (bf16[144,256]{1,0:T(8,128)(2,1)S(1)}, bf16[144,256]{1,0:T(8,128)(2,1)S(1)}, u32[]{:S(2)}, u32[]{:S(2)}) collective-permute-start(bf16[144,256]{1,0:T(8,128)(2,1)S(1)} %get-tuple-element.41), channel_id=1, source_target_pairs={{0,4},{1,5},{2,6},{3,7},{4,0},{5,1},{6,2},{7,3},{8,12},{9,13},{10,... | collective-permute-start | bytes 221192 | tf_op jit(solution)/shard_map/ppermute | solution.py:46
  2.7 2.2 %collective-permute-start.1 = (bf16[144,256]{1,0:T(8,128)(2,1)S(1)}, bf16[144,256]{1,0:T(8,128)(2,1)S(1)}, u32[]{:S(2)}, u32[]{:S(2)}) collective-permute-start(bf16[144,256]{1,0:T(8,128)(2,1)S(1)} %get-tuple-element.42), channel_id=1, source_target_pairs={{0,12},{1,13},{2,14},{3,15},{4,8},{5,9},{6,10},{7,11},{8,4},{9,5},... | collective-permute-start | bytes 221192 | tf_op jit(solution)/shard_map/ppermute | solution.py:46
  4.9 0.7 %collective-permute-start.2 = (bf16[144,256]{1,0:T(8,128)(2,1)S(1)}, bf16[144,256]{1,0:T(8,128)(2,1)S(1)}, u32[]{:S(2)}, u32[]{:S(2)}) collective-permute-start(bf16[144,256]{1,0:T(8,128)(2,1)S(1)} %get-tuple-element.43), channel_id=1, source_target_pairs={{0,8},{1,9},{2,10},{3,11},{4,12},{5,13},{6,14},{7,15},{8,0},{9,1},... | collective-permute-start | bytes 221192 | tf_op jit(solution)/shard_map/ppermute | solution.py:46
  5.6 1.2 %split_q.1 = (bf16[128,1024]{1,0:T(8,128)(2,1)S(1)}, bf16[128,1024]{1,0:T(8,128)(2,1)S(1)}, bf16[128,1024]{1,0:T(8,128)(2,1)S(1)}, bf16[128,1024]{1,0:T(8,128)(2,1)S(1)}) custom-call(bf16[128,4096]{1,0:T(8,128)(2,1)} %bitcast.4), custom_call_target="tpu_custom_call" | custom-call | tf_op jit(solution)/shard_map/split_q/pallas_call | solution.py:129
  6.8 2.2 %collective-permute-done.1.refs_2_ = bf16[144,256]{1,0:T(8,128)(2,1)S(1)} collective-permute-done((bf16[144,256]{1,0:T(8,128)(2,1)S(1)}, bf16[144,256]{1,0:T(8,128)(2,1)S(1)}, u32[]{:S(2)}, u32[]{:S(2)}) %collective-permute-start.1) | collective-permute-done | bytes 73760 | tf_op jit(solution)/shard_map/ppermute | solution.py:46
  9.0 1.7 %collective-permute-done.2.refs_3_ = bf16[144,256]{1,0:T(8,128)(2,1)S(1)} collective-permute-done((bf16[144,256]{1,0:T(8,128)(2,1)S(1)}, bf16[144,256]{1,0:T(8,128)(2,1)S(1)}, u32[]{:S(2)}, u32[]{:S(2)}) %collective-permute-start.2) | collective-permute-done | bytes 73760 | tf_op jit(solution)/shard_map/ppermute | solution.py:46
  11.1 0.8 %collective-permute-start.7 = (bf16[128,1024]{1,0:T(8,128)(2,1)S(1)}, bf16[128,1024]{1,0:T(8,128)(2,1)S(1)}, u32[]{:S(2)}, u32[]{:S(2)}) collective-permute-start(bf16[128,1024]{1,0:T(8,128)(2,1)S(1)} %get-tuple-element.52), channel_id=1, source_target_pairs={{0,4},{1,5},{2,6},{3,7},{4,0},{5,1},{6,2},{7,3},{8,12},{9,13},{10,... | collective-permute-start | bytes 786440 | tf_op jit(solution)/shard_map/ppermute | solution.py:46
  11.8 3.3 %collective-permute-start.6 = (bf16[512,256]{1,0:T(8,128)(2,1)S(1)}, bf16[512,256]{1,0:T(8,128)(2,1)S(1)}, u32[]{:S(2)}, u32[]{:S(2)}) collective-permute-start(bf16[512,256]{1,0:T(8,128)(2,1)S(1)} %stack.1.refs_1_.refs_2_), channel_id=1, source_target_pairs={{0,2},{1,3},{2,0},{3,1},{4,6},{5,7},{6,4},{7,5},{8,10},{9,11},{10,... | collective-permute-start | bytes 786440 | tf_op jit(solution)/shard_map/ppermute | solution.py:46
  15.1 1.9 %collective-permute-start.5 = (bf16[512,256]{1,0:T(8,128)(2,1)S(1)}, bf16[512,256]{1,0:T(8,128)(2,1)S(1)}, u32[]{:S(2)}, u32[]{:S(2)}) collective-permute-start(bf16[512,256]{1,0:T(8,128)(2,1)S(1)} %stack.1.refs_1_.refs_2_), channel_id=1, source_target_pairs={{0,1},{1,0},{2,3},{3,2},{4,5},{5,4},{6,7},{7,6},{8,9},{9,8},{10,11... | collective-permute-start | bytes 786440 | tf_op jit(solution)/shard_map/ppermute | solution.py:46
  17.0 0.7 %collective-permute-start.14 = (bf16[128,1024]{1,0:T(8,128)(2,1)S(1)}, bf16[128,1024]{1,0:T(8,128)(2,1)S(1)}, u32[]{:S(2)}, u32[]{:S(2)}) collective-permute-start(bf16[128,1024]{1,0:T(8,128)(2,1)S(1)} %get-tuple-element.59), channel_id=1, source_target_pairs={{0,12},{1,13},{2,14},{3,15},{4,8},{5,9},{6,10},{7,11},{8,4},{9,5},... | collective-permute-start | bytes 786440 | tf_op jit(solution)/shard_map/ppermute | solution.py:46
  17.9 1.2 %collective-permute-done.3 = bf16[8,256]{1,0:T(8,128)(2,1)S(1)} collective-permute-done((bf16[8,256]{1,0:T(8,128)(2,1)S(1)}, bf16[8,256]{1,0:T(8,128)(2,1)S(1)}, u32[]{:S(2)}, u32[]{:S(2)}) %collective-permute-start.3) | collective-permute-done | bytes 4128 | tf_op jit(solution)/shard_map/ppermute | solution.py:46
  19.1 0.9 %collective-permute-start.4 = (bf16[16,256]{1,0:T(8,128)(2,1)S(1)}, bf16[16,256]{1,0:T(8,128)(2,1)S(1)}, u32[]{:S(2)}, u32[]{:S(2)}) collective-permute-start(bf16[16,256]{1,0:T(8,128)(2,1)S(1)} %concatenate.18), channel_id=1, source_target_pairs={{0,32},{1,33},{2,34},{3,35},{4,36},{5,37},{6,38},{7,39},{8,40},{9,... | collective-permute-start | bytes 24584 | tf_op jit(solution)/shard_map/ppermute | solution.py:46
  20.0 2.8 %collective-permute-done.4 = bf16[16,256]{1,0:T(8,128)(2,1)S(1)} collective-permute-done((bf16[16,256]{1,0:T(8,128)(2,1)S(1)}, bf16[16,256]{1,0:T(8,128)(2,1)S(1)}, u32[]{:S(2)}, u32[]{:S(2)}) %collective-permute-start.4) | collective-permute-done | bytes 8224 | tf_op jit(solution)/shard_map/ppermute | solution.py:46
  24.1 2.8 %collective-permute-start.17 = (bf16[128,1024]{1,0:T(8,128)(2,1)S(1)}, bf16[128,1024]{1,0:T(8,128)(2,1)S(1)}, u32[]{:S(2)}, u32[]{:S(2)}) collective-permute-start(bf16[128,1024]{1,0:T(8,128)(2,1)S(1)} %get-tuple-element.64), channel_id=1, source_target_pairs={{0,8},{1,9},{2,10},{3,11},{4,12},{5,13},{6,14},{7,15},{8,0},{9,1},... | collective-permute-start | bytes 786440 | tf_op jit(solution)/shard_map/ppermute | solution.py:46
  27.9 5.4 %collective-permute-start.10 = (bf16[64,256]{1,0:T(8,128)(2,1)S(1)}, bf16[64,256]{1,0:T(8,128)(2,1)S(1)}, u32[]{:S(2)}, u32[]{:S(2)}) collective-permute-start(bf16[64,256]{1,0:T(8,128)(2,1)S(1)} %pad_maximum_fusion.1), channel_id=1, source_target_pairs={{0,128},{1,129},{2,130},{3,131},{4,132},{5,133},{6,134},{7,135},{8... | collective-permute-start | bytes 98312 | tf_op jit(solution)/shard_map/ppermute | solution.py:46
  33.9 5.0 %attend_first.2 = (f32[2,512,128]{2,1,0:T(8,128)S(1)}, f32[2,512,128]{2,1,0:T(8,128)S(1)}, f32[2,512,128]{2,1,0:T(8,128)S(1)}, f32[2,512,128]{2,1,0:T(8,128)S(1)}, f32[8,128]{1,0:T(8,128)}) custom-call(s32[24,128]{1,0:T(8,128)S(1)} %places.1.info_ref, bf16[128,1024]{1,0:T(8,128)(2,1)S(1)} %collective-permute-done.7.refs_0_, ...), custom_call_target="tpu_custom_call" | custom-call | flops 1610612736 | bytes 2097152 | tf_op jit(solution)/shard_map/attend_first/pallas_call | solution.py:302
  39.0 2.0 %collective-permute-start.13 = (bf16[128,256]{1,0:T(8,128)(2,1)S(1)}, bf16[128,256]{1,0:T(8,128)(2,1)S(1)}, u32[]{:S(2)}, u32[]{:S(2)}) collective-permute-start(bf16[128,256]{1,0:T(8,128)(2,1)S(1)} %pad_maximum_fusion.refs_5_.refs_2_), channel_id=1, source_target_pairs={{0,3},{1,2},{2,1},{3,0},{4,7},{5,6},{6,5},{7,4},{8,11},{9,10},{10,... | collective-permute-start | bytes 196616 | tf_op jit(solution)/shard_map/ppermute | solution.py:46
  41.0 1.4 %collective-permute-start.12 = (bf16[128,256]{1,0:T(8,128)(2,1)S(1)}, bf16[128,256]{1,0:T(8,128)(2,1)S(1)}, u32[]{:S(2)}, u32[]{:S(2)}) collective-permute-start(bf16[128,256]{1,0:T(8,128)(2,1)S(1)} %pad_maximum_fusion.refs_5_.refs_2_), channel_id=1, source_target_pairs={{0,2},{1,3},{2,0},{3,1},{4,6},{5,7},{6,4},{7,5},{8,10},{9,11},{10,... | collective-permute-start | bytes 196616 | tf_op jit(solution)/shard_map/ppermute | solution.py:46
  42.4 1.1 %collective-permute-start.11 = (bf16[128,256]{1,0:T(8,128)(2,1)S(1)}, bf16[128,256]{1,0:T(8,128)(2,1)S(1)}, u32[]{:S(2)}, u32[]{:S(2)}) collective-permute-start(bf16[128,256]{1,0:T(8,128)(2,1)S(1)} %pad_maximum_fusion.refs_5_.refs_2_), channel_id=1, source_target_pairs={{0,1},{1,0},{2,3},{3,2},{4,5},{5,4},{6,7},{7,6},{8,9},{9,8},{10,11... | collective-permute-start | bytes 196616 | tf_op jit(solution)/shard_map/ppermute | solution.py:46
  43.4 2.8 %attend_first.3 = (f32[2,512,128]{2,1,0:T(8,128)S(1)}, f32[2,512,128]{2,1,0:T(8,128)S(1)}, f32[8,128]{1,0:T(8,128)}) custom-call(s32[24,128]{1,0:T(8,128)S(1)} %places.1.info_ref, bf16[128,1024]{1,0:T(8,128)(2,1)S(1)} %collective-permute-done.17.refs_0_, bf16[512,256]{1,0:T(8,128)(2,1)S(1)} %stack.1.refs_1_.refs_2_, ...), custom_call_target="tpu_custom_call" | custom-call | flops 805306368 | bytes 1048576 | tf_op jit(solution)/shard_map/attend_first/pallas_call | solution.py:302
  46.2 2.7 %collective-permute-done.12.refs_7_.refs_4_ = bf16[128,256]{1,0:T(8,128)(2,1)S(1)} collective-permute-done((bf16[128,256]{1,0:T(8,128)(2,1)S(1)}, bf16[128,256]{1,0:T(8,128)(2,1)S(1)}, u32[]{:S(2)}, u32[]{:S(2)}) %collective-permute-start.12) | collective-permute-done | bytes 65568 | tf_op jit(solution)/shard_map/ppermute | solution.py:46
  48.9 1.7 %attend_last.7 = bf16[128,1024]{1,0:T(8,128)(2,1)S(1)} custom-call(s32[24,128]{1,0:T(8,128)S(1)} %places.1.info_ref, bf16[128,1024]{1,0:T(8,128)(2,1)S(1)} %collective-permute-done.17.refs_0_, bf16[512,256]{1,0:T(8,128)(2,1)S(1)} %collective-permute-done.9.refs_4_.refs_1_, bf16[128,256]{1,0:T(8,128)(2,1)S(1)} %pad_maximum_fusion.refs_5_.refs_2_, ...), custom_call_target="tpu_custom_call" | custom-call | flops 536870912 | bytes 1048576 | tf_op jit(solution)/shard_map/attend_last/pallas_call | solution.py:302
  50.7 2.3 %collective-permute-start.18 = (bf16[128,1024]{1,0:T(8,128)(2,1)S(1)}, bf16[128,1024]{1,0:T(8,128)(2,1)S(1)}, u32[]{:S(2)}, u32[]{:S(2)}) collective-permute-start(bf16[128,1024]{1,0:T(8,128)(2,1)S(1)} %attend_last.7), channel_id=1, source_target_pairs={{0,8},{1,9},{2,10},{3,11},{4,12},{5,13},{6,14},{7,15},{8,0},{9,1},... | collective-permute-start | bytes 786440 | tf_op jit(solution)/shard_map/ppermute | solution.py:46
  52.9 1.7 %attend_last.5 = bf16[128,1024]{1,0:T(8,128)(2,1)S(1)} custom-call(s32[24,128]{1,0:T(8,128)S(1)} %places.1.info_ref, bf16[128,1024]{1,0:T(8,128)(2,1)S(1)} %collective-permute-done.7.refs_0_, bf16[512,256]{1,0:T(8,128)(2,1)S(1)} %collective-permute-done.9.refs_4_.refs_1_, bf16[128,256]{1,0:T(8,128)(2,1)S(1)} %pad_maximum_fusion.refs_5_.refs_2_, ...), custom_call_target="tpu_custom_call" | custom-call | flops 536870912 | bytes 1048576 | tf_op jit(solution)/shard_map/attend_last/pallas_call | solution.py:302
  54.7 0.8 %collective-permute-start.15 = (bf16[128,1024]{1,0:T(8,128)(2,1)S(1)}, bf16[128,1024]{1,0:T(8,128)(2,1)S(1)}, u32[]{:S(2)}, u32[]{:S(2)}) collective-permute-start(bf16[128,1024]{1,0:T(8,128)(2,1)S(1)} %attend_last.5), channel_id=1, source_target_pairs={{0,4},{1,5},{2,6},{3,7},{4,0},{5,1},{6,2},{7,3},{8,12},{9,13},{10,... | collective-permute-start | bytes 786440 | tf_op jit(solution)/shard_map/ppermute | solution.py:46
  55.5 1.7 %attend_last.6 = bf16[128,1024]{1,0:T(8,128)(2,1)S(1)} custom-call(s32[24,128]{1,0:T(8,128)S(1)} %places.1.info_ref, bf16[128,1024]{1,0:T(8,128)(2,1)S(1)} %collective-permute-done.14.refs_1_.refs_0_, bf16[512,256]{1,0:T(8,128)(2,1)S(1)} %collective-permute-done.9.refs_4_.refs_1_, bf16[128,256]{1,0:T(8,128)(2,1)S(1)} %pad_maximum_fusion.refs_5_.refs_2_, ...), custom_call_target="tpu_custom_call" | custom-call | flops 536870912 | bytes 1048576 | tf_op jit(solution)/shard_map/attend_last/pallas_call | solution.py:302
  57.2 1.5 %collective-permute-start.16 = (bf16[128,1024]{1,0:T(8,128)(2,1)S(1)}, bf16[128,1024]{1,0:T(8,128)(2,1)S(1)}, u32[]{:S(2)}, u32[]{:S(2)}) collective-permute-start(bf16[128,1024]{1,0:T(8,128)(2,1)S(1)} %attend_last.6), channel_id=1, source_target_pairs={{0,12},{1,13},{2,14},{3,15},{4,8},{5,9},{6,10},{7,11},{8,4},{9,5},... | collective-permute-start | bytes 786440 | tf_op jit(solution)/shard_map/ppermute | solution.py:46
  58.7 3.6 %attend_last.4.refs_0_ = bf16[128,1024]{1,0:T(8,128)(2,1)S(1)} custom-call(s32[24,128]{1,0:T(8,128)S(1)} %places.1.info_ref, bf16[128,1024]{1,0:T(8,128)(2,1)S(1)} %get-tuple-element.50.refs_0_, bf16[512,256]{1,0:T(8,128)(2,1)S(1)} %stack.1.refs_1_.refs_2_, bf16[512,256]{1,0:T(8,128)(2,1)S(1)} %collective-permute-done.5.refs_2_.refs_3_, ...), custom_call_target="tpu_custom_call" | custom-call | flops 1342177280 | bytes 1048576 | tf_op jit(solution)/shard_map/attend_last/pallas_call | solution.py:302
  62.3 1.5 %collective-permute-done.15.refs_1_ = bf16[128,1024]{1,0:T(8,128)(2,1)S(1)} collective-permute-done((bf16[128,1024]{1,0:T(8,128)(2,1)S(1)}, bf16[128,1024]{1,0:T(8,128)(2,1)S(1)}, u32[]{:S(2)}, u32[]{:S(2)}) %collective-permute-start.15) | collective-permute-done | bytes 262176 | tf_op jit(solution)/shard_map/ppermute | solution.py:46
  63.8 1.1 %collective-permute-done.16.refs_2_ = bf16[128,1024]{1,0:T(8,128)(2,1)S(1)} collective-permute-done((bf16[128,1024]{1,0:T(8,128)(2,1)S(1)}, bf16[128,1024]{1,0:T(8,128)(2,1)S(1)}, u32[]{:S(2)}, u32[]{:S(2)}) %collective-permute-start.16) | collective-permute-done | bytes 262176 | tf_op jit(solution)/shard_map/ppermute | solution.py:46
  64.9 1.0 %merge.1 = bf16[128,4096]{1,0:T(8,128)(2,1)} custom-call(bf16[128,1024]{1,0:T(8,128)(2,1)S(1)} %attend_last.4.refs_0_, bf16[128,1024]{1,0:T(8,128)(2,1)S(1)} %collective-permute-done.15.refs_1_, bf16[128,1024]{1,0:T(8,128)(2,1)S(1)} %collective-permute-done.16.refs_2_, bf16[128,1024]{1,0:T(8,128)(2,1)S(1)} %collective-permute-done.18.refs_3_), custom_call_target="tpu_custom_call" | custom-call | tf_op jit(solution)/shard_map/merge/pallas_call | solution.py:194
  (28 shorter events, 2.8 us)
Async XLA Ops:
  1.0 5.8 %collective-permute-start = (bf16[144,256]{1,0:T(8,128)(2,1)S(1)}, bf16[144,256]{1,0:T(8,128)(2,1)S(1)}, u32[]{:S(2)}, u32[]{:S(2)}) collective-permute-start(bf16[144,256]{1,0:T(8,128)(2,1)S(1)} %get-tuple-element.41), channel_id=1, source_target_pairs={{0,4},{1,5},{2,6},{3,7},{4,0},{5,1},{6,2},{7,3},{8,12},{9,13},{10,... | collective-permute-start | bytes 221192 | tf_op jit(solution)/shard_map/ppermute | solution.py:46
  2.7 6.4 %collective-permute-start.1 = (bf16[144,256]{1,0:T(8,128)(2,1)S(1)}, bf16[144,256]{1,0:T(8,128)(2,1)S(1)}, u32[]{:S(2)}, u32[]{:S(2)}) collective-permute-start(bf16[144,256]{1,0:T(8,128)(2,1)S(1)} %get-tuple-element.42), channel_id=1, source_target_pairs={{0,12},{1,13},{2,14},{3,15},{4,8},{5,9},{6,10},{7,11},{8,4},{9,5},... | collective-permute-start | bytes 221192 | tf_op jit(solution)/shard_map/ppermute | solution.py:46
  4.9 5.9 %collective-permute-start.2 = (bf16[144,256]{1,0:T(8,128)(2,1)S(1)}, bf16[144,256]{1,0:T(8,128)(2,1)S(1)}, u32[]{:S(2)}, u32[]{:S(2)}) collective-permute-start(bf16[144,256]{1,0:T(8,128)(2,1)S(1)} %get-tuple-element.43), channel_id=1, source_target_pairs={{0,8},{1,9},{2,10},{3,11},{4,12},{5,13},{6,14},{7,15},{8,0},{9,1},... | collective-permute-start | bytes 221192 | tf_op jit(solution)/shard_map/ppermute | solution.py:46
  11.1 11.8 %collective-permute-start.7 = (bf16[128,1024]{1,0:T(8,128)(2,1)S(1)}, bf16[128,1024]{1,0:T(8,128)(2,1)S(1)}, u32[]{:S(2)}, u32[]{:S(2)}) collective-permute-start(bf16[128,1024]{1,0:T(8,128)(2,1)S(1)} %get-tuple-element.52), channel_id=1, source_target_pairs={{0,4},{1,5},{2,6},{3,7},{4,0},{5,1},{6,2},{7,3},{8,12},{9,13},{10,... | collective-permute-start | bytes 786440 | tf_op jit(solution)/shard_map/ppermute | solution.py:46
  11.8 16.1 %collective-permute-start.6 = (bf16[512,256]{1,0:T(8,128)(2,1)S(1)}, bf16[512,256]{1,0:T(8,128)(2,1)S(1)}, u32[]{:S(2)}, u32[]{:S(2)}) collective-permute-start(bf16[512,256]{1,0:T(8,128)(2,1)S(1)} %stack.1.refs_1_.refs_2_), channel_id=1, source_target_pairs={{0,2},{1,3},{2,0},{3,1},{4,6},{5,7},{6,4},{7,5},{8,10},{9,11},{10,... | collective-permute-start | bytes 786440 | tf_op jit(solution)/shard_map/ppermute | solution.py:46
  15.1 12.8 %collective-permute-start.5 = (bf16[512,256]{1,0:T(8,128)(2,1)S(1)}, bf16[512,256]{1,0:T(8,128)(2,1)S(1)}, u32[]{:S(2)}, u32[]{:S(2)}) collective-permute-start(bf16[512,256]{1,0:T(8,128)(2,1)S(1)} %stack.1.refs_1_.refs_2_), channel_id=1, source_target_pairs={{0,1},{1,0},{2,3},{3,2},{4,5},{5,4},{6,7},{7,6},{8,9},{9,8},{10,11... | collective-permute-start | bytes 786440 | tf_op jit(solution)/shard_map/ppermute | solution.py:46
  17.0 16.9 %collective-permute-start.14 = (bf16[128,1024]{1,0:T(8,128)(2,1)S(1)}, bf16[128,1024]{1,0:T(8,128)(2,1)S(1)}, u32[]{:S(2)}, u32[]{:S(2)}) collective-permute-start(bf16[128,1024]{1,0:T(8,128)(2,1)S(1)} %get-tuple-element.59), channel_id=1, source_target_pairs={{0,12},{1,13},{2,14},{3,15},{4,8},{5,9},{6,10},{7,11},{8,4},{9,5},... | collective-permute-start | bytes 786440 | tf_op jit(solution)/shard_map/ppermute | solution.py:46
  17.8 1.3 %collective-permute-start.3 = (bf16[8,256]{1,0:T(8,128)(2,1)S(1)}, bf16[8,256]{1,0:T(8,128)(2,1)S(1)}, u32[]{:S(2)}, u32[]{:S(2)}) collective-permute-start(bf16[8,256]{1,0:T(8,128)(2,1)S(1)} %pad_maximum_fusion.2), channel_id=1, source_target_pairs={{0,16},{1,17},{2,18},{3,19},{4,20},{5,21},{6,22},{7,23},{8,24},{9,... | collective-permute-start | bytes 12296 | tf_op jit(solution)/shard_map/ppermute | solution.py:46
  19.1 3.7 %collective-permute-start.4 = (bf16[16,256]{1,0:T(8,128)(2,1)S(1)}, bf16[16,256]{1,0:T(8,128)(2,1)S(1)}, u32[]{:S(2)}, u32[]{:S(2)}) collective-permute-start(bf16[16,256]{1,0:T(8,128)(2,1)S(1)} %concatenate.18), channel_id=1, source_target_pairs={{0,32},{1,33},{2,34},{3,35},{4,36},{5,37},{6,38},{7,39},{8,40},{9,... | collective-permute-start | bytes 24584 | tf_op jit(solution)/shard_map/ppermute | solution.py:46
  22.8 4.0 %copy-start = (s32[1,16]{1,0:T(1,128)S(1)}, s32[1,16]{1,0:T(1,128)}, u32[]{:S(2)}) copy-start(s32[1,16]{1,0:T(1,128)} %offsets) | copy-start | bytes 196
  22.9 5.0 %collective-permute-start.8 = (bf16[32,256]{1,0:T(8,128)(2,1)S(1)}, bf16[32,256]{1,0:T(8,128)(2,1)S(1)}, u32[]{:S(2)}, u32[]{:S(2)}) collective-permute-start(bf16[32,256]{1,0:T(8,128)(2,1)S(1)} %concatenate.19), channel_id=1, source_target_pairs={{0,96},{1,97},{2,98},{3,99},{4,100},{5,101},{6,102},{7,103},{8,104... | collective-permute-start | bytes 49160 | tf_op jit(solution)/shard_map/ppermute | solution.py:46
  24.1 19.4 %collective-permute-start.17 = (bf16[128,1024]{1,0:T(8,128)(2,1)S(1)}, bf16[128,1024]{1,0:T(8,128)(2,1)S(1)}, u32[]{:S(2)}, u32[]{:S(2)}) collective-permute-start(bf16[128,1024]{1,0:T(8,128)(2,1)S(1)} %get-tuple-element.64), channel_id=1, source_target_pairs={{0,8},{1,9},{2,10},{3,11},{4,12},{5,13},{6,14},{7,15},{8,0},{9,1},... | collective-permute-start | bytes 786440 | tf_op jit(solution)/shard_map/ppermute | solution.py:46
  27.9 11.0 %collective-permute-start.10 = (bf16[64,256]{1,0:T(8,128)(2,1)S(1)}, bf16[64,256]{1,0:T(8,128)(2,1)S(1)}, u32[]{:S(2)}, u32[]{:S(2)}) collective-permute-start(bf16[64,256]{1,0:T(8,128)(2,1)S(1)} %pad_maximum_fusion.1), channel_id=1, source_target_pairs={{0,128},{1,129},{2,130},{3,131},{4,132},{5,133},{6,134},{7,135},{8... | collective-permute-start | bytes 98312 | tf_op jit(solution)/shard_map/ppermute | solution.py:46
  33.3 15.6 %collective-permute-start.9 = (bf16[512,256]{1,0:T(8,128)(2,1)S(1)}, bf16[512,256]{1,0:T(8,128)(2,1)S(1)}, u32[]{:S(2)}, u32[]{:S(2)}) collective-permute-start(bf16[512,256]{1,0:T(8,128)(2,1)S(1)} %collective-permute-done.5.refs_2_.refs_3_), channel_id=1, source_target_pairs={{0,2},{1,3},{2,0},{3,1},{4,6},{5,7},{6,4},{7,5},{8,10},{9,11},{10,... | collective-permute-start | bytes 786440 | tf_op jit(solution)/shard_map/ppermute | solution.py:46
  39.0 7.3 %collective-permute-start.13 = (bf16[128,256]{1,0:T(8,128)(2,1)S(1)}, bf16[128,256]{1,0:T(8,128)(2,1)S(1)}, u32[]{:S(2)}, u32[]{:S(2)}) collective-permute-start(bf16[128,256]{1,0:T(8,128)(2,1)S(1)} %pad_maximum_fusion.refs_5_.refs_2_), channel_id=1, source_target_pairs={{0,3},{1,2},{2,1},{3,0},{4,7},{5,6},{6,5},{7,4},{8,11},{9,10},{10,... | collective-permute-start | bytes 196616 | tf_op jit(solution)/shard_map/ppermute | solution.py:46
  41.0 7.9 %collective-permute-start.12 = (bf16[128,256]{1,0:T(8,128)(2,1)S(1)}, bf16[128,256]{1,0:T(8,128)(2,1)S(1)}, u32[]{:S(2)}, u32[]{:S(2)}) collective-permute-start(bf16[128,256]{1,0:T(8,128)(2,1)S(1)} %pad_maximum_fusion.refs_5_.refs_2_), channel_id=1, source_target_pairs={{0,2},{1,3},{2,0},{3,1},{4,6},{5,7},{6,4},{7,5},{8,10},{9,11},{10,... | collective-permute-start | bytes 196616 | tf_op jit(solution)/shard_map/ppermute | solution.py:46
  42.4 6.5 %collective-permute-start.11 = (bf16[128,256]{1,0:T(8,128)(2,1)S(1)}, bf16[128,256]{1,0:T(8,128)(2,1)S(1)}, u32[]{:S(2)}, u32[]{:S(2)}) collective-permute-start(bf16[128,256]{1,0:T(8,128)(2,1)S(1)} %pad_maximum_fusion.refs_5_.refs_2_), channel_id=1, source_target_pairs={{0,1},{1,0},{2,3},{3,2},{4,5},{5,4},{6,7},{7,6},{8,9},{9,8},{10,11... | collective-permute-start | bytes 196616 | tf_op jit(solution)/shard_map/ppermute | solution.py:46
  50.7 11.7 %collective-permute-start.18 = (bf16[128,1024]{1,0:T(8,128)(2,1)S(1)}, bf16[128,1024]{1,0:T(8,128)(2,1)S(1)}, u32[]{:S(2)}, u32[]{:S(2)}) collective-permute-start(bf16[128,1024]{1,0:T(8,128)(2,1)S(1)} %attend_last.7), channel_id=1, source_target_pairs={{0,8},{1,9},{2,10},{3,11},{4,12},{5,13},{6,14},{7,15},{8,0},{9,1},... | collective-permute-start | bytes 786440 | tf_op jit(solution)/shard_map/ppermute | solution.py:46
  54.7 9.1 %collective-permute-start.15 = (bf16[128,1024]{1,0:T(8,128)(2,1)S(1)}, bf16[128,1024]{1,0:T(8,128)(2,1)S(1)}, u32[]{:S(2)}, u32[]{:S(2)}) collective-permute-start(bf16[128,1024]{1,0:T(8,128)(2,1)S(1)} %attend_last.5), channel_id=1, source_target_pairs={{0,4},{1,5},{2,6},{3,7},{4,0},{5,1},{6,2},{7,3},{8,12},{9,13},{10,... | collective-permute-start | bytes 786440 | tf_op jit(solution)/shard_map/ppermute | solution.py:46
  57.2 7.7 %collective-permute-start.16 = (bf16[128,1024]{1,0:T(8,128)(2,1)S(1)}, bf16[128,1024]{1,0:T(8,128)(2,1)S(1)}, u32[]{:S(2)}, u32[]{:S(2)}) collective-permute-start(bf16[128,1024]{1,0:T(8,128)(2,1)S(1)} %attend_last.6), channel_id=1, source_target_pairs={{0,12},{1,13},{2,14},{3,15},{4,8},{5,9},{6,10},{7,11},{8,4},{9,5},... | collective-permute-start | bytes 786440 | tf_op jit(solution)/shard_map/ppermute | solution.py:46

commit v5 on v4

--- a/solution.py
+++ b/solution.py
@@ -214,9 +214,7 @@
         if last:
             outs, refs = refs[:count], refs[count:]
         else:
-            stat_out, sum_out, mark_ref = refs[:count], refs[count : 2 * count], refs[2 * count]
-            refs = refs[2 * count + 1 :]
-            mark_ref[...] = jnp.zeros(mark_ref.shape, jnp.float32)
+            stat_out, sum_out, refs = refs[:count], refs[count : 2 * count], refs[2 * count :]
         k_aug, v_aug = refs
         token = lax.broadcasted_iota(jnp.int32, (TOK, TOK), 1)
         k_row = lax.broadcasted_iota(jnp.int32, (TOK, TOK), 0)
@@ -297,8 +295,7 @@
     keys, count = TOK * len(blocks), len(queries)
     state = jax.ShapeDtypeStruct((PAIRS, PAIR * TOK, HD), jnp.float32)
     result = jax.ShapeDtypeStruct((TOK, WIDE), jnp.bfloat16)
-    mark = jax.ShapeDtypeStruct((8, HD), jnp.float32)
-    outs = [result] * count if last else [state] * (2 * count) + [mark]
+    outs = [result] * count if last else [state] * (2 * count)
     return pl.pallas_call(
         make_kernel(queries, sizes, blocks, bool(carry), last),
         in_specs=[VMEM] * (1 + count + len(pieces) + len(carry)),
@@ -346,12 +343,11 @@
 
     def begin(group):
         out = attend(info, group, [q[i] for i in group], near, column_blocks((0, 1, 2)))
-        return {i: [out[n], out[len(group) + n]] for n, i in enumerate(group)}, out[-1]
-
-    state, mark = begin([1, 2])
-    mark, prompt = lax.optimization_barrier((mark, prompt))
+        return {i: [out[n], out[len(group) + n]] for n, i in enumerate(group)}
+
+    state = begin([1, 2])
     prompts = [send(prompt, pairs) for pairs in Z_STEPS]
-    state |= begin([3])[0]
+    state |= begin([3])
     pieces = [z_both, prompt] + prompts
     late = column_blocks((3,)) + [None] * 4
     results = [None] * 4

time: 66.7 us -> 66.8 us (level)
  Pallas kernels: 20.8 us -> 19.9 us
  waiting for transfers between devices: 13.6 us -> 14.5 us
    ppermute x19, waiting for transfers between devices: 13.6 us -> 14.5 us  [send(): return lax.ppermute(value, AXES, pairs)]
    pallas_call x6, Pallas kernels: 16.6 us -> 15.8 us  [attend(): pl.pallas_call(make_kernel(queries, sizes, blocks, bool(carry), last), in...]
  transfers between devices with their start and end apart: 19 -> 19, of which waited for: 8 -> 8; matrix products, arithmetic and copies ran while one was open for 0% -> 0% of each run, Pallas kernels for 25% -> 24%
where the time goes in v5:
time: 66.8 us; the launch traced here: 66.2 us
  starting transfers between devices  30.7 us (46%)
  Pallas kernels  19.9 us (30%)
  waiting for transfers between devices  14.5 us (22%)
  between operations  1.01 us (2%)
    ppermute x19, starting transfers between devices, send(): return lax.ppermute(value, AXES, pairs)  30.7 us
    pallas_call x6, Pallas kernels, attend(): pl.pallas_call(make_kernel(queries, sizes, blocks, bool(carry), last), in...  15.8 us
    ppermute x19, waiting for transfers between devices, send(): return lax.ppermute(value, AXES, pairs)  14.5 us
  transfers between devices with their start and end apart: 19, of which 8 were waited for; matrix products, arithmetic and copies ran while one was open for 0% of the time, Pallas kernels for 24%

profile of v5, /device:TPU:6, one launch (start us, length us, event | category | flops | bytes accessed | tf_op | source)
XLA Modules:
  0.0 66.2 jit_solution(15490169566767422252)
XLA Ops:
  0.0 1.0 %split_kv.1 = (bf16[144,256]{1,0:T(8,128)(2,1)S(1)}, bf16[144,256]{1,0:T(8,128)(2,1)S(1)}, bf16[144,256]{1,0:T(8,128)(2,1)S(1)}, bf16[144,256]{1,0:T(8,128)(2,1)S(1)}) custom-call(bf16[128,512]{1,0:T(8,128)(2,1)} %bitcast.5, bf16[128,512]{1,0:T(8,128)(2,1)} %bitcast.6, bf16[2,512]{1,0:T(2,128)(2,1)} %pk_ref.1, bf16[2,512]{1,0:T(2,128)(2,1)} %pv_ref.1), custom_call_target="tpu_custom_call" | custom-call | tf_op jit(solution)/shard_map/split_kv/pallas_call | solution.py:108
  1.0 1.7 %collective-permute-start = (bf16[144,256]{1,0:T(8,128)(2,1)S(1)}, bf16[144,256]{1,0:T(8,128)(2,1)S(1)}, u32[]{:S(2)}, u32[]{:S(2)}) collective-permute-start(bf16[144,256]{1,0:T(8,128)(2,1)S(1)} %get-tuple-element.41), channel_id=1, source_target_pairs={{0,4},{1,5},{2,6},{3,7},{4,0},{5,1},{6,2},{7,3},{8,12},{9,13},{10,... | collective-permute-start | bytes 221192 | tf_op jit(solution)/shard_map/ppermute | solution.py:46
  2.7 2.2 %collective-permute-start.1 = (bf16[144,256]{1,0:T(8,128)(2,1)S(1)}, bf16[144,256]{1,0:T(8,128)(2,1)S(1)}, u32[]{:S(2)}, u32[]{:S(2)}) collective-permute-start(bf16[144,256]{1,0:T(8,128)(2,1)S(1)} %get-tuple-element.42), channel_id=1, source_target_pairs={{0,12},{1,13},{2,14},{3,15},{4,8},{5,9},{6,10},{7,11},{8,4},{9,5},... | collective-permute-start | bytes 221192 | tf_op jit(solution)/shard_map/ppermute | solution.py:46
  4.9 0.7 %collective-permute-start.2 = (bf16[144,256]{1,0:T(8,128)(2,1)S(1)}, bf16[144,256]{1,0:T(8,128)(2,1)S(1)}, u32[]{:S(2)}, u32[]{:S(2)}) collective-permute-start(bf16[144,256]{1,0:T(8,128)(2,1)S(1)} %get-tuple-element.43), channel_id=1, source_target_pairs={{0,8},{1,9},{2,10},{3,11},{4,12},{5,13},{6,14},{7,15},{8,0},{9,1},... | collective-permute-start | bytes 221192 | tf_op jit(solution)/shard_map/ppermute | solution.py:46
  5.6 1.2 %split_q.1 = (bf16[128,1024]{1,0:T(8,128)(2,1)S(1)}, bf16[128,1024]{1,0:T(8,128)(2,1)S(1)}, bf16[128,1024]{1,0:T(8,128)(2,1)S(1)}, bf16[128,1024]{1,0:T(8,128)(2,1)S(1)}) custom-call(bf16[128,4096]{1,0:T(8,128)(2,1)} %bitcast.4), custom_call_target="tpu_custom_call" | custom-call | tf_op jit(solution)/shard_map/split_q/pallas_call | solution.py:129
  6.8 2.2 %collective-permute-done.1.refs_2_ = bf16[144,256]{1,0:T(8,128)(2,1)S(1)} collective-permute-done((bf16[144,256]{1,0:T(8,128)(2,1)S(1)}, bf16[144,256]{1,0:T(8,128)(2,1)S(1)}, u32[]{:S(2)}, u32[]{:S(2)}) %collective-permute-start.1) | collective-permute-done | bytes 73760 | tf_op jit(solution)/shard_map/ppermute | solution.py:46
  9.0 1.7 %collective-permute-done.2.refs_3_ = bf16[144,256]{1,0:T(8,128)(2,1)S(1)} collective-permute-done((bf16[144,256]{1,0:T(8,128)(2,1)S(1)}, bf16[144,256]{1,0:T(8,128)(2,1)S(1)}, u32[]{:S(2)}, u32[]{:S(2)}) %collective-permute-start.2) | collective-permute-done | bytes 73760 | tf_op jit(solution)/shard_map/ppermute | solution.py:46
  11.1 0.8 %collective-permute-start.7 = (bf16[128,1024]{1,0:T(8,128)(2,1)S(1)}, bf16[128,1024]{1,0:T(8,128)(2,1)S(1)}, u32[]{:S(2)}, u32[]{:S(2)}) collective-permute-start(bf16[128,1024]{1,0:T(8,128)(2,1)S(1)} %get-tuple-element.52), channel_id=1, source_target_pairs={{0,4},{1,5},{2,6},{3,7},{4,0},{5,1},{6,2},{7,3},{8,12},{9,13},{10,... | collective-permute-start | bytes 786440 | tf_op jit(solution)/shard_map/ppermute | solution.py:46
  11.8 3.3 %collective-permute-start.6 = (bf16[512,256]{1,0:T(8,128)(2,1)S(1)}, bf16[512,256]{1,0:T(8,128)(2,1)S(1)}, u32[]{:S(2)}, u32[]{:S(2)}) collective-permute-start(bf16[512,256]{1,0:T(8,128)(2,1)S(1)} %stack.1.refs_1_.refs_2_), channel_id=1, source_target_pairs={{0,2},{1,3},{2,0},{3,1},{4,6},{5,7},{6,4},{7,5},{8,10},{9,11},{10,... | collective-permute-start | bytes 786440 | tf_op jit(solution)/shard_map/ppermute | solution.py:46
  15.1 1.9 %collective-permute-start.5 = (bf16[512,256]{1,0:T(8,128)(2,1)S(1)}, bf16[512,256]{1,0:T(8,128)(2,1)S(1)}, u32[]{:S(2)}, u32[]{:S(2)}) collective-permute-start(bf16[512,256]{1,0:T(8,128)(2,1)S(1)} %stack.1.refs_1_.refs_2_), channel_id=1, source_target_pairs={{0,1},{1,0},{2,3},{3,2},{4,5},{5,4},{6,7},{7,6},{8,9},{9,8},{10,11... | collective-permute-start | bytes 786440 | tf_op jit(solution)/shard_map/ppermute | solution.py:46
  17.0 0.7 %collective-permute-start.14 = (bf16[128,1024]{1,0:T(8,128)(2,1)S(1)}, bf16[128,1024]{1,0:T(8,128)(2,1)S(1)}, u32[]{:S(2)}, u32[]{:S(2)}) collective-permute-start(bf16[128,1024]{1,0:T(8,128)(2,1)S(1)} %get-tuple-element.59), channel_id=1, source_target_pairs={{0,12},{1,13},{2,14},{3,15},{4,8},{5,9},{6,10},{7,11},{8,4},{9,5},... | collective-permute-start | bytes 786440 | tf_op jit(solution)/shard_map/ppermute | solution.py:46
  17.9 1.2 %collective-permute-done.3 = bf16[8,256]{1,0:T(8,128)(2,1)S(1)} collective-permute-done((bf16[8,256]{1,0:T(8,128)(2,1)S(1)}, bf16[8,256]{1,0:T(8,128)(2,1)S(1)}, u32[]{:S(2)}, u32[]{:S(2)}) %collective-permute-start.3) | collective-permute-done | bytes 4128 | tf_op jit(solution)/shard_map/ppermute | solution.py:46
  19.1 0.9 %collective-permute-start.4 = (bf16[16,256]{1,0:T(8,128)(2,1)S(1)}, bf16[16,256]{1,0:T(8,128)(2,1)S(1)}, u32[]{:S(2)}, u32[]{:S(2)}) collective-permute-start(bf16[16,256]{1,0:T(8,128)(2,1)S(1)} %concatenate.18), channel_id=1, source_target_pairs={{0,32},{1,33},{2,34},{3,35},{4,36},{5,37},{6,38},{7,39},{8,40},{9,... | collective-permute-start | bytes 24584 | tf_op jit(solution)/shard_map/ppermute | solution.py:46
  20.0 2.8 %collective-permute-done.4 = bf16[16,256]{1,0:T(8,128)(2,1)S(1)} collective-permute-done((bf16[16,256]{1,0:T(8,128)(2,1)S(1)}, bf16[16,256]{1,0:T(8,128)(2,1)S(1)}, u32[]{:S(2)}, u32[]{:S(2)}) %collective-permute-start.4) | collective-permute-done | bytes 8224 | tf_op jit(solution)/shard_map/ppermute | solution.py:46
  24.1 2.8 %collective-permute-start.17 = (bf16[128,1024]{1,0:T(8,128)(2,1)S(1)}, bf16[128,1024]{1,0:T(8,128)(2,1)S(1)}, u32[]{:S(2)}, u32[]{:S(2)}) collective-permute-start(bf16[128,1024]{1,0:T(8,128)(2,1)S(1)} %get-tuple-element.64), channel_id=1, source_target_pairs={{0,8},{1,9},{2,10},{3,11},{4,12},{5,13},{6,14},{7,15},{8,0},{9,1},... | collective-permute-start | bytes 786440 | tf_op jit(solution)/shard_map/ppermute | solution.py:46
  27.9 5.4 %collective-permute-start.10 = (bf16[64,256]{1,0:T(8,128)(2,1)S(1)}, bf16[64,256]{1,0:T(8,128)(2,1)S(1)}, u32[]{:S(2)}, u32[]{:S(2)}) collective-permute-start(bf16[64,256]{1,0:T(8,128)(2,1)S(1)} %pad_maximum_fusion), channel_id=1, source_target_pairs={{0,128},{1,129},{2,130},{3,131},{4,132},{5,133},{6,134},{7,135},{8... | collective-permute-start | bytes 98312 | tf_op jit(solution)/shard_map/ppermute | solution.py:46
  33.9 4.5 %attend_first.2 = (f32[2,512,128]{2,1,0:T(8,128)S(1)}, f32[2,512,128]{2,1,0:T(8,128)S(1)}, f32[2,512,128]{2,1,0:T(8,128)S(1)}, f32[2,512,128]{2,1,0:T(8,128)S(1)}) custom-call(s32[24,128]{1,0:T(8,128)S(1)} %places.1.info_ref, bf16[128,1024]{1,0:T(8,128)(2,1)S(1)} %collective-permute-done.7.refs_0_, ...), custom_call_target="tpu_custom_call" | custom-call | flops 1610612736 | bytes 2097152 | tf_op jit(solution)/shard_map/attend_first/pallas_call | solution.py:299
  38.5 2.0 %collective-permute-start.13 = (bf16[128,256]{1,0:T(8,128)(2,1)S(1)}, bf16[128,256]{1,0:T(8,128)(2,1)S(1)}, u32[]{:S(2)}, u32[]{:S(2)}) collective-permute-start(bf16[128,256]{1,0:T(8,128)(2,1)S(1)} %constant_dynamic-update-slice_fusion.refs_5_.refs_2_), channel_id=1, source_target_pairs={{0,3},{1,2},{2,1},{3,0},{4,7},{5,6},{6,5},{7,4},{8,11},{9,10},{10,... | collective-permute-start | bytes 196616 | tf_op jit(solution)/shard_map/ppermute | solution.py:46
  40.5 1.4 %collective-permute-start.12 = (bf16[128,256]{1,0:T(8,128)(2,1)S(1)}, bf16[128,256]{1,0:T(8,128)(2,1)S(1)}, u32[]{:S(2)}, u32[]{:S(2)}) collective-permute-start(bf16[128,256]{1,0:T(8,128)(2,1)S(1)} %constant_dynamic-update-slice_fusion.refs_5_.refs_2_), channel_id=1, source_target_pairs={{0,2},{1,3},{2,0},{3,1},{4,6},{5,7},{6,4},{7,5},{8,10},{9,11},{10,... | collective-permute-start | bytes 196616 | tf_op jit(solution)/shard_map/ppermute | solution.py:46
  41.9 1.1 %collective-permute-start.11 = (bf16[128,256]{1,0:T(8,128)(2,1)S(1)}, bf16[128,256]{1,0:T(8,128)(2,1)S(1)}, u32[]{:S(2)}, u32[]{:S(2)}) collective-permute-start(bf16[128,256]{1,0:T(8,128)(2,1)S(1)} %constant_dynamic-update-slice_fusion.refs_5_.refs_2_), channel_id=1, source_target_pairs={{0,1},{1,0},{2,3},{3,2},{4,5},{5,4},{6,7},{7,6},{8,9},{9,8},{10,11... | collective-permute-start | bytes 196616 | tf_op jit(solution)/shard_map/ppermute | solution.py:46
  43.0 2.3 %attend_first.3 = (f32[2,512,128]{2,1,0:T(8,128)S(1)}, f32[2,512,128]{2,1,0:T(8,128)S(1)}) custom-call(s32[24,128]{1,0:T(8,128)S(1)} %places.1.info_ref, bf16[128,1024]{1,0:T(8,128)(2,1)S(1)} %collective-permute-done.17.refs_0_, bf16[512,256]{1,0:T(8,128)(2,1)S(1)} %stack.1.refs_1_.refs_2_, bf16[512,256]{1,0:T(8,128)(2,1)S(1)} %collective-permute-done.5.refs_2_.refs_3_, ...), custom_call_target="tpu_custom_call" | custom-call | flops 805306368 | bytes 1048576 | tf_op jit(solution)/shard_map/attend_first/pallas_call | solution.py:299
  45.3 3.6 %collective-permute-done.12.refs_7_.refs_4_ = bf16[128,256]{1,0:T(8,128)(2,1)S(1)} collective-permute-done((bf16[128,256]{1,0:T(8,128)(2,1)S(1)}, bf16[128,256]{1,0:T(8,128)(2,1)S(1)}, u32[]{:S(2)}, u32[]{:S(2)}) %collective-permute-start.12) | collective-permute-done | bytes 65568 | tf_op jit(solution)/shard_map/ppermute | solution.py:46
  48.9 1.8 %attend_last.7 = bf16[128,1024]{1,0:T(8,128)(2,1)S(1)} custom-call(s32[24,128]{1,0:T(8,128)S(1)} %places.1.info_ref, bf16[128,1024]{1,0:T(8,128)(2,1)S(1)} %collective-permute-done.17.refs_0_, bf16[512,256]{1,0:T(8,128)(2,1)S(1)} %collective-permute-done.9.refs_4_.refs_1_, bf16[128,256]{1,0:T(8,128)(2,1)S(1)} %constant_dynamic-update-slice_fusion.refs_5_.refs_2_, ...), custom_call_target="tpu_custom_call" | custom-call | flops 536870912 | bytes 1048576 | tf_op jit(solution)/shard_map/attend_last/pallas_call | solution.py:299
  50.7 2.3 %collective-permute-start.18 = (bf16[128,1024]{1,0:T(8,128)(2,1)S(1)}, bf16[128,1024]{1,0:T(8,128)(2,1)S(1)}, u32[]{:S(2)}, u32[]{:S(2)}) collective-permute-start(bf16[128,1024]{1,0:T(8,128)(2,1)S(1)} %attend_last.7), channel_id=1, source_target_pairs={{0,8},{1,9},{2,10},{3,11},{4,12},{5,13},{6,14},{7,15},{8,0},{9,1},... | collective-permute-start | bytes 786440 | tf_op jit(solution)/shard_map/ppermute | solution.py:46
  53.0 1.8 %attend_last.5 = bf16[128,1024]{1,0:T(8,128)(2,1)S(1)} custom-call(s32[24,128]{1,0:T(8,128)S(1)} %places.1.info_ref, bf16[128,1024]{1,0:T(8,128)(2,1)S(1)} %collective-permute-done.7.refs_0_, bf16[512,256]{1,0:T(8,128)(2,1)S(1)} %collective-permute-done.9.refs_4_.refs_1_, bf16[128,256]{1,0:T(8,128)(2,1)S(1)} %constant_dynamic-update-slice_fusion.refs_5_.refs_2_, ...), custom_call_target="tpu_custom_call" | custom-call | flops 536870912 | bytes 1048576 | tf_op jit(solution)/shard_map/attend_last/pallas_call | solution.py:299
  54.8 0.8 %collective-permute-start.15 = (bf16[128,1024]{1,0:T(8,128)(2,1)S(1)}, bf16[128,1024]{1,0:T(8,128)(2,1)S(1)}, u32[]{:S(2)}, u32[]{:S(2)}) collective-permute-start(bf16[128,1024]{1,0:T(8,128)(2,1)S(1)} %attend_last.5), channel_id=1, source_target_pairs={{0,4},{1,5},{2,6},{3,7},{4,0},{5,1},{6,2},{7,3},{8,12},{9,13},{10,... | collective-permute-start | bytes 786440 | tf_op jit(solution)/shard_map/ppermute | solution.py:46
  55.6 1.8 %attend_last.6 = bf16[128,1024]{1,0:T(8,128)(2,1)S(1)} custom-call(s32[24,128]{1,0:T(8,128)S(1)} %places.1.info_ref, bf16[128,1024]{1,0:T(8,128)(2,1)S(1)} %collective-permute-done.14.refs_1_.refs_0_, bf16[512,256]{1,0:T(8,128)(2,1)S(1)} %collective-permute-done.9.refs_4_.refs_1_, bf16[128,256]{1,0:T(8,128)(2,1)S(1)} %constant_dynamic-update-slice_fusion.refs_5_.refs_2_, ...), custom_call_target="tpu_custom_call" | custom-call | flops 536870912 | bytes 1048576 | tf_op jit(solution)/shard_map/attend_last/pallas_call | solution.py:299
  57.4 1.5 %collective-permute-start.16 = (bf16[128,1024]{1,0:T(8,128)(2,1)S(1)}, bf16[128,1024]{1,0:T(8,128)(2,1)S(1)}, u32[]{:S(2)}, u32[]{:S(2)}) collective-permute-start(bf16[128,1024]{1,0:T(8,128)(2,1)S(1)} %attend_last.6), channel_id=1, source_target_pairs={{0,12},{1,13},{2,14},{3,15},{4,8},{5,9},{6,10},{7,11},{8,4},{9,5},... | collective-permute-start | bytes 786440 | tf_op jit(solution)/shard_map/ppermute | solution.py:46
  58.9 3.6 %attend_last.4.refs_0_ = bf16[128,1024]{1,0:T(8,128)(2,1)S(1)} custom-call(s32[24,128]{1,0:T(8,128)S(1)} %places.1.info_ref, bf16[128,1024]{1,0:T(8,128)(2,1)S(1)} %get-tuple-element.50.refs_0_, bf16[512,256]{1,0:T(8,128)(2,1)S(1)} %stack.1.refs_1_.refs_2_, bf16[512,256]{1,0:T(8,128)(2,1)S(1)} %collective-permute-done.5.refs_2_.refs_3_, ...), custom_call_target="tpu_custom_call" | custom-call | flops 1342177280 | bytes 1048576 | tf_op jit(solution)/shard_map/attend_last/pallas_call | solution.py:299
  62.5 1.4 %collective-permute-done.15.refs_1_ = bf16[128,1024]{1,0:T(8,128)(2,1)S(1)} collective-permute-done((bf16[128,1024]{1,0:T(8,128)(2,1)S(1)}, bf16[128,1024]{1,0:T(8,128)(2,1)S(1)}, u32[]{:S(2)}, u32[]{:S(2)}) %collective-permute-start.15) | collective-permute-done | bytes 262176 | tf_op jit(solution)/shard_map/ppermute | solution.py:46
  63.9 1.2 %collective-permute-done.16.refs_2_ = bf16[128,1024]{1,0:T(8,128)(2,1)S(1)} collective-permute-done((bf16[128,1024]{1,0:T(8,128)(2,1)S(1)}, bf16[128,1024]{1,0:T(8,128)(2,1)S(1)}, u32[]{:S(2)}, u32[]{:S(2)}) %collective-permute-start.16) | collective-permute-done | bytes 262176 | tf_op jit(solution)/shard_map/ppermute | solution.py:46
  65.0 1.0 %merge.1 = bf16[128,4096]{1,0:T(8,128)(2,1)} custom-call(bf16[128,1024]{1,0:T(8,128)(2,1)S(1)} %attend_last.4.refs_0_, bf16[128,1024]{1,0:T(8,128)(2,1)S(1)} %collective-permute-done.15.refs_1_, bf16[128,1024]{1,0:T(8,128)(2,1)S(1)} %collective-permute-done.16.refs_2_, bf16[128,1024]{1,0:T(8,128)(2,1)S(1)} %collective-permute-done.18.refs_3_), custom_call_target="tpu_custom_call" | custom-call | tf_op jit(solution)/shard_map/merge/pallas_call | solution.py:194
  (29 shorter events, 2.8 us)
Async XLA Ops:
  1.0 5.8 %collective-permute-start = (bf16[144,256]{1,0:T(8,128)(2,1)S(1)}, bf16[144,256]{1,0:T(8,128)(2,1)S(1)}, u32[]{:S(2)}, u32[]{:S(2)}) collective-permute-start(bf16[144,256]{1,0:T(8,128)(2,1)S(1)} %get-tuple-element.41), channel_id=1, source_target_pairs={{0,4},{1,5},{2,6},{3,7},{4,0},{5,1},{6,2},{7,3},{8,12},{9,13},{10,... | collective-permute-start | bytes 221192 | tf_op jit(solution)/shard_map/ppermute | solution.py:46
  2.7 6.4 %collective-permute-start.1 = (bf16[144,256]{1,0:T(8,128)(2,1)S(1)}, bf16[144,256]{1,0:T(8,128)(2,1)S(1)}, u32[]{:S(2)}, u32[]{:S(2)}) collective-permute-start(bf16[144,256]{1,0:T(8,128)(2,1)S(1)} %get-tuple-element.42), channel_id=1, source_target_pairs={{0,12},{1,13},{2,14},{3,15},{4,8},{5,9},{6,10},{7,11},{8,4},{9,5},... | collective-permute-start | bytes 221192 | tf_op jit(solution)/shard_map/ppermute | solution.py:46
  4.9 5.9 %collective-permute-start.2 = (bf16[144,256]{1,0:T(8,128)(2,1)S(1)}, bf16[144,256]{1,0:T(8,128)(2,1)S(1)}, u32[]{:S(2)}, u32[]{:S(2)}) collective-permute-start(bf16[144,256]{1,0:T(8,128)(2,1)S(1)} %get-tuple-element.43), channel_id=1, source_target_pairs={{0,8},{1,9},{2,10},{3,11},{4,12},{5,13},{6,14},{7,15},{8,0},{9,1},... | collective-permute-start | bytes 221192 | tf_op jit(solution)/shard_map/ppermute | solution.py:46
  11.1 11.8 %collective-permute-start.7 = (bf16[128,1024]{1,0:T(8,128)(2,1)S(1)}, bf16[128,1024]{1,0:T(8,128)(2,1)S(1)}, u32[]{:S(2)}, u32[]{:S(2)}) collective-permute-start(bf16[128,1024]{1,0:T(8,128)(2,1)S(1)} %get-tuple-element.52), channel_id=1, source_target_pairs={{0,4},{1,5},{2,6},{3,7},{4,0},{5,1},{6,2},{7,3},{8,12},{9,13},{10,... | collective-permute-start | bytes 786440 | tf_op jit(solution)/shard_map/ppermute | solution.py:46
  11.8 16.1 %collective-permute-start.6 = (bf16[512,256]{1,0:T(8,128)(2,1)S(1)}, bf16[512,256]{1,0:T(8,128)(2,1)S(1)}, u32[]{:S(2)}, u32[]{:S(2)}) collective-permute-start(bf16[512,256]{1,0:T(8,128)(2,1)S(1)} %stack.1.refs_1_.refs_2_), channel_id=1, source_target_pairs={{0,2},{1,3},{2,0},{3,1},{4,6},{5,7},{6,4},{7,5},{8,10},{9,11},{10,... | collective-permute-start | bytes 786440 | tf_op jit(solution)/shard_map/ppermute | solution.py:46
  15.1 12.8 %collective-permute-start.5 = (bf16[512,256]{1,0:T(8,128)(2,1)S(1)}, bf16[512,256]{1,0:T(8,128)(2,1)S(1)}, u32[]{:S(2)}, u32[]{:S(2)}) collective-permute-start(bf16[512,256]{1,0:T(8,128)(2,1)S(1)} %stack.1.refs_1_.refs_2_), channel_id=1, source_target_pairs={{0,1},{1,0},{2,3},{3,2},{4,5},{5,4},{6,7},{7,6},{8,9},{9,8},{10,11... | collective-permute-start | bytes 786440 | tf_op jit(solution)/shard_map/ppermute | solution.py:46
  17.0 16.9 %collective-permute-start.14 = (bf16[128,1024]{1,0:T(8,128)(2,1)S(1)}, bf16[128,1024]{1,0:T(8,128)(2,1)S(1)}, u32[]{:S(2)}, u32[]{:S(2)}) collective-permute-start(bf16[128,1024]{1,0:T(8,128)(2,1)S(1)} %get-tuple-element.59), channel_id=1, source_target_pairs={{0,12},{1,13},{2,14},{3,15},{4,8},{5,9},{6,10},{7,11},{8,4},{9,5},... | collective-permute-start | bytes 786440 | tf_op jit(solution)/shard_map/ppermute | solution.py:46
  17.8 1.3 %collective-permute-start.3 = (bf16[8,256]{1,0:T(8,128)(2,1)S(1)}, bf16[8,256]{1,0:T(8,128)(2,1)S(1)}, u32[]{:S(2)}, u32[]{:S(2)}) collective-permute-start(bf16[8,256]{1,0:T(8,128)(2,1)S(1)} %pad_maximum_fusion.1), channel_id=1, source_target_pairs={{0,16},{1,17},{2,18},{3,19},{4,20},{5,21},{6,22},{7,23},{8,24},{9,... | collective-permute-start | bytes 12296 | tf_op jit(solution)/shard_map/ppermute | solution.py:46
  19.1 3.7 %collective-permute-start.4 = (bf16[16,256]{1,0:T(8,128)(2,1)S(1)}, bf16[16,256]{1,0:T(8,128)(2,1)S(1)}, u32[]{:S(2)}, u32[]{:S(2)}) collective-permute-start(bf16[16,256]{1,0:T(8,128)(2,1)S(1)} %concatenate.18), channel_id=1, source_target_pairs={{0,32},{1,33},{2,34},{3,35},{4,36},{5,37},{6,38},{7,39},{8,40},{9,... | collective-permute-start | bytes 24584 | tf_op jit(solution)/shard_map/ppermute | solution.py:46
  22.8 4.0 %copy-start = (s32[1,16]{1,0:T(1,128)S(1)}, s32[1,16]{1,0:T(1,128)}, u32[]{:S(2)}) copy-start(s32[1,16]{1,0:T(1,128)} %offsets) | copy-start | bytes 196
  22.9 5.0 %collective-permute-start.8 = (bf16[32,256]{1,0:T(8,128)(2,1)S(1)}, bf16[32,256]{1,0:T(8,128)(2,1)S(1)}, u32[]{:S(2)}, u32[]{:S(2)}) collective-permute-start(bf16[32,256]{1,0:T(8,128)(2,1)S(1)} %concatenate.19), channel_id=1, source_target_pairs={{0,96},{1,97},{2,98},{3,99},{4,100},{5,101},{6,102},{7,103},{8,104... | collective-permute-start | bytes 49160 | tf_op jit(solution)/shard_map/ppermute | solution.py:46
  24.1 18.9 %collective-permute-start.17 = (bf16[128,1024]{1,0:T(8,128)(2,1)S(1)}, bf16[128,1024]{1,0:T(8,128)(2,1)S(1)}, u32[]{:S(2)}, u32[]{:S(2)}) collective-permute-start(bf16[128,1024]{1,0:T(8,128)(2,1)S(1)} %get-tuple-element.64), channel_id=1, source_target_pairs={{0,8},{1,9},{2,10},{3,11},{4,12},{5,13},{6,14},{7,15},{8,0},{9,1},... | collective-permute-start | bytes 786440 | tf_op jit(solution)/shard_map/ppermute | solution.py:46
  27.9 10.6 %collective-permute-start.10 = (bf16[64,256]{1,0:T(8,128)(2,1)S(1)}, bf16[64,256]{1,0:T(8,128)(2,1)S(1)}, u32[]{:S(2)}, u32[]{:S(2)}) collective-permute-start(bf16[64,256]{1,0:T(8,128)(2,1)S(1)} %pad_maximum_fusion), channel_id=1, source_target_pairs={{0,128},{1,129},{2,130},{3,131},{4,132},{5,133},{6,134},{7,135},{8... | collective-permute-start | bytes 98312 | tf_op jit(solution)/shard_map/ppermute | solution.py:46
  33.3 15.6 %collective-permute-start.9 = (bf16[512,256]{1,0:T(8,128)(2,1)S(1)}, bf16[512,256]{1,0:T(8,128)(2,1)S(1)}, u32[]{:S(2)}, u32[]{:S(2)}) collective-permute-start(bf16[512,256]{1,0:T(8,128)(2,1)S(1)} %collective-permute-done.5.refs_2_.refs_3_), channel_id=1, source_target_pairs={{0,2},{1,3},{2,0},{3,1},{4,6},{5,7},{6,4},{7,5},{8,10},{9,11},{10,... | collective-permute-start | bytes 786440 | tf_op jit(solution)/shard_map/ppermute | solution.py:46
  38.5 6.8 %collective-permute-start.13 = (bf16[128,256]{1,0:T(8,128)(2,1)S(1)}, bf16[128,256]{1,0:T(8,128)(2,1)S(1)}, u32[]{:S(2)}, u32[]{:S(2)}) collective-permute-start(bf16[128,256]{1,0:T(8,128)(2,1)S(1)} %constant_dynamic-update-slice_fusion.refs_5_.refs_2_), channel_id=1, source_target_pairs={{0,3},{1,2},{2,1},{3,0},{4,7},{5,6},{6,5},{7,4},{8,11},{9,10},{10,... | collective-permute-start | bytes 196616 | tf_op jit(solution)/shard_map/ppermute | solution.py:46
  40.5 8.4 %collective-permute-start.12 = (bf16[128,256]{1,0:T(8,128)(2,1)S(1)}, bf16[128,256]{1,0:T(8,128)(2,1)S(1)}, u32[]{:S(2)}, u32[]{:S(2)}) collective-permute-start(bf16[128,256]{1,0:T(8,128)(2,1)S(1)} %constant_dynamic-update-slice_fusion.refs_5_.refs_2_), channel_id=1, source_target_pairs={{0,2},{1,3},{2,0},{3,1},{4,6},{5,7},{6,4},{7,5},{8,10},{9,11},{10,... | collective-permute-start | bytes 196616 | tf_op jit(solution)/shard_map/ppermute | solution.py:46
  41.9 7.0 %collective-permute-start.11 = (bf16[128,256]{1,0:T(8,128)(2,1)S(1)}, bf16[128,256]{1,0:T(8,128)(2,1)S(1)}, u32[]{:S(2)}, u32[]{:S(2)}) collective-permute-start(bf16[128,256]{1,0:T(8,128)(2,1)S(1)} %constant_dynamic-update-slice_fusion.refs_5_.refs_2_), channel_id=1, source_target_pairs={{0,1},{1,0},{2,3},{3,2},{4,5},{5,4},{6,7},{7,6},{8,9},{9,8},{10,11... | collective-permute-start | bytes 196616 | tf_op jit(solution)/shard_map/ppermute | solution.py:46
  50.7 11.8 %collective-permute-start.18 = (bf16[128,1024]{1,0:T(8,128)(2,1)S(1)}, bf16[128,1024]{1,0:T(8,128)(2,1)S(1)}, u32[]{:S(2)}, u32[]{:S(2)}) collective-permute-start(bf16[128,1024]{1,0:T(8,128)(2,1)S(1)} %attend_last.7), channel_id=1, source_target_pairs={{0,8},{1,9},{2,10},{3,11},{4,12},{5,13},{6,14},{7,15},{8,0},{9,1},... | collective-permute-start | bytes 786440 | tf_op jit(solution)/shard_map/ppermute | solution.py:46
  54.8 9.1 %collective-permute-start.15 = (bf16[128,1024]{1,0:T(8,128)(2,1)S(1)}, bf16[128,1024]{1,0:T(8,128)(2,1)S(1)}, u32[]{:S(2)}, u32[]{:S(2)}) collective-permute-start(bf16[128,1024]{1,0:T(8,128)(2,1)S(1)} %attend_last.5), channel_id=1, source_target_pairs={{0,4},{1,5},{2,6},{3,7},{4,0},{5,1},{6,2},{7,3},{8,12},{9,13},{10,... | collective-permute-start | bytes 786440 | tf_op jit(solution)/shard_map/ppermute | solution.py:46
  57.4 7.7 %collective-permute-start.16 = (bf16[128,1024]{1,0:T(8,128)(2,1)S(1)}, bf16[128,1024]{1,0:T(8,128)(2,1)S(1)}, u32[]{:S(2)}, u32[]{:S(2)}) collective-permute-start(bf16[128,1024]{1,0:T(8,128)(2,1)S(1)} %attend_last.6), channel_id=1, source_target_pairs={{0,12},{1,13},{2,14},{3,15},{4,8},{5,9},{6,10},{7,11},{8,4},{9,5},... | collective-permute-start | bytes 786440 | tf_op jit(solution)/shard_map/ppermute | solution.py:46

commit v6 on v5

--- a/solution.py
+++ b/solution.py
@@ -331,9 +331,9 @@
     column, q_mine = lax.optimization_barrier((column, q_mine))
     q = [q_mine[0]] + [send(q_mine[bits], Y_STEPS[bits - 1]) for bits in (1, 2, 3)]
     prompt = double(prompt, CORE_STEP)
-    prompt = double(prompt, X_STEPS[0])
     block_offsets, prompt = lax.optimization_barrier((block_offsets, prompt))
     info = places(block_offsets, lengths)
+    prompt = double(prompt, X_STEPS[0])
     q[1], prompt = lax.optimization_barrier((q[1], prompt))
     prompt = double(prompt, X_STEPS[1])
     z_first, z_second, prompt = lax.optimization_barrier((z_first, z_second, prompt))

time: 66.8 us -> 66.8 us (level)
  no operation moved by 1% of the time
where the time goes in v6:
time: 66.8 us; the launch traced here: 66.2 us
  starting transfers between devices  30.7 us (46%)
  Pallas kernels  19.9 us (30%)
  waiting for transfers between devices  14.5 us (22%)
  between operations  0.99 us (1%)
    ppermute x19, starting transfers between devices, send(): return lax.ppermute(value, AXES, pairs)  30.7 us
    pallas_call x6, Pallas kernels, attend(): pl.pallas_call(make_kernel(queries, sizes, blocks, bool(carry), last), in...  15.8 us
    ppermute x19, waiting for transfers between devices, send(): return lax.ppermute(value, AXES, pairs)  14.5 us
  transfers between devices with their start and end apart: 19, of which 8 were waited for; matrix products, arithmetic and copies ran while one was open for 0% of the time, Pallas kernels for 24%

profile of v6, /device:TPU:6, one launch (start us, length us, event | category | flops | bytes accessed | tf_op | source)
XLA Modules:
  0.0 66.2 jit_solution(17607765428775585173)
XLA Ops:
  0.0 1.0 %split_kv.1 = (bf16[144,256]{1,0:T(8,128)(2,1)S(1)}, bf16[144,256]{1,0:T(8,128)(2,1)S(1)}, bf16[144,256]{1,0:T(8,128)(2,1)S(1)}, bf16[144,256]{1,0:T(8,128)(2,1)S(1)}) custom-call(bf16[128,512]{1,0:T(8,128)(2,1)} %bitcast.5, bf16[128,512]{1,0:T(8,128)(2,1)} %bitcast.6, bf16[2,512]{1,0:T(2,128)(2,1)} %pk_ref.1, bf16[2,512]{1,0:T(2,128)(2,1)} %pv_ref.1), custom_call_target="tpu_custom_call" | custom-call | tf_op jit(solution)/shard_map/split_kv/pallas_call | solution.py:108
  1.0 1.7 %collective-permute-start = (bf16[144,256]{1,0:T(8,128)(2,1)S(1)}, bf16[144,256]{1,0:T(8,128)(2,1)S(1)}, u32[]{:S(2)}, u32[]{:S(2)}) collective-permute-start(bf16[144,256]{1,0:T(8,128)(2,1)S(1)} %get-tuple-element.41), channel_id=1, source_target_pairs={{0,4},{1,5},{2,6},{3,7},{4,0},{5,1},{6,2},{7,3},{8,12},{9,13},{10,... | collective-permute-start | bytes 221192 | tf_op jit(solution)/shard_map/ppermute | solution.py:46
  2.7 2.2 %collective-permute-start.1 = (bf16[144,256]{1,0:T(8,128)(2,1)S(1)}, bf16[144,256]{1,0:T(8,128)(2,1)S(1)}, u32[]{:S(2)}, u32[]{:S(2)}) collective-permute-start(bf16[144,256]{1,0:T(8,128)(2,1)S(1)} %get-tuple-element.42), channel_id=1, source_target_pairs={{0,12},{1,13},{2,14},{3,15},{4,8},{5,9},{6,10},{7,11},{8,4},{9,5},... | collective-permute-start | bytes 221192 | tf_op jit(solution)/shard_map/ppermute | solution.py:46
  4.9 0.7 %collective-permute-start.2 = (bf16[144,256]{1,0:T(8,128)(2,1)S(1)}, bf16[144,256]{1,0:T(8,128)(2,1)S(1)}, u32[]{:S(2)}, u32[]{:S(2)}) collective-permute-start(bf16[144,256]{1,0:T(8,128)(2,1)S(1)} %get-tuple-element.43), channel_id=1, source_target_pairs={{0,8},{1,9},{2,10},{3,11},{4,12},{5,13},{6,14},{7,15},{8,0},{9,1},... | collective-permute-start | bytes 221192 | tf_op jit(solution)/shard_map/ppermute | solution.py:46
  5.6 1.2 %split_q.1 = (bf16[128,1024]{1,0:T(8,128)(2,1)S(1)}, bf16[128,1024]{1,0:T(8,128)(2,1)S(1)}, bf16[128,1024]{1,0:T(8,128)(2,1)S(1)}, bf16[128,1024]{1,0:T(8,128)(2,1)S(1)}) custom-call(bf16[128,4096]{1,0:T(8,128)(2,1)} %bitcast.4), custom_call_target="tpu_custom_call" | custom-call | tf_op jit(solution)/shard_map/split_q/pallas_call | solution.py:129
  6.8 2.2 %collective-permute-done.1.refs_2_ = bf16[144,256]{1,0:T(8,128)(2,1)S(1)} collective-permute-done((bf16[144,256]{1,0:T(8,128)(2,1)S(1)}, bf16[144,256]{1,0:T(8,128)(2,1)S(1)}, u32[]{:S(2)}, u32[]{:S(2)}) %collective-permute-start.1) | collective-permute-done | bytes 73760 | tf_op jit(solution)/shard_map/ppermute | solution.py:46
  9.0 1.7 %collective-permute-done.2.refs_3_ = bf16[144,256]{1,0:T(8,128)(2,1)S(1)} collective-permute-done((bf16[144,256]{1,0:T(8,128)(2,1)S(1)}, bf16[144,256]{1,0:T(8,128)(2,1)S(1)}, u32[]{:S(2)}, u32[]{:S(2)}) %collective-permute-start.2) | collective-permute-done | bytes 73760 | tf_op jit(solution)/shard_map/ppermute | solution.py:46
  11.1 0.8 %collective-permute-start.6 = (bf16[128,1024]{1,0:T(8,128)(2,1)S(1)}, bf16[128,1024]{1,0:T(8,128)(2,1)S(1)}, u32[]{:S(2)}, u32[]{:S(2)}) collective-permute-start(bf16[128,1024]{1,0:T(8,128)(2,1)S(1)} %get-tuple-element.52), channel_id=1, source_target_pairs={{0,4},{1,5},{2,6},{3,7},{4,0},{5,1},{6,2},{7,3},{8,12},{9,13},{10,... | collective-permute-start | bytes 786440 | tf_op jit(solution)/shard_map/ppermute | solution.py:46
  11.8 3.3 %collective-permute-start.5 = (bf16[512,256]{1,0:T(8,128)(2,1)S(1)}, bf16[512,256]{1,0:T(8,128)(2,1)S(1)}, u32[]{:S(2)}, u32[]{:S(2)}) collective-permute-start(bf16[512,256]{1,0:T(8,128)(2,1)S(1)} %stack.1.refs_1_.refs_2_), channel_id=1, source_target_pairs={{0,2},{1,3},{2,0},{3,1},{4,6},{5,7},{6,4},{7,5},{8,10},{9,11},{10,... | collective-permute-start | bytes 786440 | tf_op jit(solution)/shard_map/ppermute | solution.py:46
  15.1 1.9 %collective-permute-start.4 = (bf16[512,256]{1,0:T(8,128)(2,1)S(1)}, bf16[512,256]{1,0:T(8,128)(2,1)S(1)}, u32[]{:S(2)}, u32[]{:S(2)}) collective-permute-start(bf16[512,256]{1,0:T(8,128)(2,1)S(1)} %stack.1.refs_1_.refs_2_), channel_id=1, source_target_pairs={{0,1},{1,0},{2,3},{3,2},{4,5},{5,4},{6,7},{7,6},{8,9},{9,8},{10,11... | collective-permute-start | bytes 786440 | tf_op jit(solution)/shard_map/ppermute | solution.py:46
  17.0 0.7 %collective-permute-start.14 = (bf16[128,1024]{1,0:T(8,128)(2,1)S(1)}, bf16[128,1024]{1,0:T(8,128)(2,1)S(1)}, u32[]{:S(2)}, u32[]{:S(2)}) collective-permute-start(bf16[128,1024]{1,0:T(8,128)(2,1)S(1)} %get-tuple-element.59), channel_id=1, source_target_pairs={{0,12},{1,13},{2,14},{3,15},{4,8},{5,9},{6,10},{7,11},{8,4},{9,5},... | collective-permute-start | bytes 786440 | tf_op jit(solution)/shard_map/ppermute | solution.py:46
  17.9 1.2 %collective-permute-done.3 = bf16[8,256]{1,0:T(8,128)(2,1)S(1)} collective-permute-done((bf16[8,256]{1,0:T(8,128)(2,1)S(1)}, bf16[8,256]{1,0:T(8,128)(2,1)S(1)}, u32[]{:S(2)}, u32[]{:S(2)}) %collective-permute-start.3) | collective-permute-done | bytes 4128 | tf_op jit(solution)/shard_map/ppermute | solution.py:46
  19.1 0.9 %collective-permute-start.7 = (bf16[16,256]{1,0:T(8,128)(2,1)S(1)}, bf16[16,256]{1,0:T(8,128)(2,1)S(1)}, u32[]{:S(2)}, u32[]{:S(2)}) collective-permute-start(bf16[16,256]{1,0:T(8,128)(2,1)S(1)} %concatenate.17), channel_id=1, source_target_pairs={{0,32},{1,33},{2,34},{3,35},{4,36},{5,37},{6,38},{7,39},{8,40},{9,... | collective-permute-start | bytes 24584 | tf_op jit(solution)/shard_map/ppermute | solution.py:46
  20.0 2.8 %collective-permute-done.7 = bf16[16,256]{1,0:T(8,128)(2,1)S(1)} collective-permute-done((bf16[16,256]{1,0:T(8,128)(2,1)S(1)}, bf16[16,256]{1,0:T(8,128)(2,1)S(1)}, u32[]{:S(2)}, u32[]{:S(2)}) %collective-permute-start.7) | collective-permute-done | bytes 8224 | tf_op jit(solution)/shard_map/ppermute | solution.py:46
  24.0 2.8 %collective-permute-start.17 = (bf16[128,1024]{1,0:T(8,128)(2,1)S(1)}, bf16[128,1024]{1,0:T(8,128)(2,1)S(1)}, u32[]{:S(2)}, u32[]{:S(2)}) collective-permute-start(bf16[128,1024]{1,0:T(8,128)(2,1)S(1)} %get-tuple-element.64), channel_id=1, source_target_pairs={{0,8},{1,9},{2,10},{3,11},{4,12},{5,13},{6,14},{7,15},{8,0},{9,1},... | collective-permute-start | bytes 786440 | tf_op jit(solution)/shard_map/ppermute | solution.py:46
  27.9 5.5 %collective-permute-start.10 = (bf16[64,256]{1,0:T(8,128)(2,1)S(1)}, bf16[64,256]{1,0:T(8,128)(2,1)S(1)}, u32[]{:S(2)}, u32[]{:S(2)}) collective-permute-start(bf16[64,256]{1,0:T(8,128)(2,1)S(1)} %pad_maximum_fusion), channel_id=1, source_target_pairs={{0,128},{1,129},{2,130},{3,131},{4,132},{5,133},{6,134},{7,135},{8... | collective-permute-start | bytes 98312 | tf_op jit(solution)/shard_map/ppermute | solution.py:46
  33.9 4.5 %attend_first.2 = (f32[2,512,128]{2,1,0:T(8,128)S(1)}, f32[2,512,128]{2,1,0:T(8,128)S(1)}, f32[2,512,128]{2,1,0:T(8,128)S(1)}, f32[2,512,128]{2,1,0:T(8,128)S(1)}) custom-call(s32[24,128]{1,0:T(8,128)S(1)} %places.1.info_ref, bf16[128,1024]{1,0:T(8,128)(2,1)S(1)} %collective-permute-done.6.refs_0_, ...), custom_call_target="tpu_custom_call" | custom-call | flops 1610612736 | bytes 2097152 | tf_op jit(solution)/shard_map/attend_first/pallas_call | solution.py:299
  38.5 2.0 %collective-permute-start.13 = (bf16[128,256]{1,0:T(8,128)(2,1)S(1)}, bf16[128,256]{1,0:T(8,128)(2,1)S(1)}, u32[]{:S(2)}, u32[]{:S(2)}) collective-permute-start(bf16[128,256]{1,0:T(8,128)(2,1)S(1)} %constant_dynamic-update-slice_fusion.refs_5_.refs_2_), channel_id=1, source_target_pairs={{0,3},{1,2},{2,1},{3,0},{4,7},{5,6},{6,5},{7,4},{8,11},{9,10},{10,... | collective-permute-start | bytes 196616 | tf_op jit(solution)/shard_map/ppermute | solution.py:46
  40.4 1.4 %collective-permute-start.12 = (bf16[128,256]{1,0:T(8,128)(2,1)S(1)}, bf16[128,256]{1,0:T(8,128)(2,1)S(1)}, u32[]{:S(2)}, u32[]{:S(2)}) collective-permute-start(bf16[128,256]{1,0:T(8,128)(2,1)S(1)} %constant_dynamic-update-slice_fusion.refs_5_.refs_2_), channel_id=1, source_target_pairs={{0,2},{1,3},{2,0},{3,1},{4,6},{5,7},{6,4},{7,5},{8,10},{9,11},{10,... | collective-permute-start | bytes 196616 | tf_op jit(solution)/shard_map/ppermute | solution.py:46
  41.9 1.0 %collective-permute-start.11 = (bf16[128,256]{1,0:T(8,128)(2,1)S(1)}, bf16[128,256]{1,0:T(8,128)(2,1)S(1)}, u32[]{:S(2)}, u32[]{:S(2)}) collective-permute-start(bf16[128,256]{1,0:T(8,128)(2,1)S(1)} %constant_dynamic-update-slice_fusion.refs_5_.refs_2_), channel_id=1, source_target_pairs={{0,1},{1,0},{2,3},{3,2},{4,5},{5,4},{6,7},{7,6},{8,9},{9,8},{10,11... | collective-permute-start | bytes 196616 | tf_op jit(solution)/shard_map/ppermute | solution.py:46
  42.9 2.3 %attend_first.3 = (f32[2,512,128]{2,1,0:T(8,128)S(1)}, f32[2,512,128]{2,1,0:T(8,128)S(1)}) custom-call(s32[24,128]{1,0:T(8,128)S(1)} %places.1.info_ref, bf16[128,1024]{1,0:T(8,128)(2,1)S(1)} %collective-permute-done.17.refs_0_, bf16[512,256]{1,0:T(8,128)(2,1)S(1)} %stack.1.refs_1_.refs_2_, bf16[512,256]{1,0:T(8,128)(2,1)S(1)} %collective-permute-done.4.refs_2_.refs_3_, ...), custom_call_target="tpu_custom_call" | custom-call | flops 805306368 | bytes 1048576 | tf_op jit(solution)/shard_map/attend_first/pallas_call | solution.py:299
  45.3 3.6 %collective-permute-done.12.refs_7_.refs_4_ = bf16[128,256]{1,0:T(8,128)(2,1)S(1)} collective-permute-done((bf16[128,256]{1,0:T(8,128)(2,1)S(1)}, bf16[128,256]{1,0:T(8,128)(2,1)S(1)}, u32[]{:S(2)}, u32[]{:S(2)}) %collective-permute-start.12) | collective-permute-done | bytes 65568 | tf_op jit(solution)/shard_map/ppermute | solution.py:46
  48.9 1.8 %attend_last.7 = bf16[128,1024]{1,0:T(8,128)(2,1)S(1)} custom-call(s32[24,128]{1,0:T(8,128)S(1)} %places.1.info_ref, bf16[128,1024]{1,0:T(8,128)(2,1)S(1)} %collective-permute-done.17.refs_0_, bf16[512,256]{1,0:T(8,128)(2,1)S(1)} %collective-permute-done.9.refs_4_.refs_1_, bf16[128,256]{1,0:T(8,128)(2,1)S(1)} %constant_dynamic-update-slice_fusion.refs_5_.refs_2_, ...), custom_call_target="tpu_custom_call" | custom-call | flops 536870912 | bytes 1048576 | tf_op jit(solution)/shard_map/attend_last/pallas_call | solution.py:299
  50.7 2.2 %collective-permute-start.18 = (bf16[128,1024]{1,0:T(8,128)(2,1)S(1)}, bf16[128,1024]{1,0:T(8,128)(2,1)S(1)}, u32[]{:S(2)}, u32[]{:S(2)}) collective-permute-start(bf16[128,1024]{1,0:T(8,128)(2,1)S(1)} %attend_last.7), channel_id=1, source_target_pairs={{0,8},{1,9},{2,10},{3,11},{4,12},{5,13},{6,14},{7,15},{8,0},{9,1},... | collective-permute-start | bytes 786440 | tf_op jit(solution)/shard_map/ppermute | solution.py:46
  53.0 1.8 %attend_last.5 = bf16[128,1024]{1,0:T(8,128)(2,1)S(1)} custom-call(s32[24,128]{1,0:T(8,128)S(1)} %places.1.info_ref, bf16[128,1024]{1,0:T(8,128)(2,1)S(1)} %collective-permute-done.6.refs_0_, bf16[512,256]{1,0:T(8,128)(2,1)S(1)} %collective-permute-done.9.refs_4_.refs_1_, bf16[128,256]{1,0:T(8,128)(2,1)S(1)} %constant_dynamic-update-slice_fusion.refs_5_.refs_2_, ...), custom_call_target="tpu_custom_call" | custom-call | flops 536870912 | bytes 1048576 | tf_op jit(solution)/shard_map/attend_last/pallas_call | solution.py:299
  54.8 0.8 %collective-permute-start.15 = (bf16[128,1024]{1,0:T(8,128)(2,1)S(1)}, bf16[128,1024]{1,0:T(8,128)(2,1)S(1)}, u32[]{:S(2)}, u32[]{:S(2)}) collective-permute-start(bf16[128,1024]{1,0:T(8,128)(2,1)S(1)} %attend_last.5), channel_id=1, source_target_pairs={{0,4},{1,5},{2,6},{3,7},{4,0},{5,1},{6,2},{7,3},{8,12},{9,13},{10,... | collective-permute-start | bytes 786440 | tf_op jit(solution)/shard_map/ppermute | solution.py:46
  55.5 1.8 %attend_last.6 = bf16[128,1024]{1,0:T(8,128)(2,1)S(1)} custom-call(s32[24,128]{1,0:T(8,128)S(1)} %places.1.info_ref, bf16[128,1024]{1,0:T(8,128)(2,1)S(1)} %collective-permute-done.14.refs_1_.refs_0_, bf16[512,256]{1,0:T(8,128)(2,1)S(1)} %collective-permute-done.9.refs_4_.refs_1_, bf16[128,256]{1,0:T(8,128)(2,1)S(1)} %constant_dynamic-update-slice_fusion.refs_5_.refs_2_, ...), custom_call_target="tpu_custom_call" | custom-call | flops 536870912 | bytes 1048576 | tf_op jit(solution)/shard_map/attend_last/pallas_call | solution.py:299
  57.3 1.6 %collective-permute-start.16 = (bf16[128,1024]{1,0:T(8,128)(2,1)S(1)}, bf16[128,1024]{1,0:T(8,128)(2,1)S(1)}, u32[]{:S(2)}, u32[]{:S(2)}) collective-permute-start(bf16[128,1024]{1,0:T(8,128)(2,1)S(1)} %attend_last.6), channel_id=1, source_target_pairs={{0,12},{1,13},{2,14},{3,15},{4,8},{5,9},{6,10},{7,11},{8,4},{9,5},... | collective-permute-start | bytes 786440 | tf_op jit(solution)/shard_map/ppermute | solution.py:46
  58.9 3.6 %attend_last.4.refs_0_ = bf16[128,1024]{1,0:T(8,128)(2,1)S(1)} custom-call(s32[24,128]{1,0:T(8,128)S(1)} %places.1.info_ref, bf16[128,1024]{1,0:T(8,128)(2,1)S(1)} %get-tuple-element.50.refs_0_, bf16[512,256]{1,0:T(8,128)(2,1)S(1)} %stack.1.refs_1_.refs_2_, bf16[512,256]{1,0:T(8,128)(2,1)S(1)} %collective-permute-done.4.refs_2_.refs_3_, ...), custom_call_target="tpu_custom_call" | custom-call | flops 1342177280 | bytes 1048576 | tf_op jit(solution)/shard_map/attend_last/pallas_call | solution.py:299
  62.5 1.4 %collective-permute-done.15.refs_1_ = bf16[128,1024]{1,0:T(8,128)(2,1)S(1)} collective-permute-done((bf16[128,1024]{1,0:T(8,128)(2,1)S(1)}, bf16[128,1024]{1,0:T(8,128)(2,1)S(1)}, u32[]{:S(2)}, u32[]{:S(2)}) %collective-permute-start.15) | collective-permute-done | bytes 262176 | tf_op jit(solution)/shard_map/ppermute | solution.py:46
  63.9 1.1 %collective-permute-done.16.refs_2_ = bf16[128,1024]{1,0:T(8,128)(2,1)S(1)} collective-permute-done((bf16[128,1024]{1,0:T(8,128)(2,1)S(1)}, bf16[128,1024]{1,0:T(8,128)(2,1)S(1)}, u32[]{:S(2)}, u32[]{:S(2)}) %collective-permute-start.16) | collective-permute-done | bytes 262176 | tf_op jit(solution)/shard_map/ppermute | solution.py:46
  65.0 1.0 %merge.1 = bf16[128,4096]{1,0:T(8,128)(2,1)} custom-call(bf16[128,1024]{1,0:T(8,128)(2,1)S(1)} %attend_last.4.refs_0_, bf16[128,1024]{1,0:T(8,128)(2,1)S(1)} %collective-permute-done.15.refs_1_, bf16[128,1024]{1,0:T(8,128)(2,1)S(1)} %collective-permute-done.16.refs_2_, bf16[128,1024]{1,0:T(8,128)(2,1)S(1)} %collective-permute-done.18.refs_3_), custom_call_target="tpu_custom_call" | custom-call | tf_op jit(solution)/shard_map/merge/pallas_call | solution.py:194
  (29 shorter events, 2.7 us)
Async XLA Ops:
  1.0 5.8 %collective-permute-start = (bf16[144,256]{1,0:T(8,128)(2,1)S(1)}, bf16[144,256]{1,0:T(8,128)(2,1)S(1)}, u32[]{:S(2)}, u32[]{:S(2)}) collective-permute-start(bf16[144,256]{1,0:T(8,128)(2,1)S(1)} %get-tuple-element.41), channel_id=1, source_target_pairs={{0,4},{1,5},{2,6},{3,7},{4,0},{5,1},{6,2},{7,3},{8,12},{9,13},{10,... | collective-permute-start | bytes 221192 | tf_op jit(solution)/shard_map/ppermute | solution.py:46
  2.7 6.4 %collective-permute-start.1 = (bf16[144,256]{1,0:T(8,128)(2,1)S(1)}, bf16[144,256]{1,0:T(8,128)(2,1)S(1)}, u32[]{:S(2)}, u32[]{:S(2)}) collective-permute-start(bf16[144,256]{1,0:T(8,128)(2,1)S(1)} %get-tuple-element.42), channel_id=1, source_target_pairs={{0,12},{1,13},{2,14},{3,15},{4,8},{5,9},{6,10},{7,11},{8,4},{9,5},... | collective-permute-start | bytes 221192 | tf_op jit(solution)/shard_map/ppermute | solution.py:46
  4.9 5.9 %collective-permute-start.2 = (bf16[144,256]{1,0:T(8,128)(2,1)S(1)}, bf16[144,256]{1,0:T(8,128)(2,1)S(1)}, u32[]{:S(2)}, u32[]{:S(2)}) collective-permute-start(bf16[144,256]{1,0:T(8,128)(2,1)S(1)} %get-tuple-element.43), channel_id=1, source_target_pairs={{0,8},{1,9},{2,10},{3,11},{4,12},{5,13},{6,14},{7,15},{8,0},{9,1},... | collective-permute-start | bytes 221192 | tf_op jit(solution)/shard_map/ppermute | solution.py:46
  11.1 11.7 %collective-permute-start.6 = (bf16[128,1024]{1,0:T(8,128)(2,1)S(1)}, bf16[128,1024]{1,0:T(8,128)(2,1)S(1)}, u32[]{:S(2)}, u32[]{:S(2)}) collective-permute-start(bf16[128,1024]{1,0:T(8,128)(2,1)S(1)} %get-tuple-element.52), channel_id=1, source_target_pairs={{0,4},{1,5},{2,6},{3,7},{4,0},{5,1},{6,2},{7,3},{8,12},{9,13},{10,... | collective-permute-start | bytes 786440 | tf_op jit(solution)/shard_map/ppermute | solution.py:46
  11.8 16.0 %collective-permute-start.5 = (bf16[512,256]{1,0:T(8,128)(2,1)S(1)}, bf16[512,256]{1,0:T(8,128)(2,1)S(1)}, u32[]{:S(2)}, u32[]{:S(2)}) collective-permute-start(bf16[512,256]{1,0:T(8,128)(2,1)S(1)} %stack.1.refs_1_.refs_2_), channel_id=1, source_target_pairs={{0,2},{1,3},{2,0},{3,1},{4,6},{5,7},{6,4},{7,5},{8,10},{9,11},{10,... | collective-permute-start | bytes 786440 | tf_op jit(solution)/shard_map/ppermute | solution.py:46
  15.1 12.8 %collective-permute-start.4 = (bf16[512,256]{1,0:T(8,128)(2,1)S(1)}, bf16[512,256]{1,0:T(8,128)(2,1)S(1)}, u32[]{:S(2)}, u32[]{:S(2)}) collective-permute-start(bf16[512,256]{1,0:T(8,128)(2,1)S(1)} %stack.1.refs_1_.refs_2_), channel_id=1, source_target_pairs={{0,1},{1,0},{2,3},{3,2},{4,5},{5,4},{6,7},{7,6},{8,9},{9,8},{10,11... | collective-permute-start | bytes 786440 | tf_op jit(solution)/shard_map/ppermute | solution.py:46
  17.0 16.9 %collective-permute-start.14 = (bf16[128,1024]{1,0:T(8,128)(2,1)S(1)}, bf16[128,1024]{1,0:T(8,128)(2,1)S(1)}, u32[]{:S(2)}, u32[]{:S(2)}) collective-permute-start(bf16[128,1024]{1,0:T(8,128)(2,1)S(1)} %get-tuple-element.59), channel_id=1, source_target_pairs={{0,12},{1,13},{2,14},{3,15},{4,8},{5,9},{6,10},{7,11},{8,4},{9,5},... | collective-permute-start | bytes 786440 | tf_op jit(solution)/shard_map/ppermute | solution.py:46
  17.8 1.3 %collective-permute-start.3 = (bf16[8,256]{1,0:T(8,128)(2,1)S(1)}, bf16[8,256]{1,0:T(8,128)(2,1)S(1)}, u32[]{:S(2)}, u32[]{:S(2)}) collective-permute-start(bf16[8,256]{1,0:T(8,128)(2,1)S(1)} %pad_maximum_fusion.2), channel_id=1, source_target_pairs={{0,16},{1,17},{2,18},{3,19},{4,20},{5,21},{6,22},{7,23},{8,24},{9,... | collective-permute-start | bytes 12296 | tf_op jit(solution)/shard_map/ppermute | solution.py:46
  19.1 3.7 %collective-permute-start.7 = (bf16[16,256]{1,0:T(8,128)(2,1)S(1)}, bf16[16,256]{1,0:T(8,128)(2,1)S(1)}, u32[]{:S(2)}, u32[]{:S(2)}) collective-permute-start(bf16[16,256]{1,0:T(8,128)(2,1)S(1)} %concatenate.17), channel_id=1, source_target_pairs={{0,32},{1,33},{2,34},{3,35},{4,36},{5,37},{6,38},{7,39},{8,40},{9,... | collective-permute-start | bytes 24584 | tf_op jit(solution)/shard_map/ppermute | solution.py:46
  22.8 4.0 %copy-start = (s32[1,16]{1,0:T(1,128)S(1)}, s32[1,16]{1,0:T(1,128)}, u32[]{:S(2)}) copy-start(s32[1,16]{1,0:T(1,128)} %offsets) | copy-start | bytes 196
  22.8 5.0 %collective-permute-start.8 = (bf16[32,256]{1,0:T(8,128)(2,1)S(1)}, bf16[32,256]{1,0:T(8,128)(2,1)S(1)}, u32[]{:S(2)}, u32[]{:S(2)}) collective-permute-start(bf16[32,256]{1,0:T(8,128)(2,1)S(1)} %pad_maximum_fusion.1), channel_id=1, source_target_pairs={{0,96},{1,97},{2,98},{3,99},{4,100},{5,101},{6,102},{7,103},{8,104... | collective-permute-start | bytes 49160 | tf_op jit(solution)/shard_map/ppermute | solution.py:46
  24.0 18.9 %collective-permute-start.17 = (bf16[128,1024]{1,0:T(8,128)(2,1)S(1)}, bf16[128,1024]{1,0:T(8,128)(2,1)S(1)}, u32[]{:S(2)}, u32[]{:S(2)}) collective-permute-start(bf16[128,1024]{1,0:T(8,128)(2,1)S(1)} %get-tuple-element.64), channel_id=1, source_target_pairs={{0,8},{1,9},{2,10},{3,11},{4,12},{5,13},{6,14},{7,15},{8,0},{9,1},... | collective-permute-start | bytes 786440 | tf_op jit(solution)/shard_map/ppermute | solution.py:46
  27.9 10.6 %collective-permute-start.10 = (bf16[64,256]{1,0:T(8,128)(2,1)S(1)}, bf16[64,256]{1,0:T(8,128)(2,1)S(1)}, u32[]{:S(2)}, u32[]{:S(2)}) collective-permute-start(bf16[64,256]{1,0:T(8,128)(2,1)S(1)} %pad_maximum_fusion), channel_id=1, source_target_pairs={{0,128},{1,129},{2,130},{3,131},{4,132},{5,133},{6,134},{7,135},{8... | collective-permute-start | bytes 98312 | tf_op jit(solution)/shard_map/ppermute | solution.py:46
  33.3 15.6 %collective-permute-start.9 = (bf16[512,256]{1,0:T(8,128)(2,1)S(1)}, bf16[512,256]{1,0:T(8,128)(2,1)S(1)}, u32[]{:S(2)}, u32[]{:S(2)}) collective-permute-start(bf16[512,256]{1,0:T(8,128)(2,1)S(1)} %collective-permute-done.4.refs_2_.refs_3_), channel_id=1, source_target_pairs={{0,2},{1,3},{2,0},{3,1},{4,6},{5,7},{6,4},{7,5},{8,10},{9,11},{10,... | collective-permute-start | bytes 786440 | tf_op jit(solution)/shard_map/ppermute | solution.py:46
  38.5 6.8 %collective-permute-start.13 = (bf16[128,256]{1,0:T(8,128)(2,1)S(1)}, bf16[128,256]{1,0:T(8,128)(2,1)S(1)}, u32[]{:S(2)}, u32[]{:S(2)}) collective-permute-start(bf16[128,256]{1,0:T(8,128)(2,1)S(1)} %constant_dynamic-update-slice_fusion.refs_5_.refs_2_), channel_id=1, source_target_pairs={{0,3},{1,2},{2,1},{3,0},{4,7},{5,6},{6,5},{7,4},{8,11},{9,10},{10,... | collective-permute-start | bytes 196616 | tf_op jit(solution)/shard_map/ppermute | solution.py:46
  40.4 8.5 %collective-permute-start.12 = (bf16[128,256]{1,0:T(8,128)(2,1)S(1)}, bf16[128,256]{1,0:T(8,128)(2,1)S(1)}, u32[]{:S(2)}, u32[]{:S(2)}) collective-permute-start(bf16[128,256]{1,0:T(8,128)(2,1)S(1)} %constant_dynamic-update-slice_fusion.refs_5_.refs_2_), channel_id=1, source_target_pairs={{0,2},{1,3},{2,0},{3,1},{4,6},{5,7},{6,4},{7,5},{8,10},{9,11},{10,... | collective-permute-start | bytes 196616 | tf_op jit(solution)/shard_map/ppermute | solution.py:46
  41.9 7.0 %collective-permute-start.11 = (bf16[128,256]{1,0:T(8,128)(2,1)S(1)}, bf16[128,256]{1,0:T(8,128)(2,1)S(1)}, u32[]{:S(2)}, u32[]{:S(2)}) collective-permute-start(bf16[128,256]{1,0:T(8,128)(2,1)S(1)} %constant_dynamic-update-slice_fusion.refs_5_.refs_2_), channel_id=1, source_target_pairs={{0,1},{1,0},{2,3},{3,2},{4,5},{5,4},{6,7},{7,6},{8,9},{9,8},{10,11... | collective-permute-start | bytes 196616 | tf_op jit(solution)/shard_map/ppermute | solution.py:46
  50.7 11.8 %collective-permute-start.18 = (bf16[128,1024]{1,0:T(8,128)(2,1)S(1)}, bf16[128,1024]{1,0:T(8,128)(2,1)S(1)}, u32[]{:S(2)}, u32[]{:S(2)}) collective-permute-start(bf16[128,1024]{1,0:T(8,128)(2,1)S(1)} %attend_last.7), channel_id=1, source_target_pairs={{0,8},{1,9},{2,10},{3,11},{4,12},{5,13},{6,14},{7,15},{8,0},{9,1},... | collective-permute-start | bytes 786440 | tf_op jit(solution)/shard_map/ppermute | solution.py:46
  54.8 9.1 %collective-permute-start.15 = (bf16[128,1024]{1,0:T(8,128)(2,1)S(1)}, bf16[128,1024]{1,0:T(8,128)(2,1)S(1)}, u32[]{:S(2)}, u32[]{:S(2)}) collective-permute-start(bf16[128,1024]{1,0:T(8,128)(2,1)S(1)} %attend_last.5), channel_id=1, source_target_pairs={{0,4},{1,5},{2,6},{3,7},{4,0},{5,1},{6,2},{7,3},{8,12},{9,13},{10,... | collective-permute-start | bytes 786440 | tf_op jit(solution)/shard_map/ppermute | solution.py:46
  57.3 7.7 %collective-permute-start.16 = (bf16[128,1024]{1,0:T(8,128)(2,1)S(1)}, bf16[128,1024]{1,0:T(8,128)(2,1)S(1)}, u32[]{:S(2)}, u32[]{:S(2)}) collective-permute-start(bf16[128,1024]{1,0:T(8,128)(2,1)S(1)} %attend_last.6), channel_id=1, source_target_pairs={{0,12},{1,13},{2,14},{3,15},{4,8},{5,9},{6,10},{7,11},{8,4},{9,5},... | collective-permute-start | bytes 786440 | tf_op jit(solution)/shard_map/ppermute | solution.py:46
